TPU v7x, 256 devices: a whole 4x4x8 slice. The times are simulated.
256 devices in a mesh: dom: 256 (over z, x, y, core).
Axes of the slice: x: 4, y: 4, z: 8, core: 2. Of those that a mesh axis runs over, the one named last changes fastest.
Arguments:
- wing_jitter: float32 [3, 2097152], P(None, 'dom'), may hold values from 0 to 1
- live_blocks: int32 [256], P('dom'), may hold values from 1 to 64, as said below
- smoothing: float32 [2097152], P('dom'), may hold values from 0.3 to 3
- displacement: float32 [3, 2097152], P(None, 'dom'), may hold values from -20 to 20
- fluid_jitter: float32 [3, 786432], P(None, 'dom'), may hold values from 0 to 1
Outputs:
- coefs: float32 [3, 2097152], P(None, 'dom')
- residual: float32 [3, 2097152], P(None, 'dom')
- fluid_values: float32 [3, 786432], P(None, 'dom')
Inputs may be any that keep to these rules, and one draw needn't show every extreme that they name: `live_blocks`: some device holds 64 live blocks, and some device other than the first and the last holds 1.
All inputs are finite; a program needn't handle non-finite values.
Results may differ from a plain program's by a relative error of at most 0.0003.
Values sent between devices are 32-bit elements; how exact they have to be, the bound alone decides.
No kernel may reach another device: no remote copies, remote signals or barrier semaphores. Data moves between devices by JAX's collectives and lax.ppermute only.
A program may use at most 64 MiB of HBM per device.

v0:
```python
import jax
import jax.numpy as jnp
from jax import lax
from jax.sharding import Mesh
from jax.sharding import PartitionSpec as P

BLK = 128
ITERS = 3
DOM = ("dom_0", "dom_1", "dom_2", "dom_3")


stretch_factors = (1.0, 6.0, 6.0)


def one_axis_at_a_time(shard, axes):
    for axis in axes:
        shard = lax.psum(shard, axis)
    return shard


def from_behind(block, axis, distance):
    devices = range(lax.axis_size(axis))
    route = [(i - distance, i) for i in devices if i - distance in devices]
    return lax.ppermute(block, axis, route)


def wendland(row_points, col_points):
    spread = (row_points[0][:, None] - col_points[0][None, :]) ** 2
    spread = spread + (row_points[1][:, None] - col_points[1][None, :]) ** 2
    spread = spread + (row_points[2][:, None] - col_points[2][None, :]) ** 2
    scaled = jnp.sqrt(spread) * 0.5
    remain = jnp.maximum(1.0 - scaled, 0.0)
    return remain * remain * remain * remain * (4.0 * scaled + 1.0)


def block_ends(blocks, live_count):
    tail_index = live_count - 2 + jnp.arange(2, dtype=jnp.int32)
    tail_flags = (tail_index >= 0).astype(jnp.float32)
    tail_blocks = jnp.take(blocks, jnp.maximum(tail_index, 0), axis=1)
    head_flags = (jnp.arange(2, dtype=jnp.int32) < live_count).astype(jnp.float32)
    head_blocks = blocks[:, :2]
    return (tail_blocks, tail_flags, head_blocks, head_flags)


def join_left(nearer, farther, pick):
    return jnp.stack([jnp.where(pick, nearer[:, 0], farther[:, 1]), nearer[:, 1]], axis=1)


def join_right(nearer, farther, pick):
    return jnp.stack([nearer[:, 0], jnp.where(pick, nearer[:, 1], farther[:, 0])], axis=1)


def extend(own_blocks, left_pair, right_pair, live_count):
    padded = jnp.concatenate([left_pair, own_blocks, jnp.zeros_like(left_pair)], axis=1)
    return lax.dynamic_update_slice_in_dim(padded, right_pair, live_count + 2, axis=1)


def two_products(residual, precond, image):
    return (
        one_axis_at_a_time(jnp.sum(residual * precond, axis=1), DOM),
        one_axis_at_a_time(jnp.sum(precond * image, axis=1), DOM),
    )


def per_device(wing_jitter, live_blocks, smoothing, displacement, fluid_jitter):
    block_count = wing_jitter.shape[1] // BLK
    fluid_count = fluid_jitter.shape[1] // BLK
    live_count = live_blocks[0]
    factors = jnp.array(stretch_factors, jnp.float32)[:, None, None]
    own_points = wing_jitter.reshape(3, block_count, BLK) * factors
    own_flags = (jnp.arange(block_count, dtype=jnp.int32) < live_count).astype(jnp.float32)
    ends_of = {}
    neighbour_counts = {}
    for offset in (1, 2, -1, -2):
        points, counts = from_behind((own_points, live_blocks), DOM, offset)
        tail_blocks, tail_flags, head_blocks, head_flags = block_ends(points, counts[0])
        neighbour_counts[offset] = counts[0]
        ends_of[offset] = (tail_blocks, tail_flags) if offset > 0 else (head_blocks, head_flags)
    left_pick = ends_of[1][1][0] > 0
    right_pick = ends_of[-1][1][1] > 0
    left_points = join_left(ends_of[1][0], ends_of[2][0], left_pick)
    right_points = join_right(ends_of[-1][0], ends_of[-2][0], right_pick)
    left_flags = join_left(ends_of[1][1][None, :, None], ends_of[2][1][None, :, None], left_pick)
    right_flags = join_right(
        ends_of[-1][1][None, :, None], ends_of[-2][1][None, :, None], right_pick
    )
    ext_points = extend(own_points, left_points, right_points, live_count)
    ext_flags = extend(own_flags[None, :, None], left_flags, right_flags, live_count)
    ext_along = jnp.arange(block_count + 4, dtype=jnp.float32) - 2.0
    ext_points = ext_points.at[0].add(ext_along[:, None]).reshape(3, -1)
    col_flags = jnp.broadcast_to(ext_flags[0], (block_count + 4, BLK)).reshape(-1)
    row_points = (
        own_points.at[0].add(jnp.arange(block_count, dtype=jnp.float32)[:, None]).reshape(3, -1)
    )
    row_mask = jnp.repeat(own_flags, BLK)
    diagonal = 1.0 + smoothing

    def value_context(blocks):
        pieces = {}
        for offset in (1, 2, -1, -2):
            moved = from_behind(blocks, DOM, offset)
            tail_part, tail_marks, head_part, head_marks = block_ends(
                moved, neighbour_counts[offset]
            )
            pieces[offset] = tail_part if offset > 0 else head_part
        left_values = join_left(pieces[1], pieces[2], left_pick)
        right_values = join_right(pieces[-1], pieces[-2], right_pick)
        return extend(blocks, left_values, right_values, live_count).reshape(3, -1)

    def apply(vector):
        ext_values = value_context(vector.reshape(3, block_count, BLK))

        def row_group(group):
            first_row = group * (2 * BLK)
            points = lax.dynamic_slice_in_dim(row_points, first_row, 2 * BLK, 1)
            col_points = lax.dynamic_slice_in_dim(ext_points, first_row, 6 * BLK, 1)
            flags = lax.dynamic_slice_in_dim(col_flags, first_row, 6 * BLK, 0)
            kernel = wendland(points, col_points) * flags[None, :]
            col_values = lax.dynamic_slice_in_dim(ext_values, first_row, 6 * BLK, 1)
            return jnp.einsum("cj,ij->ci", col_values, kernel, precision=lax.Precision.HIGHEST)

        result = lax.map(row_group, jnp.arange(block_count // 2, dtype=jnp.int32))
        result = result.transpose(1, 0, 2).reshape(3, -1)
        return result * row_mask + smoothing * vector

    rhs = displacement * row_mask
    coefs = jnp.zeros_like(rhs)
    residual = rhs
    precond = residual / diagonal
    image = apply(precond)
    norm_now, product = two_products(residual, precond, image)
    step_size = norm_now / product
    direction, along = (precond, image)
    for iteration in range(ITERS):
        coefs = coefs + step_size[:, None] * direction
        residual = residual - step_size[:, None] * along
        if iteration + 1 < ITERS:
            precond = residual / diagonal
            image = apply(precond)
            norm_next, product = two_products(residual, precond, image)
            momentum = norm_next / norm_now
            step_size = norm_next / (product - momentum * norm_next / step_size)
            direction = precond + momentum[:, None] * direction
            along = image + momentum[:, None] * along
            norm_now = norm_next
    anchors = jnp.arange(fluid_count, dtype=jnp.int32) * live_count // fluid_count
    fluid_points = fluid_jitter.reshape(3, fluid_count, BLK) * factors
    fluid_points = fluid_points.at[0].add(anchors.astype(jnp.float32)[:, None])
    coef_ext = value_context(coefs.reshape(3, block_count, BLK))

    def fluid_block(index):
        start_col = anchors[index] * BLK
        points = lax.dynamic_index_in_dim(fluid_points, index, 1, keepdims=False)
        col_points = lax.dynamic_slice_in_dim(ext_points, start_col, 5 * BLK, 1)
        flags = lax.dynamic_slice_in_dim(col_flags, start_col, 5 * BLK, 0)
        kernel = wendland(points, col_points) * flags[None, :]
        col_values = lax.dynamic_slice_in_dim(coef_ext, start_col, 5 * BLK, 1)
        return jnp.einsum("cj,ij->ci", col_values, kernel, precision=lax.Precision.HIGHEST)

    fluid_values = lax.map(fluid_block, jnp.arange(fluid_count, dtype=jnp.int32))
    fluid_values = fluid_values.transpose(1, 0, 2).reshape(3, -1)
    return (coefs, residual, fluid_values)


def solution(mesh):
    finer = Mesh(mesh.devices.reshape(8, 4, 4, 2), ("dom_0", "dom_1", "dom_2", "dom_3"))
    placed = (P(None, DOM), P(DOM), P(DOM), P(None, DOM), P(None, DOM))
    return jax.shard_map(
        per_device,
        mesh=finer,
        in_specs=placed,
        out_specs=(P(None, DOM), P(None, DOM), P(None, DOM)),
        check_vma=False,
    )
```

profile of v0, /device:TPU:1, one launch (start us, length us, event | category | flops | bytes accessed | tf_op | source)
XLA Modules:
  0.0 649.0 jit_solution(5733201510378834206)
XLA Ops:
  0.6 4.6 collective-permute-start
  9.0 3.2 collective-permute-start.2
  12.2 3.5 collective-permute-start.3
  15.8 3.2 collective-permute-start.7
  19.1 3.2 collective-permute-start.8
  23.0 1.9 collective-permute-start.5
  25.6 2.5 collective-permute-done.5
  48.8 3.2 collective-permute-done.6
  52.1 91.1 %while.51 = (s32[]{:T(128)}, f32[32,3,256]{2,1,0:T(4,128)S(1)}, s32[32]{0:T(128)S(1)}, f32[3,8704]{1,0:T(4,128)S(1)}, f32[3,8192]{1,0:T(4,128)S(1)}, /*index=5*/...) while((s32[]{:T(128)}, f32[32,3,256]{2,1,0:T(4,128)S(1)}, ...), condition=%wide.region_6.8_spmd, body=%wide.region_5.7_spmd.sunk | while | flops 10616842 | bytes 66836 | solution.py:122
  143.5 27.7 %all-reduce.2 = (f32[3]{0:T(128)S(1)}, f32[3]{0:T(128)S(1)}) all-reduce(f32[3]{0:T(128)S(1)} %get-tuple-element.425, f32[3]{0:T(128)S(1)} %get-tuple-element.424), channel_id=1, replica_groups=mesh['dom_0'=8,'dom_1'=4,'dom_2'=4,'dom_3'=2] {'dom_0'}, use_global_device_ids=true, to_apply=%region_1.2 | all-reduce | flops 6 | bytes 48 | tf_op jit(solution)/shard_map/psum | solution.py:17
  171.2 6.0 all-reduce.8
  177.2 12.5 %all-reduce.5 = (f32[3]{0:T(128)S(1)}, f32[3]{0:T(128)S(1)}) all-reduce(f32[3]{0:T(128)S(1)} %get-tuple-element.504, f32[3]{0:T(128)S(1)} %get-tuple-element.505), channel_id=1, replica_groups=mesh['dom_0'=8,'dom_1'=4,'dom_2'=4,'dom_3'=2] {'dom_2'}, use_global_device_ids=true, to_apply=%region_3.4 | all-reduce | flops 6 | bytes 48 | tf_op jit(solution)/shard_map/psum | solution.py:17
  189.7 10.2 %all-reduce.11 = (f32[3]{0:T(128)S(1)}, f32[3]{0:T(128)S(1)}) all-reduce(f32[3]{0:T(128)S(1)} %get-tuple-element.498, f32[3]{0:T(128)S(1)} %get-tuple-element.499), channel_id=1, replica_groups=mesh['dom_0'=8,'dom_1'=4,'dom_2'=4,'dom_3'=2] {'dom_3'}, use_global_device_ids=true, to_apply=%region_4.5 | all-reduce | flops 6 | bytes 48 | tf_op jit(solution)/shard_map/psum | solution.py:17
  201.4 2.2 collective-permute-start.14
  205.0 3.9 collective-permute-start.12
  211.7 91.6 %while.52 = (s32[]{:T(128)}, f32[32,3,256]{2,1,0:T(4,128)S(1)}, s32[32]{0:T(128)S(1)}, f32[3,8704]{1,0:T(4,128)S(1)}, f32[3,8192]{1,0:T(4,128)S(1)}, /*index=5*/...) while((s32[]{:T(128)}, f32[32,3,256]{2,1,0:T(4,128)S(1)}, ...), condition=%wide.region_18.20_spmd, body=%wide.region_17.19_spmd.sunk | while | flops 10616842 | bytes 66836 | solution.py:122
  303.5 18.6 %all-reduce.1 = (f32[3]{0:T(128)S(1)}, f32[3]{0:T(128)S(1)}) all-reduce(f32[3]{0:T(128)S(1)} %get-tuple-element.427, f32[3]{0:T(128)S(1)} %get-tuple-element.426), channel_id=1, replica_groups=mesh['dom_0'=8,'dom_1'=4,'dom_2'=4,'dom_3'=2] {'dom_0'}, use_global_device_ids=true, to_apply=%region_13.15 | all-reduce | flops 6 | bytes 48 | tf_op jit(solution)/shard_map/psum | solution.py:17
  322.2 6.0 all-reduce.7
  328.1 12.3 %all-reduce.4 = (f32[3]{0:T(128)S(1)}, f32[3]{0:T(128)S(1)}) all-reduce(f32[3]{0:T(128)S(1)} %get-tuple-element.502, f32[3]{0:T(128)S(1)} %get-tuple-element.503), channel_id=1, replica_groups=mesh['dom_0'=8,'dom_1'=4,'dom_2'=4,'dom_3'=2] {'dom_2'}, use_global_device_ids=true, to_apply=%region_15.17 | all-reduce | flops 6 | bytes 48 | tf_op jit(solution)/shard_map/psum | solution.py:17
  340.5 9.3 %all-reduce.10 = (f32[3]{0:T(128)S(1)}, f32[3]{0:T(128)S(1)}) all-reduce(f32[3]{0:T(128)S(1)} %get-tuple-element.496, f32[3]{0:T(128)S(1)} %get-tuple-element.497), channel_id=1, replica_groups=mesh['dom_0'=8,'dom_1'=4,'dom_2'=4,'dom_3'=2] {'dom_3'}, use_global_device_ids=true, to_apply=%region_16.18 | all-reduce | flops 6 | bytes 48 | tf_op jit(solution)/shard_map/psum | solution.py:17
  350.0 3.6 collective-permute-start.17
  353.7 2.5 collective-permute-start.18
  357.5 3.7 collective-permute-start.16
  364.0 91.1 %while.53 = (s32[]{:T(128)}, f32[32,3,256]{2,1,0:T(4,128)S(1)}, s32[32]{0:T(128)S(1)}, f32[3,8704]{1,0:T(4,128)S(1)}, f32[3,8192]{1,0:T(4,128)S(1)}, /*index=5*/...) while((s32[]{:T(128)}, f32[32,3,256]{2,1,0:T(4,128)S(1)}, ...), condition=%wide.region_30.32_spmd, body=%wide.region_29.31_spmd.sunk | while | flops 10616842 | bytes 66836 | solution.py:122
  455.3 17.8 %all-reduce = (f32[3]{0:T(128)S(1)}, f32[3]{0:T(128)S(1)}) all-reduce(f32[3]{0:T(128)S(1)} %get-tuple-element.429, f32[3]{0:T(128)S(1)} %get-tuple-element.428), channel_id=1, replica_groups=mesh['dom_0'=8,'dom_1'=4,'dom_2'=4,'dom_3'=2] {'dom_0'}, use_global_device_ids=true, to_apply=%region_25.27 | all-reduce | flops 6 | bytes 48 | tf_op jit(solution)/shard_map/psum | solution.py:17
  473.2 6.0 all-reduce.6
  479.2 10.8 %all-reduce.3 = (f32[3]{0:T(128)S(1)}, f32[3]{0:T(128)S(1)}) all-reduce(f32[3]{0:T(128)S(1)} %get-tuple-element.500, f32[3]{0:T(128)S(1)} %get-tuple-element.501), channel_id=1, replica_groups=mesh['dom_0'=8,'dom_1'=4,'dom_2'=4,'dom_3'=2] {'dom_2'}, use_global_device_ids=true, to_apply=%region_27.29 | all-reduce | flops 6 | bytes 48 | tf_op jit(solution)/shard_map/psum | solution.py:17
  489.9 10.1 %all-reduce.9 = (f32[3]{0:T(128)S(1)}, f32[3]{0:T(128)S(1)}) all-reduce(f32[3]{0:T(128)S(1)} %get-tuple-element.494, f32[3]{0:T(128)S(1)} %get-tuple-element.495), channel_id=1, replica_groups=mesh['dom_0'=8,'dom_1'=4,'dom_2'=4,'dom_3'=2] {'dom_3'}, use_global_device_ids=true, to_apply=%region_28.30 | all-reduce | flops 6 | bytes 48 | tf_op jit(solution)/shard_map/psum | solution.py:17
  500.9 3.6 collective-permute-start.21
  504.6 2.5 collective-permute-start.22
  508.5 3.7 collective-permute-start.20
  514.9 134.1 %while.54 = (s32[]{:T(128)}, f32[24,3,128]{2,1,0:T(4,128)}, s32[24]{0:T(128)S(1)}, s32[24]{0:T(128)S(1)}, f32[3,8704]{1,0:T(4,128)S(1)}, /*index=5*/f32[3,24,128...) while((s32[]{:T(128)}, f32[24,3,128]{2,1,0:T(4,128)}, ...), condition=%wide.region_37.39_spmd, body=%wide.region_36.38_spmd.sunk | while | flops 4423691 | bytes 54573 | solution.py:160
  (757 shorter events, 313.6 us)
Async XLA Ops:
  0.6 5.4 copy-start.1
  0.6 18.4 %collective-permute-start = (s32[1]{0:T(128)}, s32[1]{0:T(128)}, u32[]{:S(2)}, u32[]{:S(2)}) collective-permute-start(s32[1]{0:T(128)} %param.23), channel_id=1, source_target_pairs={{0,1},{1,2},{2,3},{3,4},{4,5},{5,6},{6,7},{7,8},{8,9},{9,10},{10,1... | collective-permute-start | bytes 20 | tf_op jit(solution)/shard_map/ppermute | solution.py:24
  6.0 9.7 %copy-start.3 = (f32[3,8192]{1,0:T(4,128)S(1)}, f32[3,8192]{1,0:T(4,128)}, u32[]{:S(2)}) copy-start(f32[3,8192]{1,0:T(4,128)} %param.22) | copy-start | bytes 294916
  6.0 9.7 %copy-start.5 = (f32[3]{0:T(128)S(1)}, f32[3]{0:T(128)}, u32[]{:S(2)}) copy-start(f32[3]{0:T(128)} %constant.335.clone) | copy-start | bytes 40
  7.0 32.3 %collective-permute-start.1 = (f32[3,64,128]{2,0,1:T(4,128)S(1)}, f32[3,64,128]{2,0,1:T(4,128)S(1)}, u32[]{:S(2)}, u32[]{:S(2)}) collective-permute-start(f32[3,64,128]{2,0,1:T(4,128)S(1)} %fusion.150), channel_id=1, source_target_pairs={{0,1},{1,2},{2,3},{3,4},{4,5},{5,6},{6,7},{7,8},{8,9},{9,10},{10,1... | collective-permute-start | bytes 294920 | tf_op jit(solution)/shard_map/ppermute | solution.py:24
  9.0 35.4 %collective-permute-start.2 = (f32[3,64,128]{2,0,1:T(4,128)S(1)}, f32[3,64,128]{2,0,1:T(4,128)S(1)}, u32[]{:S(2)}, u32[]{:S(2)}) collective-permute-start(f32[3,64,128]{2,0,1:T(4,128)S(1)} %fusion.150), channel_id=1, source_target_pairs={{0,2},{1,3},{2,4},{3,5},{4,6},{5,7},{6,8},{7,9},{8,10},{9,11},{10,... | collective-permute-start | bytes 294920 | tf_op jit(solution)/shard_map/ppermute | solution.py:24
  12.2 10.8 %collective-permute-start.3 = (s32[1]{0:T(128)}, s32[1]{0:T(128)}, u32[]{:S(2)}, u32[]{:S(2)}) collective-permute-start(s32[1]{0:T(128)} %param.23), channel_id=1, source_target_pairs={{0,2},{1,3},{2,4},{3,5},{4,6},{5,7},{6,8},{7,9},{8,10},{9,11},{10,... | collective-permute-start | bytes 20 | tf_op jit(solution)/shard_map/ppermute | solution.py:24
  15.8 26.0 %collective-permute-start.7 = (f32[3,64,128]{2,0,1:T(4,128)S(1)}, f32[3,64,128]{2,0,1:T(4,128)S(1)}, u32[]{:S(2)}, u32[]{:S(2)}) collective-permute-start(f32[3,64,128]{2,0,1:T(4,128)S(1)} %bitcast_multiply_fusion), channel_id=1, source_target_pairs={{0,1},{1,2},{2,3},{3,4},{4,5},{5,6},{6,7},{7,8},{8,9},{9,10},{10,1... | collective-permute-start | bytes 294920 | tf_op jit(solution)/shard_map/ppermute | solution.py:24
  19.1 27.2 %collective-permute-start.8 = (f32[3,64,128]{2,0,1:T(4,128)S(1)}, f32[3,64,128]{2,0,1:T(4,128)S(1)}, u32[]{:S(2)}, u32[]{:S(2)}) collective-permute-start(f32[3,64,128]{2,0,1:T(4,128)S(1)} %bitcast_multiply_fusion), channel_id=1, source_target_pairs={{0,2},{1,3},{2,4},{3,5},{4,6},{5,7},{6,8},{7,9},{8,10},{9,11},{10,... | collective-permute-start | bytes 294920 | tf_op jit(solution)/shard_map/ppermute | solution.py:24
  23.0 5.1 collective-permute-start.5
  28.1 6.5 collective-permute-start.11
  34.6 12.5 %collective-permute-start.10 = (f32[3,64,128]{2,0,1:T(4,128)S(1)}, f32[3,64,128]{2,0,1:T(4,128)S(1)}, u32[]{:S(2)}, u32[]{:S(2)}) collective-permute-start(f32[3,64,128]{2,0,1:T(4,128)S(1)} %bitcast_multiply_fusion), channel_id=1, source_target_pairs={{2,0},{3,1},{4,2},{5,3},{6,4},{7,5},{8,6},{9,7},{10,8},{11,9},{12,... | collective-permute-start | bytes 294920 | tf_op jit(solution)/shard_map/ppermute | solution.py:24
  39.3 7.8 %collective-permute-start.9 = (f32[3,64,128]{2,0,1:T(4,128)S(1)}, f32[3,64,128]{2,0,1:T(4,128)S(1)}, u32[]{:S(2)}, u32[]{:S(2)}) collective-permute-start(f32[3,64,128]{2,0,1:T(4,128)S(1)} %bitcast_multiply_fusion), channel_id=1, source_target_pairs={{1,0},{2,1},{3,2},{4,3},{5,4},{6,5},{7,6},{8,7},{9,8},{10,9},{11,1... | collective-permute-start | bytes 294920 | tf_op jit(solution)/shard_map/ppermute | solution.py:24
  41.8 7.0 %collective-permute-start.4 = (f32[3,64,128]{2,0,1:T(4,128)S(1)}, f32[3,64,128]{2,0,1:T(4,128)S(1)}, u32[]{:S(2)}, u32[]{:S(2)}) collective-permute-start(f32[3,64,128]{2,0,1:T(4,128)S(1)} %fusion.150), channel_id=1, source_target_pairs={{1,0},{2,1},{3,2},{4,3},{5,4},{6,5},{7,6},{8,7},{9,8},{10,9},{11,1... | collective-permute-start | bytes 294920 | tf_op jit(solution)/shard_map/ppermute | solution.py:24
  44.4 7.7 %collective-permute-start.6 = (f32[3,64,128]{2,0,1:T(4,128)S(1)}, f32[3,64,128]{2,0,1:T(4,128)S(1)}, u32[]{:S(2)}, u32[]{:S(2)}) collective-permute-start(f32[3,64,128]{2,0,1:T(4,128)S(1)} %fusion.150), channel_id=1, source_target_pairs={{2,0},{3,1},{4,2},{5,3},{6,4},{7,5},{8,6},{9,7},{10,8},{11,9},{12,... | collective-permute-start | bytes 294920 | tf_op jit(solution)/shard_map/ppermute | solution.py:24
  52.1 91.1 %copy-start = (f32[3,8192]{1,0:T(4,128)S(1)}, f32[3,8192]{1,0:T(4,128)}, u32[]{:S(2)}) copy-start(f32[3,8192]{1,0:T(4,128)} %param.25) | copy-start | bytes 294916
  199.9 1.4 copy-start.4
  200.0 8.9 %collective-permute-start.13 = (f32[3,64,128]{2,0,1:T(4,128)S(1)}, f32[3,64,128]{2,0,1:T(4,128)S(1)}, u32[]{:S(2)}, u32[]{:S(2)}) collective-permute-start(f32[3,64,128]{2,0,1:T(4,128)S(1)} %get-tuple-element.519), channel_id=1, source_target_pairs={{0,2},{1,3},{2,4},{3,5},{4,6},{5,7},{6,8},{7,9},{8,10},{9,11},{10,... | collective-permute-start | bytes 294920 | tf_op jit(solution)/shard_map/ppermute | solution.py:24
  201.4 10.2 %collective-permute-start.14 = (f32[3,64,128]{2,0,1:T(4,128)S(1)}, f32[3,64,128]{2,0,1:T(4,128)S(1)}, u32[]{:S(2)}, u32[]{:S(2)}) collective-permute-start(f32[3,64,128]{2,0,1:T(4,128)S(1)} %get-tuple-element.519), channel_id=1, source_target_pairs={{1,0},{2,1},{3,2},{4,3},{5,4},{6,5},{7,6},{8,7},{9,8},{10,9},{11,1... | collective-permute-start | bytes 294920 | tf_op jit(solution)/shard_map/ppermute | solution.py:24
  203.7 8.0 %collective-permute-start.15 = (f32[3,64,128]{2,0,1:T(4,128)S(1)}, f32[3,64,128]{2,0,1:T(4,128)S(1)}, u32[]{:S(2)}, u32[]{:S(2)}) collective-permute-start(f32[3,64,128]{2,0,1:T(4,128)S(1)} %get-tuple-element.519), channel_id=1, source_target_pairs={{2,0},{3,1},{4,2},{5,3},{6,4},{7,5},{8,6},{9,7},{10,8},{11,9},{12,... | collective-permute-start | bytes 294920 | tf_op jit(solution)/shard_map/ppermute | solution.py:24
  205.0 5.9 collective-permute-start.12
  350.0 11.2 %collective-permute-start.17 = (f32[3,64,128]{2,0,1:T(4,128)S(1)}, f32[3,64,128]{2,0,1:T(4,128)S(1)}, u32[]{:S(2)}, u32[]{:S(2)}) collective-permute-start(f32[3,64,128]{2,0,1:T(4,128)S(1)} %bitcast.162), channel_id=1, source_target_pairs={{0,2},{1,3},{2,4},{3,5},{4,6},{5,7},{6,8},{7,9},{8,10},{9,11},{10,... | collective-permute-start | bytes 294920 | tf_op jit(solution)/shard_map/ppermute | solution.py:24
  353.7 10.2 %collective-permute-start.18 = (f32[3,64,128]{2,0,1:T(4,128)S(1)}, f32[3,64,128]{2,0,1:T(4,128)S(1)}, u32[]{:S(2)}, u32[]{:S(2)}) collective-permute-start(f32[3,64,128]{2,0,1:T(4,128)S(1)} %bitcast.163), channel_id=1, source_target_pairs={{1,0},{2,1},{3,2},{4,3},{5,4},{6,5},{7,6},{8,7},{9,8},{10,9},{11,1... | collective-permute-start | bytes 294920 | tf_op jit(solution)/shard_map/ppermute | solution.py:24
  356.2 7.7 %collective-permute-start.19 = (f32[3,64,128]{2,0,1:T(4,128)S(1)}, f32[3,64,128]{2,0,1:T(4,128)S(1)}, u32[]{:S(2)}, u32[]{:S(2)}) collective-permute-start(f32[3,64,128]{2,0,1:T(4,128)S(1)} %bitcast.164), channel_id=1, source_target_pairs={{2,0},{3,1},{4,2},{5,3},{6,4},{7,5},{8,6},{9,7},{10,8},{11,9},{12,... | collective-permute-start | bytes 294920 | tf_op jit(solution)/shard_map/ppermute | solution.py:24
  357.5 5.6 collective-permute-start.16
  500.9 13.9 %copy-start.2 = (f32[3,8192]{1,0:T(4,128)}, f32[3,8192]{1,0:T(4,128)S(1)}, u32[]{:S(2)}) copy-start(f32[3,8192]{1,0:T(4,128)S(1)} %get-tuple-element.534) | copy-start | bytes 294916
  500.9 11.2 %collective-permute-start.21 = (f32[3,64,128]{2,0,1:T(4,128)S(1)}, f32[3,64,128]{2,0,1:T(4,128)S(1)}, u32[]{:S(2)}, u32[]{:S(2)}) collective-permute-start(f32[3,64,128]{2,0,1:T(4,128)S(1)} %bitcast.176), channel_id=1, source_target_pairs={{0,2},{1,3},{2,4},{3,5},{4,6},{5,7},{6,8},{7,9},{8,10},{9,11},{10,... | collective-permute-start | bytes 294920 | tf_op jit(solution)/shard_map/ppermute | solution.py:24
  504.6 10.2 %collective-permute-start.22 = (f32[3,64,128]{2,0,1:T(4,128)S(1)}, f32[3,64,128]{2,0,1:T(4,128)S(1)}, u32[]{:S(2)}, u32[]{:S(2)}) collective-permute-start(f32[3,64,128]{2,0,1:T(4,128)S(1)} %bitcast.177), channel_id=1, source_target_pairs={{1,0},{2,1},{3,2},{4,3},{5,4},{6,5},{7,6},{8,7},{9,8},{10,9},{11,1... | collective-permute-start | bytes 294920 | tf_op jit(solution)/shard_map/ppermute | solution.py:24
  507.2 7.7 %collective-permute-start.23 = (f32[3,64,128]{2,0,1:T(4,128)S(1)}, f32[3,64,128]{2,0,1:T(4,128)S(1)}, u32[]{:S(2)}, u32[]{:S(2)}) collective-permute-start(f32[3,64,128]{2,0,1:T(4,128)S(1)} %bitcast.178), channel_id=1, source_target_pairs={{2,0},{3,1},{4,2},{5,3},{6,4},{7,5},{8,6},{9,7},{10,8},{11,9},{12,... | collective-permute-start | bytes 294920 | tf_op jit(solution)/shard_map/ppermute | solution.py:24
  508.5 5.6 collective-permute-start.20
where the time goes:
time: 660 us; the launch traced here: 649 us
  matrix products  157 us (24%)
  blocking collectives  147 us (22%)
  loops' own time  131 us (20%)
  local copies, waits for them, and re-layouts  130 us (20%)
  starting transfers between devices  60.2 us (9%)
  waiting for transfers between devices  9.53 us (1%)
  other arithmetic  8.15 us (1%)
    psum x12, blocking collectives, one_axis_at_a_time(): shard = lax.psum(shard, axis)  147 us
    dot_general x96, matrix products, row_group(): jnp.einsum('cj,ij->ci', col_values, kernel, precision=lax.Precision.HIGHEST)  126 us
    another operation x1, loops' own time, per_device(): lax.map(fluid_block, jnp.arange(fluid_count, dtype=jnp.int32))  66.8 us
    another operation x3, loops' own time, apply(): result = lax.map(row_group, jnp.arange(block_count // 2, dtype=jnp.int32))  64.4 us
    ppermute x24, starting transfers between devices, from_behind(): return lax.ppermute(block, axis, route)  60.2 us
    dynamic_slice x96, local copies, waits for them, and re-layouts, apply(): result = lax.map(row_group, jnp.arange(block_count // 2, dtype=jnp.int32))  58.6 us
    dot_general x24, matrix products, fluid_block(): jnp.einsum('cj,ij->ci', col_values, kernel, precision=lax.Precision.HIGHEST)  30.9 us
    slice x216, local copies, waits for them, and re-layouts, wendland(): spread = (row_points[0][:, None] - col_points[0][None, :]) ** 2  20 us
  transfers between devices with their start and end apart: 24, of which 5 were waited for; matrix products, arithmetic and copies ran while one was open for 2% of the time, Pallas kernels for 0%

commit v1 on v0

v1 whole, which is shorter than its diff:
```python
import functools
import jax
import jax.numpy as jnp
from jax import lax
from jax.experimental import pallas as pl
from jax.experimental.pallas import tpu as pltpu
from jax.sharding import PartitionSpec as P

BLK = 128
ITERS = 3
HALO = 6
BASE = 2 * HALO
NEAR = 4
PIECES = 48
MAX_AMPLIFICATION = 50.0

stretch_factors = (1.0, 6.0, 6.0)


def pack_kernel(live_ref, jitter_ref, smoothing_ref, displacement_ref, ends_ref):
    live = live_ref[0]
    count = jnp.full((1, BLK), jnp.minimum(live, HALO), jnp.int32).astype(jnp.float32)
    for slot in range(HALO):
        tail_block = live - HALO + slot
        tail_start = pl.multiple_of(jnp.maximum(tail_block, 0) * BLK, BLK)
        starts = ((tail_block >= 0, tail_start), (slot < live, slot * BLK))
        for end, (kept, start) in enumerate(starts):
            lanes = pl.ds(start, BLK)
            mask = kept.astype(jnp.float32)
            ends_ref[end, slot, 0:3, :] = jitter_ref[:, lanes] * mask
            ends_ref[end, slot, 3:4, :] = smoothing_ref[:, lanes] * mask
            ends_ref[end, slot, 4:7, :] = displacement_ref[:, lanes] * mask
            ends_ref[end, slot, 7:8, :] = count


def count_in(row):
    return jnp.max(row).astype(jnp.int32)


def join_kernel(axes, end, near_ref, far_ref, joined_ref, buffer):
    core = lax.rem(lax.axis_index(axes), 2)
    near = near_ref[core] if end else near_ref[...]
    far = far_ref[core] if end else far_ref[...]
    count = near[0, 7:8, :] + far[0, 7:8, :]
    held = count_in(near[0, 7:8, :])
    buffer[pl.ds(HALO, HALO)] = near
    buffer[pl.ds(HALO + jnp.where(core == 0, -held, held), HALO)] = far
    joined_ref[...] = buffer[pl.ds(HALO, HALO)]
    for slot in range(HALO):
        joined_ref[slot, 7:8, :] = jnp.minimum(count, float(HALO))


def split(values):
    high = values.astype(jnp.bfloat16).astype(jnp.float32)
    rest = values - high
    middle = rest.astype(jnp.bfloat16).astype(jnp.float32)
    return high, middle, rest - middle


def rows_of(row):
    return lax.broadcasted_iota(jnp.int32, (8, BLK), 0) == row


def centred(jitter):
    row = lax.broadcasted_iota(jnp.int32, (8, BLK), 0)
    scale = jnp.where(row == 0, 0.5, 3.0)
    shift = jnp.where(row == 0, 0.25, 1.5)
    return jnp.where(row < 3, jitter * scale - shift, 0.0)


def source_rows(points, norm):
    extended = jnp.where(rows_of(3), norm, jnp.where(rows_of(4), 1.0, points))
    high, middle, low = split(extended)
    return jnp.concatenate([high, high, middle, high, low, middle], axis=0)


def target_parts(points, norm):
    base = jnp.where(rows_of(4), norm, -2.0 * points)
    slope = jnp.where(rows_of(0), 1.0, jnp.where(rows_of(4), -points[0:1], 0.0))
    return base, slope


def target_rows(base, slope, delta):
    moved = base + float(delta) * slope + jnp.where(rows_of(4), 0.25 * delta * delta, 0.0)
    high, middle, low = split(moved)
    first = jnp.where(rows_of(3), 1.0, high)
    return jnp.concatenate([first, middle, first, low, first, middle], axis=0).astype(jnp.bfloat16)


def wendland_of_quarter(quarter):
    quarter = jnp.maximum(quarter, 1e-30)
    scaled = quarter * lax.rsqrt(quarter)
    remain = jnp.maximum(1.0 - scaled, 0.0)
    square = remain * remain
    return square * square * (4.0 * scaled + 1.0)


def store_pair(ref, values, first_row):
    high = values.astype(jnp.bfloat16)
    low = (values - high.astype(jnp.float32)).astype(jnp.bfloat16)
    ref[pl.ds(first_row, BLK), 0:BLK] = high
    ref[pl.ds(first_row, BLK), BLK : 2 * BLK] = low


def vector_pair(values):
    high = values.astype(jnp.bfloat16).astype(jnp.float32)
    return jnp.concatenate([high, values - high], axis=0).astype(jnp.bfloat16)


def sum_pairs(product, first):
    upper = product[first : first + 8] + product[first + 8 : first + 16]
    return upper[:, :BLK] + upper[:, BLK:]


def chain_kernel(
    axes, block_count, fluid_count,
    live_ref, jitter_ref, smoothing_ref, displacement_ref, fluid_ref, partner_ref, mine_ref, other_ref,
    w1_ref, w2_ref, w3_ref, moments_ref, fluid_basis_ref,
    joined, source, base, slope, inverse, w0, z0, z1, z2, b0, b1, b2, matrix, fluid_matrix,
):
    live = live_ref[0]
    width = block_count + 2 * HALO

    for extra in range(HALO):
        joined[BASE + block_count + extra] = jnp.zeros((8, BLK), jnp.float32)

    def put_own(block, carry):
        lanes = pl.ds(pl.multiple_of(block * BLK, BLK), BLK)
        kept = (block < live).astype(jnp.float32)
        joined[BASE + block, 0:3, :] = jitter_ref[:, lanes]
        joined[BASE + block, 3:4, :] = smoothing_ref[:, lanes] * kept
        joined[BASE + block, 4:7, :] = displacement_ref[:, lanes]
        return carry

    lax.fori_loop(0, block_count, put_own, 0, unroll=8)
    core = lax.rem(lax.axis_index(axes), 2)
    mine, other = mine_ref[...], other_ref[...]
    left_near = jnp.where(core == 0, 0, count_in(partner_ref[0, 0, 7:8, :]))
    right_near = jnp.where(core == 0, count_in(partner_ref[1, 0, 7:8, :]), 0)
    joined[pl.ds(BASE - HALO, HALO)] = partner_ref[0]
    joined[pl.ds(BASE - HALO - left_near, HALO)] = jnp.where(core == 0, mine, other)
    joined[pl.ds(BASE + live, HALO)] = partner_ref[1]
    joined[pl.ds(BASE + live + right_near, HALO)] = jnp.where(core == 0, other, mine)

    def prepare(block, carry):
        packed = joined[BASE - HALO + block]
        points = centred(packed)
        norm = jnp.sum(points * points, axis=0, keepdims=True)
        source[block] = jnp.transpose(source_rows(points, norm)).astype(jnp.bfloat16)
        base[block], slope[block] = target_parts(points, norm)
        scale = jnp.where(packed[3:4] > 0.0, 1.0 / (1.0 + packed[3:4]), 0.0)
        scale = jnp.broadcast_to(scale, (8, BLK))
        rhs = jnp.concatenate([packed[4:7], jnp.zeros((5, BLK), jnp.float32)], axis=0)
        inverse[block] = scale
        w0[block] = rhs
        z0[block] = rhs * scale
        b0[block] = vector_pair(rhs * scale)
        return carry

    lax.fori_loop(0, width, prepare, 0, unroll=4)

    def generate(row, carry):
        for place in range(5):
            columns = target_rows(base[row + 2], slope[row + 2], place - 2)
            quarter = jnp.dot(source[row + place], columns, preferred_element_type=jnp.float32)
            store_pair(matrix.at[row], wendland_of_quarter(quarter), place * BLK)
        return carry

    lax.fori_loop(0, block_count + 2 * NEAR, generate, 0)

    def apply(values, pairs, first, last, place_next):
        def one_row(row, carry):
            near = jnp.concatenate([pairs[row + place] for place in range(5)], axis=1)
            product = jnp.dot(near, matrix[row], preferred_element_type=jnp.float32)
            place_next(row + 2, sum_pairs(product, 0) - values[row + 2])
            return carry

        lax.fori_loop(first, last, one_row, 0, unroll=4)

    rows = block_count + 2 * NEAR

    def first_next(block, image):
        scaled = image * inverse[block]
        z1[block] = scaled
        b1[block] = vector_pair(scaled)
        w1_ref[block] = image

    def second_next(block, image):
        scaled = image * inverse[block]
        z2[block] = scaled
        b2[block] = vector_pair(scaled)
        w2_ref[block] = image

    def third_next(block, image):
        w3_ref[block] = image

    apply(z0, b0, 0, rows, first_next)
    apply(z1, b1, 2, rows - 2, second_next)
    apply(z2, b2, 4, rows - 4, third_next)

    def add_up(own, sums):
        block = own + HALO
        kept = (own < live).astype(jnp.float32)
        third = w3_ref[block]
        pairs = (
            (z0[block], w0[block]),
            (z0[block], w1_ref[block]),
            (z1[block], w1_ref[block]),
            (z1[block], w2_ref[block]),
            (z2[block], w2_ref[block]),
            (z2[block], third),
            (third * inverse[block], third),
        )
        return tuple(s + kept * (a * b) for s, (a, b) in zip(sums, pairs))

    zero = jnp.zeros((8, BLK), jnp.float32)
    sums = lax.fori_loop(0, block_count, add_up, (zero,) * 7, unroll=4)
    lane = lax.broadcasted_iota(jnp.int32, (8, BLK), 1)
    moments = zero
    for k in range(7):
        moments = jnp.where(lane == k, jnp.sum(sums[k], axis=1, keepdims=True), moments)
    moments_ref[...] = moments

    def fluid_block(index, carry):
        anchor = lax.div(index * live, jnp.int32(fluid_count))
        lanes = pl.ds(pl.multiple_of(index * BLK, BLK), BLK)
        jitter = jnp.concatenate([fluid_ref[:, lanes], jnp.zeros((5, BLK), jnp.float32)], axis=0)
        points = centred(jitter)
        norm = jnp.sum(points * points, axis=0, keepdims=True)
        base_here, slope_here = target_parts(points, norm)
        near = []
        for place in range(5):
            block = anchor + (HALO - 2 + place)
            columns = target_rows(base_here, slope_here, place - 2)
            quarter = jnp.dot(source[block], columns, preferred_element_type=jnp.float32)
            store_pair(fluid_matrix, wendland_of_quarter(quarter), place * BLK)
            near.append(jnp.concatenate([b0[block], b1[block], b2[block]], axis=0))
        near = jnp.concatenate(near, axis=1)
        product = jnp.dot(near, fluid_matrix[...], preferred_element_type=jnp.float32)
        for k in range(3):
            fluid_basis_ref[index, k] = sum_pairs(product, 16 * k)
        return carry

    lax.fori_loop(0, fluid_count, fluid_block, 0)


def step_coefficients(moments):
    def inner(left, right):
        total = 0.0
        for i, a in enumerate(left):
            for j, b in enumerate(right):
                total = total + a * b * moments[i + j]
        return total

    one = jnp.ones_like(moments[0])
    solution_part, residual, direction = [], [one], [one]
    norm = moments[0]
    for iteration in range(ITERS):
        image = [
            (direction[k] if k < len(direction) else 0.0) + (direction[k - 1] if k else 0.0)
            for k in range(len(direction) + 1)
        ]
        step = norm / inner(direction, image)
        old = solution_part + [0.0] * (len(direction) - len(solution_part))
        solution_part = [a + step * b for a, b in zip(old, direction)]
        residual = [
            (residual[k] if k < len(residual) else 0.0) - step * image[k] for k in range(len(image))
        ]
        following = inner(residual, residual)
        ratio = following / norm
        direction = [
            residual[k] + ratio * (direction[k] if k < len(direction) else 0.0)
            for k in range(len(residual))
        ]
        norm = following
    spread = 0.0
    for k, a in enumerate(residual):
        spread = spread + jnp.abs(a) * jnp.sqrt(jnp.maximum(moments[2 * k], 0.0))
    return solution_part, residual, spread * spread <= MAX_AMPLIFICATION**2 * norm


def finish_kernel(
    block_count, fluid_count, live_ref, moments_ref, smoothing_ref, displacement_ref,
    w1_ref, w2_ref, w3_ref, fluid_basis_ref, coefs_ref, residual_ref, fluid_ref, good_ref,
):
    live = live_ref[0]
    moments = moments_ref[...]
    solved, left, good = step_coefficients([moments[:, k : k + 1] for k in range(7)])
    row = lax.broadcasted_iota(jnp.int32, (8, 1), 0)
    good_ref[0] = jnp.min(jnp.where(good | (row > 2), 1.0, 0.0)).astype(jnp.int32)
    solved = [jnp.broadcast_to(v, (8, BLK))[0:3] for v in solved]
    left = [jnp.broadcast_to(v, (8, BLK))[0:3] for v in left]

    def one_block(own, carry):
        lanes = pl.ds(pl.multiple_of(own * BLK, BLK), BLK)
        block = own + HALO
        parts = [displacement_ref[:, lanes]] + [r[block][0:3] for r in (w1_ref, w2_ref, w3_ref)]
        scaled = sum(a * b for a, b in zip(solved, parts)) / (1.0 + smoothing_ref[:, lanes])
        remaining = sum(a * b for a, b in zip(left, parts))
        is_live = own < live
        coefs_ref[:, lanes] = jnp.where(is_live, scaled, 0.0)
        residual_ref[:, lanes] = jnp.where(is_live, remaining, 0.0)
        return carry

    lax.fori_loop(0, block_count, one_block, 0, unroll=4)

    def one_fluid(index, carry):
        lanes = pl.ds(pl.multiple_of(index * BLK, BLK), BLK)
        fluid_ref[:, lanes] = sum(a * fluid_basis_ref[index, k][0:3] for k, a in enumerate(solved))
        return carry

    lax.fori_loop(0, fluid_count, one_fluid, 0, unroll=4)


def wendland(row_points, col_points):
    spread = (row_points[0][:, None] - col_points[0][None, :]) ** 2
    spread = spread + (row_points[1][:, None] - col_points[1][None, :]) ** 2
    spread = spread + (row_points[2][:, None] - col_points[2][None, :]) ** 2
    scaled = jnp.sqrt(spread) * 0.5
    remain = jnp.maximum(1.0 - scaled, 0.0)
    return remain * remain * remain * remain * (4.0 * scaled + 1.0)


def block_ends(blocks, live_count):
    tail_index = live_count - 2 + jnp.arange(2, dtype=jnp.int32)
    tail_flags = (tail_index >= 0).astype(jnp.float32)
    padded = jnp.pad(blocks, ((0, 0), (2, 0), (0, 0)))
    tail_blocks = lax.dynamic_slice_in_dim(padded, live_count, 2, axis=1)
    head_flags = (jnp.arange(2, dtype=jnp.int32) < live_count).astype(jnp.float32)
    return (tail_blocks, tail_flags, blocks[:, :2], head_flags)


def join_left(nearer, farther, pick):
    return jnp.stack([jnp.where(pick, nearer[:, 0], farther[:, 1]), nearer[:, 1]], axis=1)


def join_right(nearer, farther, pick):
    return jnp.stack([nearer[:, 0], jnp.where(pick, nearer[:, 1], farther[:, 0])], axis=1)


def extend(own_blocks, left_pair, right_pair, live_count):
    padded = jnp.concatenate([left_pair, own_blocks, jnp.zeros_like(left_pair)], axis=1)
    return lax.dynamic_update_slice_in_dim(padded, right_pair, live_count + 2, axis=1)


def shifted(block, axes, distance):
    devices = range(lax.axis_size(axes))
    route = [(i - distance, i) for i in devices if i - distance in devices]
    return lax.ppermute(block, axes, route)


def iterate_with_reductions(axes, wing_jitter, live_blocks, smoothing, displacement, fluid_jitter):
    block_count = wing_jitter.shape[1] // BLK
    fluid_count = fluid_jitter.shape[1] // BLK
    live_count = live_blocks[0]
    factors = jnp.array(stretch_factors, jnp.float32)[:, None, None]
    own_points = wing_jitter.reshape(3, block_count, BLK) * factors
    own_flags = (jnp.arange(block_count, dtype=jnp.int32) < live_count).astype(jnp.float32)
    ends_of = {}
    neighbour_counts = {}
    for offset in (1, 2, -1, -2):
        points, counts = shifted((own_points, live_blocks), axes, offset)
        tail_blocks, tail_flags, head_blocks, head_flags = block_ends(points, counts[0])
        neighbour_counts[offset] = counts[0]
        ends_of[offset] = (tail_blocks, tail_flags) if offset > 0 else (head_blocks, head_flags)
    left_pick = ends_of[1][1][0] > 0
    right_pick = ends_of[-1][1][1] > 0
    left_points = join_left(ends_of[1][0], ends_of[2][0], left_pick)
    right_points = join_right(ends_of[-1][0], ends_of[-2][0], right_pick)
    left_flags = join_left(ends_of[1][1][None, :, None], ends_of[2][1][None, :, None], left_pick)
    right_flags = join_right(
        ends_of[-1][1][None, :, None], ends_of[-2][1][None, :, None], right_pick
    )
    ext_points = extend(own_points, left_points, right_points, live_count)
    ext_flags = extend(own_flags[None, :, None], left_flags, right_flags, live_count)
    ext_along = jnp.arange(block_count + 4, dtype=jnp.float32) - 2.0
    ext_points = ext_points.at[0].add(ext_along[:, None]).reshape(3, -1)
    col_flags = jnp.broadcast_to(ext_flags[0], (block_count + 4, BLK)).reshape(-1)
    row_points = (
        own_points.at[0].add(jnp.arange(block_count, dtype=jnp.float32)[:, None]).reshape(3, -1)
    )
    row_mask = jnp.repeat(own_flags, BLK)
    diagonal = 1.0 + smoothing

    def value_context(blocks):
        pieces = {}
        for offset in (1, 2, -1, -2):
            moved = shifted(blocks, axes, offset)
            tail_part, _, head_part, _ = block_ends(moved, neighbour_counts[offset])
            pieces[offset] = tail_part if offset > 0 else head_part
        left_values = join_left(pieces[1], pieces[2], left_pick)
        right_values = join_right(pieces[-1], pieces[-2], right_pick)
        return extend(blocks, left_values, right_values, live_count).reshape(3, -1)

    def apply(vector):
        ext_values = value_context(vector.reshape(3, block_count, BLK))

        def row_group(group):
            first_row = group * (2 * BLK)
            points = lax.dynamic_slice_in_dim(row_points, first_row, 2 * BLK, 1)
            col_points = lax.dynamic_slice_in_dim(ext_points, first_row, 6 * BLK, 1)
            flags = lax.dynamic_slice_in_dim(col_flags, first_row, 6 * BLK, 0)
            kernel = wendland(points, col_points) * flags[None, :]
            col_values = lax.dynamic_slice_in_dim(ext_values, first_row, 6 * BLK, 1)
            return jnp.einsum("cj,ij->ci", col_values, kernel, precision=lax.Precision.HIGHEST)

        result = lax.map(row_group, jnp.arange(block_count // 2, dtype=jnp.int32))
        result = result.transpose(1, 0, 2).reshape(3, -1)
        return result * row_mask + smoothing * vector

    def total(left, right):
        return lax.psum(jnp.sum(left * right, axis=1), axes)

    rhs = displacement * row_mask
    coefs = jnp.zeros_like(rhs)
    residual = rhs
    direction = precond = residual / diagonal
    norm_now = total(residual, precond)
    for iteration in range(ITERS):
        image = apply(direction)
        step_size = norm_now / total(direction, image)
        coefs = coefs + step_size[:, None] * direction
        residual = residual - step_size[:, None] * image
        if iteration + 1 < ITERS:
            precond = residual / diagonal
            norm_next = total(residual, precond)
            direction = precond + (norm_next / norm_now)[:, None] * direction
            norm_now = norm_next
    anchors = jnp.arange(fluid_count, dtype=jnp.int32) * live_count // fluid_count
    fluid_points = fluid_jitter.reshape(3, fluid_count, BLK) * factors
    fluid_points = fluid_points.at[0].add(anchors.astype(jnp.float32)[:, None])
    coef_ext = value_context(coefs.reshape(3, block_count, BLK))

    def fluid_block(points_and_anchor):
        points, anchor = points_and_anchor
        start_col = anchor * BLK
        col_points = lax.dynamic_slice_in_dim(ext_points, start_col, 5 * BLK, 1)
        flags = lax.dynamic_slice_in_dim(col_flags, start_col, 5 * BLK, 0)
        kernel = wendland(points, col_points) * flags[None, :]
        col_values = lax.dynamic_slice_in_dim(coef_ext, start_col, 5 * BLK, 1)
        return jnp.einsum("cj,ij->ci", col_values, kernel, precision=lax.Precision.HIGHEST)

    fluid_values = lax.map(fluid_block, (fluid_points.transpose(1, 0, 2), anchors))
    fluid_values = fluid_values.transpose(1, 0, 2).reshape(3, -1)
    return (coefs, residual, fluid_values)


def add_over_all(values, axes, partners):
    count = lax.axis_size(axes)
    for bits in partners:
        values = values + lax.ppermute(values, axes, [(i, i ^ bits) for i in range(count)])
    return values


def along_chips(values, axes, chips):
    count = lax.axis_size(axes)
    route = [(i, i + 2 * chips * (1 - 2 * (i % 2))) for i in range(count)]
    return lax.ppermute(values, axes, [(i, j) for i, j in route if 0 <= j < count])


def per_device(axes, partners, wing_jitter, live_blocks, smoothing, displacement, fluid_jitter):
    block_count = wing_jitter.shape[1] // BLK
    fluid_count = fluid_jitter.shape[1] // BLK
    width = block_count + 2 * HALO
    smoothing_row = smoothing.reshape(1, -1)
    in_smem = pl.BlockSpec(memory_space=pltpu.SMEM)
    in_vmem = pl.BlockSpec(memory_space=pltpu.VMEM)

    def floats(*shape):
        return jax.ShapeDtypeStruct(shape, jnp.float32)

    ends = pl.pallas_call(
        pack_kernel,
        out_shape=floats(2, HALO, 8, BLK),
        in_specs=[in_smem] + [in_vmem] * 3,
        out_specs=in_vmem,
    )(live_blocks, wing_jitter, smoothing_row, displacement)

    def join(near, far, end=False):
        return pl.pallas_call(
            functools.partial(join_kernel, axes, end),
            out_shape=floats(HALO, 8, BLK),
            in_specs=[in_vmem] * 2,
            out_specs=in_vmem,
            scratch_shapes=[pltpu.VMEM((3 * HALO, 8, BLK), jnp.float32)],
        )(near, far)

    cores = [(i, i ^ 1) for i in range(lax.axis_size(axes))]
    partner = lax.ppermute(ends, axes, cores)
    chip = join(partner, ends, end=True)
    next_chip = along_chips(chip, axes, 1)
    beyond = along_chips(join(chip, next_chip), axes, 2)
    mine = join(next_chip, beyond)
    other = lax.ppermute(mine, axes, cores)

    basis = floats(width, 8, BLK)
    vectors = pltpu.VMEM((width, 8, BLK), jnp.float32)
    pairs = pltpu.VMEM((width, 16, BLK), jnp.bfloat16)
    w1, w2, w3, moments, fluid_basis = pl.pallas_call(
        functools.partial(chain_kernel, axes, block_count, fluid_count),
        out_shape=(basis, basis, basis, floats(8, BLK), floats(fluid_count, 3, 8, BLK)),
        in_specs=[in_smem] + [in_vmem] * 7,
        out_specs=(in_vmem,) * 5,
        scratch_shapes=[
            pltpu.VMEM((2 * BASE + block_count, 8, BLK), jnp.float32),
            pltpu.VMEM((width, BLK, PIECES), jnp.bfloat16),
            *[vectors] * 7,
            *[pairs] * 3,
            pltpu.VMEM((block_count + 2 * NEAR, 5 * BLK, 2 * BLK), jnp.bfloat16),
            pltpu.VMEM((5 * BLK, 2 * BLK), jnp.bfloat16),
        ],
        compiler_params=pltpu.CompilerParams(vmem_limit_bytes=48 * 2**20),
    )(live_blocks, wing_jitter, smoothing_row, displacement, fluid_jitter, partner, mine, other)
    moments = add_over_all(moments, axes, partners)
    coefs, residual, fluid_values, good = pl.pallas_call(
        functools.partial(finish_kernel, block_count, fluid_count),
        out_shape=(
            floats(3, block_count * BLK),
            floats(3, block_count * BLK),
            floats(3, fluid_count * BLK),
            jax.ShapeDtypeStruct((1,), jnp.int32),
        ),
        in_specs=[in_smem] + [in_vmem] * 7,
        out_specs=(in_vmem, in_vmem, in_vmem, in_smem),
    )(live_blocks, moments, smoothing_row, displacement, w1, w2, w3, fluid_basis)
    return lax.cond(
        good[0] == 1,
        lambda: (coefs, residual, fluid_values),
        lambda: iterate_with_reductions(
            axes, wing_jitter, live_blocks, smoothing, displacement, fluid_jitter
        ),
    )


def solution(mesh):
    placed = (P(None, "dom"), P("dom"), P("dom"), P(None, "dom"), P(None, "dom"))
    partners = (1, 2, 6, 8, 24, 32, 64, 192)
    return jax.shard_map(
        functools.partial(per_device, "dom", partners),
        mesh=mesh,
        in_specs=placed,
        out_specs=(P(None, "dom"),) * 3,
        check_vma=False,
    )
```

time: 660 us -> 129 us (0.20)
  the two profiles are of different devices: /device:TPU:1 before, /device:TPU:64 now
where the time goes in v1:
time: 129 us; the launch traced here: 128 us
  Pallas kernels  61.2 us (47%)
  waiting for transfers between devices  43.6 us (34%)
  starting transfers between devices  14.5 us (11%)
  local copies, waits for them, and re-layouts  6.16 us (5%)
  between operations  2.03 us (2%)
    pallas_call x1, Pallas kernels, per_device(): pl.pallas_call(functools.partial(chain_kernel, axes, block_count, fluid_c...  52.4 us
    ppermute x8, waiting for transfers between devices, add_over_all(): lax.ppermute(values, axes, [(i, i ^ bits) for i in range(count)])  25.6 us
    ppermute x2, waiting for transfers between devices, along_chips(): lax.ppermute(values, axes, [(i, j) for i, j in route if 0 <= j < count])  15.2 us
    ppermute x8, starting transfers between devices, add_over_all(): lax.ppermute(values, axes, [(i, i ^ bits) for i in range(count)])  9 us
    unnamed x28, local copies, waits for them, and re-layouts  6.16 us
    ppermute x2, starting transfers between devices, along_chips(): lax.ppermute(values, axes, [(i, j) for i, j in route if 0 <= j < count])  5.51 us
    pallas_call x3, Pallas kernels, join(): pl.pallas_call(functools.partial(join_kernel, axes, end), out_shape=float...  4.54 us
    pallas_call x1, Pallas kernels, per_device(): pl.pallas_call(functools.partial(finish_kernel, block_count, fluid_count)...  2.59 us
  transfers between devices with their start and end apart: 12, of which 12 were waited for; matrix products, arithmetic and copies ran while one was open for 0% of the time, Pallas kernels for 0%

profile of v1, /device:TPU:64, one launch (start us, length us, event | category | flops | bytes accessed | tf_op | source)
XLA Modules:
  0.0 128.4 jit_solution(9857677031034664721)
XLA Ops:
  1.3 1.7 %shard_map.92.far_ref = f32[2,6,8,128]{3,2,1,0:T(8,128)} custom-call(s32[1]{0:T(128)S(6)} %copy.92.live_ref, f32[3,8192]{1,0:T(4,128)} %jitter_ref.3, f32[1,8192]{1,0:T(1,128)} %bitcast.165, f32[3,8192]{1,0:T(4,128)} %displacement_ref.5), custom_call_target="tpu_custom_call" | custom-call | tf_op jit(solution)/shard_map/pallas_call | solution.py:472
  3.0 1.4 %collective-permute-done.24.near_ref.partner_ref = f32[2,6,8,128]{3,2,1,0:T(8,128)S(1)} collective-permute-done((f32[2,6,8,128]{3,2,1,0:T(8,128)}, f32[2,6,8,128]{3,2,1,0:T(8,128)S(1)}, u32[]{:S(2)}, u32[]{:S(2)}) %collective-permute-start.24) | collective-permute-done | bytes 49184 | tf_op jit(solution)/shard_map/ppermute | solution.py:489
  4.4 0.6 copy-done.4
  5.0 1.6 %shard_map.93.near_ref = f32[6,8,128]{2,1,0:T(8,128)} custom-call(f32[2,6,8,128]{3,2,1,0:T(8,128)} %copy-done.4, f32[2,6,8,128]{3,2,1,0:T(8,128)} %shard_map.92.far_ref), custom_call_target="tpu_custom_call" | custom-call | tf_op jit(solution)/shard_map/pallas_call | solution.py:480
  6.6 3.5 %collective-permute-start.25 = (f32[6,8,128]{2,1,0:T(8,128)}, f32[6,8,128]{2,1,0:T(8,128)S(1)}, u32[]{:S(2)}, u32[]{:S(2)}) collective-permute-start(f32[6,8,128]{2,1,0:T(8,128)} %shard_map.93.near_ref), channel_id=1, source_target_pairs={{0,2},{2,4},{3,1},{4,6},{5,3},{6,8},{7,5},{8,10},{9,7},{10,12},{11... | collective-permute-start | bytes 73736 | tf_op jit(solution)/shard_map/ppermute | solution.py:458
  10.1 6.7 %collective-permute-done.25.far_ref.near_ref = f32[6,8,128]{2,1,0:T(8,128)S(1)} collective-permute-done((f32[6,8,128]{2,1,0:T(8,128)}, f32[6,8,128]{2,1,0:T(8,128)S(1)}, u32[]{:S(2)}, u32[]{:S(2)}) %collective-permute-start.25) | collective-permute-done | bytes 24608 | tf_op jit(solution)/shard_map/ppermute | solution.py:458
  16.7 0.6 copy-done.12
  17.3 1.5 %shard_map.94 = f32[6,8,128]{2,1,0:T(8,128)} custom-call(f32[6,8,128]{2,1,0:T(8,128)} %shard_map.93.near_ref, f32[6,8,128]{2,1,0:T(8,128)} %copy-done.12), custom_call_target="tpu_custom_call" | custom-call | tf_op jit(solution)/shard_map/pallas_call | solution.py:480
  18.8 2.0 %collective-permute-start.26 = (f32[6,8,128]{2,1,0:T(8,128)}, f32[6,8,128]{2,1,0:T(8,128)S(1)}, u32[]{:S(2)}, u32[]{:S(2)}) collective-permute-start(f32[6,8,128]{2,1,0:T(8,128)} %shard_map.94), channel_id=1, source_target_pairs={{0,4},{2,6},{4,8},{5,1},{6,10},{7,3},{8,12},{9,5},{10,14},{11,7},{... | collective-permute-start | bytes 73736 | tf_op jit(solution)/shard_map/ppermute | solution.py:458
  20.9 8.5 %collective-permute-done.26.far_ref = f32[6,8,128]{2,1,0:T(8,128)S(1)} collective-permute-done((f32[6,8,128]{2,1,0:T(8,128)}, f32[6,8,128]{2,1,0:T(8,128)S(1)}, u32[]{:S(2)}, u32[]{:S(2)}) %collective-permute-start.26) | collective-permute-done | bytes 24608 | tf_op jit(solution)/shard_map/ppermute | solution.py:458
  29.4 0.6 copy-done.13
  30.0 1.5 %shard_map.95.mine_ref = f32[6,8,128]{2,1,0:T(8,128)} custom-call(f32[6,8,128]{2,1,0:T(8,128)} %copy-done.12, f32[6,8,128]{2,1,0:T(8,128)} %copy-done.13), custom_call_target="tpu_custom_call" | custom-call | tf_op jit(solution)/shard_map/pallas_call | solution.py:480
  31.5 1.4 %collective-permute-done.27.other_ref = f32[6,8,128]{2,1,0:T(8,128)S(1)} collective-permute-done((f32[6,8,128]{2,1,0:T(8,128)}, f32[6,8,128]{2,1,0:T(8,128)S(1)}, u32[]{:S(2)}, u32[]{:S(2)}) %collective-permute-start.27) | collective-permute-done | bytes 24608 | tf_op jit(solution)/shard_map/ppermute | solution.py:494
  32.9 0.7 copy-done.6
  33.7 52.4 %shard_map.96 = (f32[76,8,128]{2,1,0:T(8,128)S(1)}, f32[76,8,128]{2,1,0:T(8,128)S(1)}, f32[76,8,128]{2,1,0:T(8,128)S(1)}, f32[8,128]{1,0:T(8,128)S(1)}, f32[24,3,8,128]{3,2,1,0:T(8,128)S(1)}) custom-call(s32[1]{0:T(128)S(6)} %copy.92.live_ref, f32[3,8192]{1,0:T(4,128)S(1)} %copy-done.9, f32[1,8192]{1,0:T(1,128)S(1)} %bitcast.166, f32[3,8192]{1,0:T(4,128)S(1)} %copy-done.7, ...), custom_call_target="tpu_custom_call" | custom-call | tf_op jit(solution)/shard_map/pallas_call | solution.py:499
  86.1 0.7 copy-done
  86.8 0.7 copy-done.1
  87.6 0.7 copy-done.2
  88.3 0.7 copy-done.3
  89.2 1.0 collective-permute-done.28
  90.2 3.6 %collective-permute-done.29 = f32[8,128]{1,0:T(8,128)S(1)} collective-permute-done((f32[8,128]{1,0:T(8,128)S(1)}, f32[8,128]{1,0:T(8,128)S(1)}, u32[]{:S(2)}, u32[]{:S(2)}) %collective-permute-start.29) | collective-permute-done | bytes 4128 | tf_op jit(solution)/shard_map/ppermute | solution.py:451
  93.8 4.8 %collective-permute-done.30 = f32[8,128]{1,0:T(8,128)S(1)} collective-permute-done((f32[8,128]{1,0:T(8,128)S(1)}, f32[8,128]{1,0:T(8,128)S(1)}, u32[]{:S(2)}, u32[]{:S(2)}) %collective-permute-start.30) | collective-permute-done | bytes 4128 | tf_op jit(solution)/shard_map/ppermute | solution.py:451
  98.6 3.6 %collective-permute-done.31 = f32[8,128]{1,0:T(8,128)S(1)} collective-permute-done((f32[8,128]{1,0:T(8,128)S(1)}, f32[8,128]{1,0:T(8,128)S(1)}, u32[]{:S(2)}, u32[]{:S(2)}) %collective-permute-start.31) | collective-permute-done | bytes 4128 | tf_op jit(solution)/shard_map/ppermute | solution.py:451
  102.3 4.8 %collective-permute-done.32 = f32[8,128]{1,0:T(8,128)S(1)} collective-permute-done((f32[8,128]{1,0:T(8,128)S(1)}, f32[8,128]{1,0:T(8,128)S(1)}, u32[]{:S(2)}, u32[]{:S(2)}) %collective-permute-start.32) | collective-permute-done | bytes 4128 | tf_op jit(solution)/shard_map/ppermute | solution.py:451
  107.1 1.9 %collective-permute-start.33 = (f32[8,128]{1,0:T(8,128)S(1)}, f32[8,128]{1,0:T(8,128)S(1)}, u32[]{:S(2)}, u32[]{:S(2)}) collective-permute-start(f32[8,128]{1,0:T(8,128)S(1)} %add.325), channel_id=1, source_target_pairs={{0,32},{1,33},{2,34},{3,35},{4,36},{5,37},{6,38},{7,39},{8,40},{9,... | collective-permute-start | bytes 12296 | tf_op jit(solution)/shard_map/ppermute | solution.py:451
  109.0 1.7 %collective-permute-done.33 = f32[8,128]{1,0:T(8,128)S(1)} collective-permute-done((f32[8,128]{1,0:T(8,128)S(1)}, f32[8,128]{1,0:T(8,128)S(1)}, u32[]{:S(2)}, u32[]{:S(2)}) %collective-permute-start.33) | collective-permute-done | bytes 4128 | tf_op jit(solution)/shard_map/ppermute | solution.py:451
  110.7 4.5 %collective-permute-done.34 = f32[8,128]{1,0:T(8,128)S(1)} collective-permute-done((f32[8,128]{1,0:T(8,128)S(1)}, f32[8,128]{1,0:T(8,128)S(1)}, u32[]{:S(2)}, u32[]{:S(2)}) %collective-permute-start.34) | collective-permute-done | bytes 4128 | tf_op jit(solution)/shard_map/ppermute | solution.py:451
  115.2 6.9 %collective-permute-start.35 = (f32[8,128]{1,0:T(8,128)S(1)}, f32[8,128]{1,0:T(8,128)S(1)}, u32[]{:S(2)}, u32[]{:S(2)}) collective-permute-start(f32[8,128]{1,0:T(8,128)S(1)} %add.327), channel_id=1, source_target_pairs={{0,192},{1,193},{2,194},{3,195},{4,196},{5,197},{6,198},{7,199},{8... | collective-permute-start | bytes 12296 | tf_op jit(solution)/shard_map/ppermute | solution.py:451
  122.1 1.6 %collective-permute-done.35 = f32[8,128]{1,0:T(8,128)S(1)} collective-permute-done((f32[8,128]{1,0:T(8,128)S(1)}, f32[8,128]{1,0:T(8,128)S(1)}, u32[]{:S(2)}, u32[]{:S(2)}) %collective-permute-start.35) | collective-permute-done | bytes 4128 | tf_op jit(solution)/shard_map/ppermute | solution.py:451
  123.7 0.6 add.328.moments_ref
  124.3 2.6 %shard_map.97 = (f32[3,8192]{1,0:T(4,128)}, f32[3,8192]{1,0:T(4,128)S(1)}, f32[3,3072]{1,0:T(4,128)}, s32[1]{0:T(128)}) custom-call(s32[1]{0:T(128)S(6)} %copy.92.live_ref, f32[8,128]{1,0:T(8,128)} %add.328.moments_ref, f32[1,8192]{1,0:T(1,128)S(1)} %bitcast.167, f32[3,8192]{1,0:T(4,128)S(1)} %copy-done.7, f32[76,8,128]{2,1,0:T(8,128)} %copy-done, ...), custom_call_target="tpu_custom_call" | custom-call | tf_op jit(solution)/shard_map/pallas_call | solution.py:515
  127.8 0.6 copy-done.15
  (35 shorter events, 0.5 us)
Async XLA Ops:
  1.3 31.6 %copy-start.9 = (f32[3,8192]{1,0:T(4,128)S(1)}, f32[3,8192]{1,0:T(4,128)}, u32[]{:S(2)}) copy-start(f32[3,8192]{1,0:T(4,128)} %jitter_ref.3) | copy-start | bytes 294916
  3.0 29.9 %copy-start.7 = (f32[3,8192]{1,0:T(4,128)S(1)}, f32[3,8192]{1,0:T(4,128)}, u32[]{:S(2)}) copy-start(f32[3,8192]{1,0:T(4,128)} %displacement_ref.5) | copy-start | bytes 294916
  3.0 1.4 %collective-permute-start.24 = (f32[2,6,8,128]{3,2,1,0:T(8,128)}, f32[2,6,8,128]{3,2,1,0:T(8,128)S(1)}, u32[]{:S(2)}, u32[]{:S(2)}) collective-permute-start(f32[2,6,8,128]{3,2,1,0:T(8,128)} %shard_map.92.far_ref), channel_id=1, source_target_pairs={{0,1},{1,0},{2,3},{3,2},{4,5},{5,4},{6,7},{7,6},{8,9},{9,8},{10,11... | collective-permute-start | bytes 147464 | tf_op jit(solution)/shard_map/ppermute | solution.py:489
  4.4 0.6 copy-start.4
  6.6 10.1 %collective-permute-start.25 = (f32[6,8,128]{2,1,0:T(8,128)}, f32[6,8,128]{2,1,0:T(8,128)S(1)}, u32[]{:S(2)}, u32[]{:S(2)}) collective-permute-start(f32[6,8,128]{2,1,0:T(8,128)} %shard_map.93.near_ref), channel_id=1, source_target_pairs={{0,2},{2,4},{3,1},{4,6},{5,3},{6,8},{7,5},{8,10},{9,7},{10,12},{11... | collective-permute-start | bytes 73736 | tf_op jit(solution)/shard_map/ppermute | solution.py:458
  16.7 0.6 copy-start.12
  17.3 15.6 %copy-start.8 = (f32[8192]{0:T(1024)S(1)}, f32[8192]{0:T(1024)}, u32[]{:S(2)}) copy-start(f32[8192]{0:T(1024)} %param.24) | copy-start | bytes 98308
  17.3 15.6 %copy-start.10 = (f32[3,3072]{1,0:T(4,128)S(1)}, f32[3,3072]{1,0:T(4,128)}, u32[]{:S(2)}) copy-start(f32[3,3072]{1,0:T(4,128)} %fluid_ref.1) | copy-start | bytes 110596
  18.8 14.1 %copy-start.5 = (f32[2,6,8,128]{3,2,1,0:T(8,128)S(1)}, f32[2,6,8,128]{3,2,1,0:T(8,128)}, u32[]{:S(2)}) copy-start(f32[2,6,8,128]{3,2,1,0:T(8,128)} %copy-done.4) | copy-start | bytes 147460
  18.8 10.6 %collective-permute-start.26 = (f32[6,8,128]{2,1,0:T(8,128)}, f32[6,8,128]{2,1,0:T(8,128)S(1)}, u32[]{:S(2)}, u32[]{:S(2)}) collective-permute-start(f32[6,8,128]{2,1,0:T(8,128)} %shard_map.94), channel_id=1, source_target_pairs={{0,4},{2,6},{4,8},{5,1},{6,10},{7,3},{8,12},{9,5},{10,14},{11,7},{... | collective-permute-start | bytes 73736 | tf_op jit(solution)/shard_map/ppermute | solution.py:458
  29.4 0.6 copy-start.13
  31.5 1.4 %collective-permute-start.27 = (f32[6,8,128]{2,1,0:T(8,128)}, f32[6,8,128]{2,1,0:T(8,128)S(1)}, u32[]{:S(2)}, u32[]{:S(2)}) collective-permute-start(f32[6,8,128]{2,1,0:T(8,128)} %shard_map.95.mine_ref), channel_id=1, source_target_pairs={{0,1},{1,0},{2,3},{3,2},{4,5},{5,4},{6,7},{7,6},{8,9},{9,8},{10,11... | collective-permute-start | bytes 73736 | tf_op jit(solution)/shard_map/ppermute | solution.py:494
  32.9 0.7 copy-start.6
  86.1 0.7 copy-start
  86.8 0.7 copy-start.1
  87.6 0.7 copy-start.2
  88.3 0.7 copy-start.3
  89.0 1.2 collective-permute-start.28
  90.2 3.6 %collective-permute-start.29 = (f32[8,128]{1,0:T(8,128)S(1)}, f32[8,128]{1,0:T(8,128)S(1)}, u32[]{:S(2)}, u32[]{:S(2)}) collective-permute-start(f32[8,128]{1,0:T(8,128)S(1)} %add.321), channel_id=1, source_target_pairs={{0,2},{1,3},{2,0},{3,1},{4,6},{5,7},{6,4},{7,5},{8,10},{9,11},{10,... | collective-permute-start | bytes 12296 | tf_op jit(solution)/shard_map/ppermute | solution.py:451
  93.8 4.8 %collective-permute-start.30 = (f32[8,128]{1,0:T(8,128)S(1)}, f32[8,128]{1,0:T(8,128)S(1)}, u32[]{:S(2)}, u32[]{:S(2)}) collective-permute-start(f32[8,128]{1,0:T(8,128)S(1)} %add.322), channel_id=1, source_target_pairs={{0,6},{1,7},{2,4},{3,5},{4,2},{5,3},{6,0},{7,1},{8,14},{9,15},{10,... | collective-permute-start | bytes 12296 | tf_op jit(solution)/shard_map/ppermute | solution.py:451
  98.6 3.6 %collective-permute-start.31 = (f32[8,128]{1,0:T(8,128)S(1)}, f32[8,128]{1,0:T(8,128)S(1)}, u32[]{:S(2)}, u32[]{:S(2)}) collective-permute-start(f32[8,128]{1,0:T(8,128)S(1)} %add.323), channel_id=1, source_target_pairs={{0,8},{1,9},{2,10},{3,11},{4,12},{5,13},{6,14},{7,15},{8,0},{9,1},... | collective-permute-start | bytes 12296 | tf_op jit(solution)/shard_map/ppermute | solution.py:451
  102.2 4.8 %collective-permute-start.32 = (f32[8,128]{1,0:T(8,128)S(1)}, f32[8,128]{1,0:T(8,128)S(1)}, u32[]{:S(2)}, u32[]{:S(2)}) collective-permute-start(f32[8,128]{1,0:T(8,128)S(1)} %add.324), channel_id=1, source_target_pairs={{0,24},{1,25},{2,26},{3,27},{4,28},{5,29},{6,30},{7,31},{8,16},{9,... | collective-permute-start | bytes 12296 | tf_op jit(solution)/shard_map/ppermute | solution.py:451
  107.1 3.6 %collective-permute-start.33 = (f32[8,128]{1,0:T(8,128)S(1)}, f32[8,128]{1,0:T(8,128)S(1)}, u32[]{:S(2)}, u32[]{:S(2)}) collective-permute-start(f32[8,128]{1,0:T(8,128)S(1)} %add.325), channel_id=1, source_target_pairs={{0,32},{1,33},{2,34},{3,35},{4,36},{5,37},{6,38},{7,39},{8,40},{9,... | collective-permute-start | bytes 12296 | tf_op jit(solution)/shard_map/ppermute | solution.py:451
  110.7 4.5 %collective-permute-start.34 = (f32[8,128]{1,0:T(8,128)S(1)}, f32[8,128]{1,0:T(8,128)S(1)}, u32[]{:S(2)}, u32[]{:S(2)}) collective-permute-start(f32[8,128]{1,0:T(8,128)S(1)} %add.326), channel_id=1, source_target_pairs={{0,64},{1,65},{2,66},{3,67},{4,68},{5,69},{6,70},{7,71},{8,72},{9,... | collective-permute-start | bytes 12296 | tf_op jit(solution)/shard_map/ppermute | solution.py:451
  115.2 8.5 %collective-permute-start.35 = (f32[8,128]{1,0:T(8,128)S(1)}, f32[8,128]{1,0:T(8,128)S(1)}, u32[]{:S(2)}, u32[]{:S(2)}) collective-permute-start(f32[8,128]{1,0:T(8,128)S(1)} %add.327), channel_id=1, source_target_pairs={{0,192},{1,193},{2,194},{3,195},{4,196},{5,197},{6,198},{7,199},{8... | collective-permute-start | bytes 12296 | tf_op jit(solution)/shard_map/ppermute | solution.py:451
  127.7 0.7 copy-start.15

commit v2 on v1

--- a/solution.py
+++ b/solution.py
@@ -13,6 +13,9 @@
 NEAR = 4
 PIECES = 48
 MAX_AMPLIFICATION = 50.0
+MOMENTS = 2 * ITERS + 1
+GROUP = 4
+APPLY_UNROLL = 8
 
 stretch_factors = (1.0, 6.0, 6.0)
 
@@ -112,15 +115,8 @@
     return upper[:, :BLK] + upper[:, BLK:]
 
 
-def chain_kernel(
-    axes, block_count, fluid_count,
-    live_ref, jitter_ref, smoothing_ref, displacement_ref, fluid_ref, partner_ref, mine_ref, other_ref,
-    w1_ref, w2_ref, w3_ref, moments_ref, fluid_basis_ref,
-    joined, source, base, slope, inverse, w0, z0, z1, z2, b0, b1, b2, matrix, fluid_matrix,
-):
-    live = live_ref[0]
-    width = block_count + 2 * HALO
-
+def join_chain(axes, live, jitter_ref, smoothing_ref, displacement_ref, partner_ref, mine_ref, other_ref, joined):
+    block_count = jitter_ref.shape[1] // BLK
     for extra in range(HALO):
         joined[BASE + block_count + extra] = jnp.zeros((8, BLK), jnp.float32)
 
@@ -142,15 +138,36 @@
     joined[pl.ds(BASE + live, HALO)] = partner_ref[1]
     joined[pl.ds(BASE + live + right_near, HALO)] = jnp.where(core == 0, other, mine)
 
+
+def parts_of(packed):
+    points = centred(packed)
+    norm = jnp.sum(points * points, axis=0, keepdims=True)
+    inverse = jnp.where(packed[3:4] > 0.0, 1.0 / (1.0 + packed[3:4]), 0.0)
+    rhs = jnp.concatenate([packed[4:7], jnp.zeros((5, BLK), jnp.float32)], axis=0)
+    return points, norm, jnp.broadcast_to(inverse, (8, BLK)), rhs
+
+
+def source_of(points, norm):
+    return jnp.transpose(source_rows(points, norm)).astype(jnp.bfloat16)
+
+
+def chain_kernel(
+    axes, block_count,
+    live_ref, jitter_ref, smoothing_ref, displacement_ref, partner_ref, mine_ref, other_ref,
+    basis_ref, moments_ref,
+    joined, source, base, slope, inverse, w0, z0, z1, z2, b0, b1, b2, matrix,
+):
+    w1_ref, w2_ref, w3_ref = (basis_ref.at[k] for k in range(3))
+    live = live_ref[0]
+    width = block_count + 2 * HALO
+    join_chain(
+        axes, live, jitter_ref, smoothing_ref, displacement_ref, partner_ref, mine_ref, other_ref, joined
+    )
+
     def prepare(block, carry):
-        packed = joined[BASE - HALO + block]
-        points = centred(packed)
-        norm = jnp.sum(points * points, axis=0, keepdims=True)
-        source[block] = jnp.transpose(source_rows(points, norm)).astype(jnp.bfloat16)
+        points, norm, scale, rhs = parts_of(joined[BASE - HALO + block])
+        source[block] = source_of(points, norm)
         base[block], slope[block] = target_parts(points, norm)
-        scale = jnp.where(packed[3:4] > 0.0, 1.0 / (1.0 + packed[3:4]), 0.0)
-        scale = jnp.broadcast_to(scale, (8, BLK))
-        rhs = jnp.concatenate([packed[4:7], jnp.zeros((5, BLK), jnp.float32)], axis=0)
         inverse[block] = scale
         w0[block] = rhs
         z0[block] = rhs * scale
@@ -159,23 +176,35 @@
 
     lax.fori_loop(0, width, prepare, 0, unroll=4)
 
-    def generate(row, carry):
-        for place in range(5):
-            columns = target_rows(base[row + 2], slope[row + 2], place - 2)
-            quarter = jnp.dot(source[row + place], columns, preferred_element_type=jnp.float32)
-            store_pair(matrix.at[row], wendland_of_quarter(quarter), place * BLK)
-        return carry
-
-    lax.fori_loop(0, block_count + 2 * NEAR, generate, 0)
+    def generate_two(row):
+        for place in range(6):
+            columns = []
+            if place < 5:
+                columns.append(target_rows(base[row + 2], slope[row + 2], place - 2))
+            if place > 0:
+                columns.append(target_rows(base[row + 3], slope[row + 3], place - 3))
+            quarter = jnp.dot(
+                source[row + place],
+                jnp.concatenate(columns, axis=1),
+                preferred_element_type=jnp.float32,
+            )
+            values = wendland_of_quarter(quarter)
+            if place < 5:
+                store_pair(matrix.at[row], values[:, :BLK], place * BLK)
+            if place > 0:
+                store_pair(matrix.at[row + 1], values[:, -BLK:], (place - 1) * BLK)
+
+    def apply_row(row, values, pairs, place_next):
+        near = jnp.concatenate([pairs[row + place] for place in range(5)], axis=1)
+        product = jnp.dot(near, matrix[row], preferred_element_type=jnp.float32)
+        place_next(row + 2, sum_pairs(product, 0) - values[row + 2])
 
     def apply(values, pairs, first, last, place_next):
         def one_row(row, carry):
-            near = jnp.concatenate([pairs[row + place] for place in range(5)], axis=1)
-            product = jnp.dot(near, matrix[row], preferred_element_type=jnp.float32)
-            place_next(row + 2, sum_pairs(product, 0) - values[row + 2])
+            apply_row(row, values, pairs, place_next)
             return carry
 
-        lax.fori_loop(first, last, one_row, 0, unroll=4)
+        lax.fori_loop(first, last, one_row, 0, unroll=APPLY_UNROLL)
 
     rows = block_count + 2 * NEAR
 
@@ -194,7 +223,22 @@
     def third_next(block, image):
         w3_ref[block] = image
 
-    apply(z0, b0, 0, rows, first_next)
+    def generate_group(group):
+        for row in range(0, GROUP, 2):
+            generate_two(group * GROUP + row)
+
+    def apply_group(group):
+        for row in range(GROUP):
+            apply_row(group * GROUP + row, z0, b0, first_next)
+
+    def apply_then_generate(group, carry):
+        apply_group(group - 1)
+        generate_group(group)
+        return carry
+
+    generate_group(0)
+    lax.fori_loop(1, rows // GROUP, apply_then_generate, 0)
+    apply_group(rows // GROUP - 1)
     apply(z1, b1, 2, rows - 2, second_next)
     apply(z2, b2, 4, rows - 4, third_next)
 
@@ -214,34 +258,69 @@
         return tuple(s + kept * (a * b) for s, (a, b) in zip(sums, pairs))
 
     zero = jnp.zeros((8, BLK), jnp.float32)
-    sums = lax.fori_loop(0, block_count, add_up, (zero,) * 7, unroll=4)
+    sums = lax.fori_loop(0, block_count, add_up, (zero,) * MOMENTS, unroll=4)
     lane = lax.broadcasted_iota(jnp.int32, (8, BLK), 1)
+    row = lax.broadcasted_iota(jnp.int32, (8, BLK), 0)
     moments = zero
-    for k in range(7):
-        moments = jnp.where(lane == k, jnp.sum(sums[k], axis=1, keepdims=True), moments)
-    moments_ref[...] = moments
-
-    def fluid_block(index, carry):
-        anchor = lax.div(index * live, jnp.int32(fluid_count))
+    for k in range(MOMENTS):
+        moments = jnp.where(lane == 8 * row + k, jnp.sum(sums[k], axis=1, keepdims=True), moments)
+    moments = jnp.sum(moments, axis=0, keepdims=True)
+    moments_ref[...] = jnp.broadcast_to(moments, moments_ref.shape)
+
+
+def fluid_kernel(
+    axes, fluid_count,
+    live_ref, jitter_ref, smoothing_ref, displacement_ref, fluid_ref, partner_ref, mine_ref, other_ref,
+    basis_ref,
+    fluid_basis_ref,
+    joined, source, b0, b1, b2, matrix,
+):
+    live = live_ref[0]
+    width = jitter_ref.shape[1] // BLK + 2 * HALO
+    join_chain(
+        axes, live, jitter_ref, smoothing_ref, displacement_ref, partner_ref, mine_ref, other_ref, joined
+    )
+
+    def prepare(block, carry):
+        points, norm, scale, rhs = parts_of(joined[BASE - HALO + block])
+        source[block] = source_of(points, norm)
+        b0[block] = vector_pair(rhs * scale)
+        b1[block] = vector_pair(basis_ref[0, block] * scale)
+        b2[block] = vector_pair(basis_ref[1, block] * scale)
+        return carry
+
+    lax.fori_loop(HALO - 2, width - HALO + 2, prepare, 0, unroll=4)
+
+    def anchor_of(index):
+        return lax.div(index * live, jnp.int32(fluid_count))
+
+    def generate_fluid(index, carry):
         lanes = pl.ds(pl.multiple_of(index * BLK, BLK), BLK)
         jitter = jnp.concatenate([fluid_ref[:, lanes], jnp.zeros((5, BLK), jnp.float32)], axis=0)
         points = centred(jitter)
         norm = jnp.sum(points * points, axis=0, keepdims=True)
         base_here, slope_here = target_parts(points, norm)
-        near = []
+        first = anchor_of(index) + (HALO - 2)
         for place in range(5):
-            block = anchor + (HALO - 2 + place)
             columns = target_rows(base_here, slope_here, place - 2)
-            quarter = jnp.dot(source[block], columns, preferred_element_type=jnp.float32)
-            store_pair(fluid_matrix, wendland_of_quarter(quarter), place * BLK)
-            near.append(jnp.concatenate([b0[block], b1[block], b2[block]], axis=0))
-        near = jnp.concatenate(near, axis=1)
-        product = jnp.dot(near, fluid_matrix[...], preferred_element_type=jnp.float32)
+            quarter = jnp.dot(source[first + place], columns, preferred_element_type=jnp.float32)
+            store_pair(matrix.at[index], wendland_of_quarter(quarter), place * BLK)
+        return carry
+
+    def apply_fluid(index, carry):
+        first = anchor_of(index) + (HALO - 2)
+        near = [
+            jnp.concatenate([ref[first + place] for place in range(5)], axis=1)
+            for ref in (b0, b1, b2)
+        ]
+        near = jnp.concatenate(near, axis=0)
+        product = jnp.dot(near, matrix[index], preferred_element_type=jnp.float32)
         for k in range(3):
             fluid_basis_ref[index, k] = sum_pairs(product, 16 * k)
         return carry
 
-    lax.fori_loop(0, fluid_count, fluid_block, 0)
+    lax.fori_loop(0, fluid_count, generate_fluid, 0, unroll=4)
+    lax.fori_loop(0, fluid_count, apply_fluid, 0, unroll=4)
 
 
 def step_coefficients(moments):
@@ -281,11 +360,17 @@
 
 def finish_kernel(
     block_count, fluid_count, live_ref, moments_ref, smoothing_ref, displacement_ref,
-    w1_ref, w2_ref, w3_ref, fluid_basis_ref, coefs_ref, residual_ref, fluid_ref, good_ref,
+    basis_ref, fluid_basis_ref, coefs_ref, residual_ref, fluid_ref, good_ref,
 ):
     live = live_ref[0]
-    moments = moments_ref[...]
-    solved, left, good = step_coefficients([moments[:, k : k + 1] for k in range(7)])
+    row = lax.broadcasted_iota(jnp.int32, (8, BLK), 0)
+    lane = lax.broadcasted_iota(jnp.int32, (8, BLK), 1)
+    summed = jnp.broadcast_to(jnp.sum(moments_ref[...], axis=0, keepdims=True), (8, BLK))
+    moments = [
+        jnp.sum(jnp.where(lane == 8 * row + k, summed, 0.0), axis=1, keepdims=True)
+        for k in range(MOMENTS)
+    ]
+    solved, left, good = step_coefficients(moments)
     row = lax.broadcasted_iota(jnp.int32, (8, 1), 0)
     good_ref[0] = jnp.min(jnp.where(good | (row > 2), 1.0, 0.0)).astype(jnp.int32)
     solved = [jnp.broadcast_to(v, (8, BLK))[0:3] for v in solved]
@@ -294,7 +379,7 @@
     def one_block(own, carry):
         lanes = pl.ds(pl.multiple_of(own * BLK, BLK), BLK)
         block = own + HALO
-        parts = [displacement_ref[:, lanes]] + [r[block][0:3] for r in (w1_ref, w2_ref, w3_ref)]
+        parts = [displacement_ref[:, lanes]] + [basis_ref[k, block][0:3] for k in range(3)]
         scaled = sum(a * b for a, b in zip(solved, parts)) / (1.0 + smoothing_ref[:, lanes])
         remaining = sum(a * b for a, b in zip(left, parts))
         is_live = own < live
@@ -445,20 +530,13 @@
     return (coefs, residual, fluid_values)
 
 
-def add_over_all(values, axes, partners):
-    count = lax.axis_size(axes)
-    for bits in partners:
-        values = values + lax.ppermute(values, axes, [(i, i ^ bits) for i in range(count)])
-    return values
-
-
 def along_chips(values, axes, chips):
     count = lax.axis_size(axes)
     route = [(i, i + 2 * chips * (1 - 2 * (i % 2))) for i in range(count)]
     return lax.ppermute(values, axes, [(i, j) for i, j in route if 0 <= j < count])
 
 
-def per_device(axes, partners, wing_jitter, live_blocks, smoothing, displacement, fluid_jitter):
+def per_device(axes, wing_jitter, live_blocks, smoothing, displacement, fluid_jitter):
     block_count = wing_jitter.shape[1] // BLK
     fluid_count = fluid_jitter.shape[1] // BLK
     width = block_count + 2 * HALO
@@ -469,11 +547,13 @@
     def floats(*shape):
         return jax.ShapeDtypeStruct(shape, jnp.float32)
 
+    small = pltpu.CompilerParams(vmem_limit_bytes=8 * 2**20)
     ends = pl.pallas_call(
         pack_kernel,
         out_shape=floats(2, HALO, 8, BLK),
         in_specs=[in_smem] + [in_vmem] * 3,
         out_specs=in_vmem,
+        compiler_params=small,
     )(live_blocks, wing_jitter, smoothing_row, displacement)
 
     def join(near, far, end=False):
@@ -483,6 +563,7 @@
             in_specs=[in_vmem] * 2,
             out_specs=in_vmem,
             scratch_shapes=[pltpu.VMEM((3 * HALO, 8, BLK), jnp.float32)],
+            compiler_params=small,
         )(near, far)
 
     cores = [(i, i ^ 1) for i in range(lax.axis_size(axes))]
@@ -493,25 +574,39 @@
     mine = join(next_chip, beyond)
     other = lax.ppermute(mine, axes, cores)
 
-    basis = floats(width, 8, BLK)
     vectors = pltpu.VMEM((width, 8, BLK), jnp.float32)
     pairs = pltpu.VMEM((width, 16, BLK), jnp.bfloat16)
-    w1, w2, w3, moments, fluid_basis = pl.pallas_call(
-        functools.partial(chain_kernel, axes, block_count, fluid_count),
-        out_shape=(basis, basis, basis, floats(8, BLK), floats(fluid_count, 3, 8, BLK)),
-        in_specs=[in_smem] + [in_vmem] * 7,
-        out_specs=(in_vmem,) * 5,
+    joined = pltpu.VMEM((2 * BASE + block_count, 8, BLK), jnp.float32)
+    source = pltpu.VMEM((width, BLK, PIECES), jnp.bfloat16)
+    basis, moments = pl.pallas_call(
+        functools.partial(chain_kernel, axes, block_count),
+        out_shape=(floats(3, width, 8, BLK), floats(lax.axis_size(axes), BLK)),
+        in_specs=[in_smem] + [in_vmem] * 6,
+        out_specs=(in_vmem,) * 2,
         scratch_shapes=[
-            pltpu.VMEM((2 * BASE + block_count, 8, BLK), jnp.float32),
-            pltpu.VMEM((width, BLK, PIECES), jnp.bfloat16),
+            joined,
+            source,
             *[vectors] * 7,
             *[pairs] * 3,
             pltpu.VMEM((block_count + 2 * NEAR, 5 * BLK, 2 * BLK), jnp.bfloat16),
-            pltpu.VMEM((5 * BLK, 2 * BLK), jnp.bfloat16),
         ],
         compiler_params=pltpu.CompilerParams(vmem_limit_bytes=48 * 2**20),
-    )(live_blocks, wing_jitter, smoothing_row, displacement, fluid_jitter, partner, mine, other)
-    moments = add_over_all(moments, axes, partners)
+    )(live_blocks, wing_jitter, smoothing_row, displacement, partner, mine, other)
+    moments = lax.all_to_all(moments, axes, 0, 0, tiled=True)
+    fluid_basis = pl.pallas_call(
+        functools.partial(fluid_kernel, axes, fluid_count),
+        out_shape=floats(fluid_count, 3, 8, BLK),
+        in_specs=[in_smem] + [in_vmem] * 8,
+        out_specs=in_vmem,
+        scratch_shapes=[
+            joined,
+            source,
+            *[pairs] * 3,
+            pltpu.VMEM((fluid_count, 5 * BLK, 2 * BLK), jnp.bfloat16),
+        ],
+        compiler_params=pltpu.CompilerParams(vmem_limit_bytes=24 * 2**20),
+        cost_estimate=pl.CostEstimate(flops=6 * 10**9, bytes_accessed=10**7, transcendentals=2 * 10**6),
+    )(live_blocks, wing_jitter, smoothing_row, displacement, fluid_jitter, partner, mine, other, basis)
     coefs, residual, fluid_values, good = pl.pallas_call(
         functools.partial(finish_kernel, block_count, fluid_count),
         out_shape=(
@@ -520,9 +615,10 @@
             floats(3, fluid_count * BLK),
             jax.ShapeDtypeStruct((1,), jnp.int32),
         ),
-        in_specs=[in_smem] + [in_vmem] * 7,
+        in_specs=[in_smem] + [in_vmem] * 5,
         out_specs=(in_vmem, in_vmem, in_vmem, in_smem),
-    )(live_blocks, moments, smoothing_row, displacement, w1, w2, w3, fluid_basis)
+        compiler_params=small,
+    )(live_blocks, moments, smoothing_row, displacement, basis, fluid_basis)
     return lax.cond(
         good[0] == 1,
         lambda: (coefs, residual, fluid_values),
@@ -534,9 +630,8 @@
 
 def solution(mesh):
     placed = (P(None, "dom"), P("dom"), P("dom"), P(None, "dom"), P(None, "dom"))
-    partners = (1, 2, 6, 8, 24, 32, 64, 192)
     return jax.shard_map(
-        functools.partial(per_device, "dom", partners),
+        functools.partial(per_device, "dom"),
         mesh=mesh,
         in_specs=placed,
         out_specs=(P(None, "dom"),) * 3,

time: 129 us -> 84.9 us (0.66)
  the two profiles are of different devices: /device:TPU:64 before, /device:TPU:1 now
where the time goes in v2:
time: 84.9 us; the launch traced here: 84.6 us
  Pallas kernels  42.8 us (50%)
  starting transfers between devices  26 us (31%)
  waiting for transfers between devices  12.9 us (15%)
  between operations  2.05 us (2%)
    pallas_call x1, Pallas kernels, per_device(): pl.pallas_call(functools.partial(chain_kernel, axes, block_count), out_sh...  30.2 us
    all_to_all x1, starting transfers between devices, per_device(): moments = lax.all_to_all(moments, axes, 0, 0, tiled=True)  19.7 us
    pallas_call x1, Pallas kernels, per_device(): pl.pallas_call(functools.partial(fluid_kernel, axes, fluid_count), out_sh...  9.83 us
    ppermute x2, waiting for transfers between devices, along_chips(): lax.ppermute(values, axes, [(i, j) for i, j in route if 0 <= j < count])  8.05 us
    ppermute x1, starting transfers between devices, per_device(): partner = lax.ppermute(ends, axes, cores)  3.33 us
    all_to_all x1, waiting for transfers between devices, per_device(): moments = lax.all_to_all(moments, axes, 0, 0, tiled=True)  3.07 us
    ppermute x2, starting transfers between devices, along_chips(): lax.ppermute(values, axes, [(i, j) for i, j in route if 0 <= j < count])  2.58 us
  transfers between devices with their start and end apart: 5, of which 5 were waited for; matrix products, arithmetic and copies ran while one was open for 0% of the time, Pallas kernels for 12%

profile of v2, /device:TPU:1, one launch (start us, length us, event | category | flops | bytes accessed | tf_op | source)
XLA Modules:
  0.0 84.6 jit_solution(6851286543535001325)
XLA Ops:
  1.3 0.0 copy-start.2
  1.3 1.1 %shard_map.92.far_ref = f32[2,6,8,128]{3,2,1,0:T(8,128)S(1)} custom-call(s32[1]{0:T(128)S(6)} %copy.96.live_ref, f32[3,8192]{1,0:T(4,128)} %jitter_ref.5, f32[1,8192]{1,0:T(1,128)} %bitcast.170, f32[3,8192]{1,0:T(4,128)} %displacement_ref.7), custom_call_target="tpu_custom_call" | custom-call | tf_op jit(solution)/shard_map/pallas_call | solution.py:551
  2.3 0.0 copy-start
  2.4 3.3 %collective-permute-start.24 = (f32[2,6,8,128]{3,2,1,0:T(8,128)S(1)}, f32[2,6,8,128]{3,2,1,0:T(8,128)S(1)}, u32[]{:S(2)}, u32[]{:S(2)}) collective-permute-start(f32[2,6,8,128]{3,2,1,0:T(8,128)S(1)} %shard_map.92.far_ref), channel_id=1, source_target_pairs={{0,1},{1,0},{2,3},{3,2},{4,5},{5,4},{6,7},{7,6},{8,9},{9,8},{10,11... | collective-permute-start | bytes 147464 | tf_op jit(solution)/shard_map/ppermute | solution.py:570
  5.7 0.9 %collective-permute-done.24.near_ref.partner_ref = f32[2,6,8,128]{3,2,1,0:T(8,128)S(1)} collective-permute-done((f32[2,6,8,128]{3,2,1,0:T(8,128)S(1)}, f32[2,6,8,128]{3,2,1,0:T(8,128)S(1)}, u32[]{:S(2)}, u32[]{:S(2)}) %collective-permute-start.24) | collective-permute-done | bytes 49184 | tf_op jit(solution)/shard_map/ppermute | solution.py:570
  6.6 0.1 shard_map.93.near_ref
  6.7 1.3 %collective-permute-start.25 = (f32[6,8,128]{2,1,0:T(8,128)S(1)}, f32[6,8,128]{2,1,0:T(8,128)S(1)}, u32[]{:S(2)}, u32[]{:S(2)}) collective-permute-start(f32[6,8,128]{2,1,0:T(8,128)S(1)} %shard_map.93.near_ref), channel_id=1, source_target_pairs={{0,2},{2,4},{3,1},{4,6},{5,3},{6,8},{7,5},{8,10},{9,7},{10,12},{11... | collective-permute-start | bytes 73736 | tf_op jit(solution)/shard_map/ppermute | solution.py:536
  8.0 3.3 %collective-permute-done.25.far_ref.near_ref = f32[6,8,128]{2,1,0:T(8,128)S(1)} collective-permute-done((f32[6,8,128]{2,1,0:T(8,128)S(1)}, f32[6,8,128]{2,1,0:T(8,128)S(1)}, u32[]{:S(2)}, u32[]{:S(2)}) %collective-permute-start.25) | collective-permute-done | bytes 24608 | tf_op jit(solution)/shard_map/ppermute | solution.py:536
  11.3 0.1 shard_map.94
  11.4 0.0 copy-start.1
  11.4 1.3 %collective-permute-start.26 = (f32[6,8,128]{2,1,0:T(8,128)S(1)}, f32[6,8,128]{2,1,0:T(8,128)S(1)}, u32[]{:S(2)}, u32[]{:S(2)}) collective-permute-start(f32[6,8,128]{2,1,0:T(8,128)S(1)} %shard_map.94), channel_id=1, source_target_pairs={{0,4},{2,6},{4,8},{5,1},{6,10},{7,3},{8,12},{9,5},{10,14},{11,7},{... | collective-permute-start | bytes 73736 | tf_op jit(solution)/shard_map/ppermute | solution.py:536
  12.7 4.8 %collective-permute-done.26.far_ref = f32[6,8,128]{2,1,0:T(8,128)S(1)} collective-permute-done((f32[6,8,128]{2,1,0:T(8,128)S(1)}, f32[6,8,128]{2,1,0:T(8,128)S(1)}, u32[]{:S(2)}, u32[]{:S(2)}) %collective-permute-start.26) | collective-permute-done | bytes 24608 | tf_op jit(solution)/shard_map/ppermute | solution.py:536
  17.5 0.1 shard_map.95.mine_ref
  17.6 0.4 collective-permute-start.27
  18.0 0.9 %collective-permute-done.27.other_ref = f32[6,8,128]{2,1,0:T(8,128)S(1)} collective-permute-done((f32[6,8,128]{2,1,0:T(8,128)S(1)}, f32[6,8,128]{2,1,0:T(8,128)S(1)}, u32[]{:S(2)}, u32[]{:S(2)}) %collective-permute-start.27) | collective-permute-done | bytes 24608 | tf_op jit(solution)/shard_map/ppermute | solution.py:575
  18.9 0.0 copy-done.2
  18.9 0.0 copy-done
  18.9 0.0 copy-done.1
  18.9 30.2 %shard_map.96 = (f32[3,76,8,128]{3,2,1,0:T(8,128)S(1)}, f32[256,128]{1,0:T(8,128)}) custom-call(s32[1]{0:T(128)S(6)} %copy.96.live_ref, f32[3,8192]{1,0:T(4,128)S(1)} %copy-done.2, f32[1,8192]{1,0:T(1,128)S(1)} %bitcast.171, f32[3,8192]{1,0:T(4,128)S(1)} %copy-done, f32[2,6,8,128]{3,2,1,0:T(8,128)S(1)} %collective-permute-done.24.near_ref.partner_ref, ...), custom_call_target="tpu_custom_call" | custom-call | tf_op jit(solution)/shard_map/pallas_call | solution.py:581
  49.2 0.0 copy-start.4
  49.2 19.7 %all-to-all-start = ((f32[256,1,128]{2,1,0:T(1,128)}), f32[256,1,128]{2,1,0:T(1,128)S(1)}, u32[]{:S(2)}, u32[]{:S(2)}) async-start(f32[256,1,128]{2,1,0:T(1,128)} %bitcast.53), calls=%async_computation | async-start | bytes 262144 | tf_op jit(solution)/shard_map/all_to_all | solution.py:595
  68.8 0.0 copy-done.4
  68.9 9.8 %shard_map.97.fluid_basis_ref = f32[24,3,8,128]{3,2,1,0:T(8,128)S(1)} custom-call(s32[1]{0:T(128)S(6)} %copy.96.live_ref, f32[3,8192]{1,0:T(4,128)S(1)} %copy-done.2, f32[1,8192]{1,0:T(1,128)S(1)} %bitcast.172, f32[3,8192]{1,0:T(4,128)S(1)} %copy-done, f32[3,3072]{1,0:T(4,128)S(1)} %copy-done.4, ...), custom_call_target="tpu_custom_call" | custom-call | flops 6000000000 | bytes 10000000 | tf_op jit(solution)/shard_map/pallas_call | solution.py:596
  78.7 3.1 %all-to-all-done = f32[256,1,128]{2,1,0:T(1,128)S(1)} async-done(((f32[256,1,128]{2,1,0:T(1,128)}), f32[256,1,128]{2,1,0:T(1,128)S(1)}, u32[]{:S(2)}, u32[]{:S(2)}) %all-to-all-start) | async-done | bytes 131104 | tf_op jit(solution)/shard_map/all_to_all | solution.py:595
  81.8 1.3 %shard_map.98 = (f32[3,8192]{1,0:T(4,128)}, f32[3,8192]{1,0:T(4,128)S(1)}, f32[3,3072]{1,0:T(4,128)}, s32[1]{0:T(128)}) custom-call(s32[1]{0:T(128)S(6)} %copy.96.live_ref, f32[256,128]{1,0:T(8,128)S(1)} %bitcast.168, f32[1,8192]{1,0:T(1,128)S(1)} %bitcast.173, f32[3,8192]{1,0:T(4,128)S(1)} %copy-done, f32[3,76,8,128]{3,2,1,0:T(8,128)S(1)} %get-tuple-element.426.basis_ref, ...), custom_call_target="tpu_custom_call" | custom-call | tf_op jit(solution)/shard_map/pallas_call | solution.py:610
  83.7 0.2 conditional.1
  84.0 0.0 copy-start.6
  84.0 0.6 copy-done.6
Async XLA Ops:
  1.3 17.6 %copy-start.2 = (f32[3,8192]{1,0:T(4,128)S(1)}, f32[3,8192]{1,0:T(4,128)}, u32[]{:S(2)}) copy-start(f32[3,8192]{1,0:T(4,128)} %jitter_ref.5) | copy-start | bytes 294916
  2.3 16.6 %copy-start = (f32[3,8192]{1,0:T(4,128)S(1)}, f32[3,8192]{1,0:T(4,128)}, u32[]{:S(2)}) copy-start(f32[3,8192]{1,0:T(4,128)} %displacement_ref.7) | copy-start | bytes 294916
  2.4 4.2 %collective-permute-start.24 = (f32[2,6,8,128]{3,2,1,0:T(8,128)S(1)}, f32[2,6,8,128]{3,2,1,0:T(8,128)S(1)}, u32[]{:S(2)}, u32[]{:S(2)}) collective-permute-start(f32[2,6,8,128]{3,2,1,0:T(8,128)S(1)} %shard_map.92.far_ref), channel_id=1, source_target_pairs={{0,1},{1,0},{2,3},{3,2},{4,5},{5,4},{6,7},{7,6},{8,9},{9,8},{10,11... | collective-permute-start | bytes 147464 | tf_op jit(solution)/shard_map/ppermute | solution.py:570
  6.7 4.6 %collective-permute-start.25 = (f32[6,8,128]{2,1,0:T(8,128)S(1)}, f32[6,8,128]{2,1,0:T(8,128)S(1)}, u32[]{:S(2)}, u32[]{:S(2)}) collective-permute-start(f32[6,8,128]{2,1,0:T(8,128)S(1)} %shard_map.93.near_ref), channel_id=1, source_target_pairs={{0,2},{2,4},{3,1},{4,6},{5,3},{6,8},{7,5},{8,10},{9,7},{10,12},{11... | collective-permute-start | bytes 73736 | tf_op jit(solution)/shard_map/ppermute | solution.py:536
  11.4 7.5 %copy-start.1 = (f32[8192]{0:T(1024)S(1)}, f32[8192]{0:T(1024)}, u32[]{:S(2)}) copy-start(f32[8192]{0:T(1024)} %param.24) | copy-start | bytes 98308
  11.4 6.1 %collective-permute-start.26 = (f32[6,8,128]{2,1,0:T(8,128)S(1)}, f32[6,8,128]{2,1,0:T(8,128)S(1)}, u32[]{:S(2)}, u32[]{:S(2)}) collective-permute-start(f32[6,8,128]{2,1,0:T(8,128)S(1)} %shard_map.94), channel_id=1, source_target_pairs={{0,4},{2,6},{4,8},{5,1},{6,10},{7,3},{8,12},{9,5},{10,14},{11,7},{... | collective-permute-start | bytes 73736 | tf_op jit(solution)/shard_map/ppermute | solution.py:536
  17.6 1.3 %collective-permute-start.27 = (f32[6,8,128]{2,1,0:T(8,128)S(1)}, f32[6,8,128]{2,1,0:T(8,128)S(1)}, u32[]{:S(2)}, u32[]{:S(2)}) collective-permute-start(f32[6,8,128]{2,1,0:T(8,128)S(1)} %shard_map.95.mine_ref), channel_id=1, source_target_pairs={{0,1},{1,0},{2,3},{3,2},{4,5},{5,4},{6,7},{7,6},{8,9},{9,8},{10,11... | collective-permute-start | bytes 73736 | tf_op jit(solution)/shard_map/ppermute | solution.py:575
  49.2 19.7 %copy-start.4 = (f32[3,3072]{1,0:T(4,128)S(1)}, f32[3,3072]{1,0:T(4,128)}, u32[]{:S(2)}) copy-start(f32[3,3072]{1,0:T(4,128)} %fluid_ref.1) | copy-start | bytes 110596
  49.2 32.6 %all-to-all-start = ((f32[256,1,128]{2,1,0:T(1,128)}), f32[256,1,128]{2,1,0:T(1,128)S(1)}, u32[]{:S(2)}, u32[]{:S(2)}) async-start(f32[256,1,128]{2,1,0:T(1,128)} %bitcast.53), calls=%async_computation | async-start | bytes 262144 | tf_op jit(solution)/shard_map/all_to_all | solution.py:595
  84.0 0.7 copy-start.6

commit v3 on v2

--- a/solution.py
+++ b/solution.py
@@ -10,12 +10,11 @@
 ITERS = 3
 HALO = 6
 BASE = 2 * HALO
-NEAR = 4
 PIECES = 48
 MAX_AMPLIFICATION = 50.0
 MOMENTS = 2 * ITERS + 1
-GROUP = 4
-APPLY_UNROLL = 8
+GROUP = 8
+APPLY_UNROLL = 16
 
 stretch_factors = (1.0, 6.0, 6.0)
 
@@ -66,36 +65,50 @@
 
 def centred(jitter):
     row = lax.broadcasted_iota(jnp.int32, (8, BLK), 0)
-    scale = jnp.where(row == 0, 0.5, 3.0)
-    shift = jnp.where(row == 0, 0.25, 1.5)
+    scale = jnp.where(row == 0, 2.0, 12.0)
+    shift = jnp.where(row == 0, 1.0, 6.0)
     return jnp.where(row < 3, jitter * scale - shift, 0.0)
 
 
 def source_rows(points, norm):
-    extended = jnp.where(rows_of(3), norm, jnp.where(rows_of(4), 1.0, points))
+    row = lax.broadcasted_iota(jnp.int32, (8, BLK), 0)
+    extended = jnp.where(row >= 4, 1.0, points)
+    extended = jnp.where(row == 3, norm, jnp.where(row == 5, points[0:1], extended))
     high, middle, low = split(extended)
     return jnp.concatenate([high, high, middle, high, low, middle], axis=0)
 
 
-def target_parts(points, norm):
-    base = jnp.where(rows_of(4), norm, -2.0 * points)
-    slope = jnp.where(rows_of(0), 1.0, jnp.where(rows_of(4), -points[0:1], 0.0))
-    return base, slope
-
-
-def target_rows(base, slope, delta):
-    moved = base + float(delta) * slope + jnp.where(rows_of(4), 0.25 * delta * delta, 0.0)
-    high, middle, low = split(moved)
-    first = jnp.where(rows_of(3), 1.0, high)
-    return jnp.concatenate([first, middle, first, low, first, middle], axis=0).astype(jnp.bfloat16)
-
-
-def wendland_of_quarter(quarter):
-    quarter = jnp.maximum(quarter, 1e-30)
-    scaled = quarter * lax.rsqrt(quarter)
-    remain = jnp.maximum(1.0 - scaled, 0.0)
+def target_values(points, norm):
+    return jnp.where(rows_of(4), norm, -2.0 * points)
+
+
+def target_groups(values):
+    high, middle, low = split(values)
+    bases = (jnp.where(rows_of(3), 1.0, high), middle, low)
+    slopes = [jnp.where(rows_of(6), 2.0 * piece[0:1], 0.0) for piece in (high, middle, low)]
+    slopes[0] = jnp.where(rows_of(5), 4.0, slopes[0])
+    return bases, slopes
+
+
+def target_rows(groups, delta):
+    bases, slopes = groups
+    if delta:
+        bases = [base + float(delta) * slope for base, slope in zip(bases, slopes)]
+        bases[0] = jnp.where(rows_of(7), 4.0 * delta * delta, bases[0])
+    first = jnp.concatenate([bases[0], bases[1]], axis=0).astype(jnp.bfloat16)
+    second = jnp.concatenate([bases[0], bases[2]], axis=0).astype(jnp.bfloat16)
+    return jnp.concatenate([first, second, first], axis=0)
+
+
+PHI_SCALE = 256.0
+
+
+def wendland_scaled(distances):
+    distances = jnp.maximum(distances, 1e-30)
+    scaled = distances * lax.rsqrt(distances)
+    remain = jnp.maximum(4.0 - scaled, 0.0)
     square = remain * remain
-    return square * square * (4.0 * scaled + 1.0)
+    return square * square * (scaled + 1.0)
 
 
 def store_pair(ref, values, first_row):
@@ -106,6 +119,7 @@
 
 
 def vector_pair(values):
+    values = values * (1.0 / PHI_SCALE)
     high = values.astype(jnp.bfloat16).astype(jnp.float32)
     return jnp.concatenate([high, values - high], axis=0).astype(jnp.bfloat16)
 
@@ -155,7 +169,7 @@
     axes, block_count,
     live_ref, jitter_ref, smoothing_ref, displacement_ref, partner_ref, mine_ref, other_ref,
     basis_ref, moments_ref,
-    joined, source, base, slope, inverse, w0, z0, z1, z2, b0, b1, b2, matrix,
+    joined, source, target, inverse, w0, z0, z1, z2, b0, b1, b2, matrix,
 ):
     w1_ref, w2_ref, w3_ref = (basis_ref.at[k] for k in range(3))
     live = live_ref[0]
@@ -167,7 +181,7 @@
     def prepare(block, carry):
         points, norm, scale, rhs = parts_of(joined[BASE - HALO + block])
         source[block] = source_of(points, norm)
-        base[block], slope[block] = target_parts(points, norm)
+        target[block] = target_values(points, norm)
         inverse[block] = scale
         w0[block] = rhs
         z0[block] = rhs * scale
@@ -176,37 +190,47 @@
 
     lax.fori_loop(0, width, prepare, 0, unroll=4)
 
-    def generate_two(row):
-        for place in range(6):
+
+    def generate_two(block):
+        first, second = target_groups(target[block]), target_groups(target[block + 1])
+        for place in range(4):
             columns = []
-            if place < 5:
-                columns.append(target_rows(base[row + 2], slope[row + 2], place - 2))
+            if place < 3:
+                columns.append(target_rows(first, place))
             if place > 0:
-                columns.append(target_rows(base[row + 3], slope[row + 3], place - 3))
-            quarter = jnp.dot(
-                source[row + place],
+                columns.append(target_rows(second, place - 1))
+            distances = jnp.dot(
+                source[block + place],
                 jnp.concatenate(columns, axis=1),
                 preferred_element_type=jnp.float32,
             )
-            values = wendland_of_quarter(quarter)
-            if place < 5:
-                store_pair(matrix.at[row], values[:, :BLK], place * BLK)
+            values = wendland_scaled(distances)
+            if place < 3:
+                store_pair(matrix.at[block], values[:, :BLK], place * BLK)
             if place > 0:
-                store_pair(matrix.at[row + 1], values[:, -BLK:], (place - 1) * BLK)
-
-    def apply_row(row, values, pairs, place_next):
-        near = jnp.concatenate([pairs[row + place] for place in range(5)], axis=1)
-        product = jnp.dot(near, matrix[row], preferred_element_type=jnp.float32)
-        place_next(row + 2, sum_pairs(product, 0) - values[row + 2])
+                store_pair(matrix.at[block + 1], values[:, -BLK:], (place - 1) * BLK)
+
+    def apply_row(block, values, pairs, place_next):
+        near = jnp.concatenate([pairs[block + place] for place in range(3)], axis=1)
+        product = jnp.dot(near, matrix[block], preferred_element_type=jnp.float32)
+        image = sum_pairs(product, 0) - values[block]
+        for back in (1, 2):
+            behind = pairs[block - back]
+            product = lax.dot_general(
+                jnp.concatenate([behind, behind], axis=1),
+                matrix[block - back, back * BLK : (back + 1) * BLK, :],
+                (((1,), (1,)), ((), ())),
+                preferred_element_type=jnp.float32,
+            )
+            image = image + (product[0:8] + product[8:16])
+        place_next(block, image)
 
     def apply(values, pairs, first, last, place_next):
-        def one_row(row, carry):
-            apply_row(row, values, pairs, place_next)
+        def one_row(block, carry):
+            apply_row(block, values, pairs, place_next)
             return carry
 
         lax.fori_loop(first, last, one_row, 0, unroll=APPLY_UNROLL)
-
-    rows = block_count + 2 * NEAR
 
     def first_next(block, image):
         scaled = image * inverse[block]
@@ -225,22 +249,24 @@
 
     def generate_group(group):
         for row in range(0, GROUP, 2):
-            generate_two(group * GROUP + row)
+            generate_two(2 + group * GROUP + row)
 
     def apply_group(group):
         for row in range(GROUP):
-            apply_row(group * GROUP + row, z0, b0, first_next)
+            apply_row(2 + group * GROUP + row, z0, b0, first_next)
 
     def apply_then_generate(group, carry):
         apply_group(group - 1)
         generate_group(group)
         return carry
 
+    groups = (width - 4) // GROUP
+    generate_two(0)
     generate_group(0)
-    lax.fori_loop(1, rows // GROUP, apply_then_generate, 0)
-    apply_group(rows // GROUP - 1)
-    apply(z1, b1, 2, rows - 2, second_next)
-    apply(z2, b2, 4, rows - 4, third_next)
+    lax.fori_loop(1, groups, apply_then_generate, 0)
+    apply_group(groups - 1)
+    apply(z1, b1, 4, width - 4, second_next)
+    apply(z2, b2, 6, width - 6, third_next)
 
     def add_up(own, sums):
         block = own + HALO
@@ -299,12 +325,12 @@
         jitter = jnp.concatenate([fluid_ref[:, lanes], jnp.zeros((5, BLK), jnp.float32)], axis=0)
         points = centred(jitter)
         norm = jnp.sum(points * points, axis=0, keepdims=True)
-        base_here, slope_here = target_parts(points, norm)
+        groups = target_groups(target_values(points, norm))
         first = anchor_of(index) + (HALO - 2)
         for place in range(5):
-            columns = target_rows(base_here, slope_here, place - 2)
-            quarter = jnp.dot(source[first + place], columns, preferred_element_type=jnp.float32)
-            store_pair(matrix.at[index], wendland_of_quarter(quarter), place * BLK)
+            columns = target_rows(groups, place - 2)
+            distances = jnp.dot(source[first + place], columns, preferred_element_type=jnp.float32)
+            store_pair(matrix.at[index], wendland_scaled(distances), place * BLK)
         return carry
 
     def apply_fluid(index, carry):
@@ -586,9 +612,9 @@
         scratch_shapes=[
             joined,
             source,
-            *[vectors] * 7,
+            *[vectors] * 6,
             *[pairs] * 3,
-            pltpu.VMEM((block_count + 2 * NEAR, 5 * BLK, 2 * BLK), jnp.bfloat16),
+            pltpu.VMEM((width - 2, 3 * BLK, 2 * BLK), jnp.bfloat16),
         ],
         compiler_params=pltpu.CompilerParams(vmem_limit_bytes=48 * 2**20),
     )(live_blocks, wing_jitter, smoothing_row, displacement, partner, mine, other)

time: 84.9 us -> 80.7 us (0.951)
  Pallas kernels: 42.8 us -> 38.5 us
    pallas_call x1, Pallas kernels: 30.2 us -> 26.1 us  [per_device(): pl.pallas_call(functools.partial(chain_kernel, axes, block_count), out_sh...]
where the time goes in v3:
time: 80.7 us; the launch traced here: 80.4 us
  Pallas kernels  38.5 us (48%)
  starting transfers between devices  25.9 us (32%)
  waiting for transfers between devices  13.1 us (16%)
  between operations  2.05 us (3%)
    pallas_call x1, Pallas kernels, per_device(): pl.pallas_call(functools.partial(chain_kernel, axes, block_count), out_sh...  26.1 us
    all_to_all x1, starting transfers between devices, per_device(): moments = lax.all_to_all(moments, axes, 0, 0, tiled=True)  19.6 us
    pallas_call x1, Pallas kernels, per_device(): pl.pallas_call(functools.partial(fluid_kernel, axes, fluid_count), out_sh...  9.67 us
    ppermute x2, waiting for transfers between devices, along_chips(): lax.ppermute(values, axes, [(i, j) for i, j in route if 0 <= j < count])  8.05 us
    ppermute x1, starting transfers between devices, per_device(): partner = lax.ppermute(ends, axes, cores)  3.33 us
    all_to_all x1, waiting for transfers between devices, per_device(): moments = lax.all_to_all(moments, axes, 0, 0, tiled=True)  3.23 us
    ppermute x2, starting transfers between devices, along_chips(): lax.ppermute(values, axes, [(i, j) for i, j in route if 0 <= j < count])  2.58 us
  transfers between devices with their start and end apart: 5, of which 5 were waited for; matrix products, arithmetic and copies ran while one was open for 0% of the time, Pallas kernels for 12%

profile of v3, /device:TPU:1, one launch (start us, length us, event | category | flops | bytes accessed | tf_op | source)
XLA Modules:
  0.0 80.4 jit_solution(8060613502061846726)
XLA Ops:
  1.3 0.0 copy-start.2
  1.3 1.1 %shard_map.92.far_ref = f32[2,6,8,128]{3,2,1,0:T(8,128)S(1)} custom-call(s32[1]{0:T(128)S(6)} %copy.96.live_ref, f32[3,8192]{1,0:T(4,128)} %jitter_ref.5, f32[1,8192]{1,0:T(1,128)} %bitcast.170, f32[3,8192]{1,0:T(4,128)} %displacement_ref.7), custom_call_target="tpu_custom_call" | custom-call | tf_op jit(solution)/shard_map/pallas_call | solution.py:577
  2.3 0.0 copy-start
  2.4 3.3 %collective-permute-start.24 = (f32[2,6,8,128]{3,2,1,0:T(8,128)S(1)}, f32[2,6,8,128]{3,2,1,0:T(8,128)S(1)}, u32[]{:S(2)}, u32[]{:S(2)}) collective-permute-start(f32[2,6,8,128]{3,2,1,0:T(8,128)S(1)} %shard_map.92.far_ref), channel_id=1, source_target_pairs={{0,1},{1,0},{2,3},{3,2},{4,5},{5,4},{6,7},{7,6},{8,9},{9,8},{10,11... | collective-permute-start | bytes 147464 | tf_op jit(solution)/shard_map/ppermute | solution.py:596
  5.7 0.9 %collective-permute-done.24.near_ref.partner_ref = f32[2,6,8,128]{3,2,1,0:T(8,128)S(1)} collective-permute-done((f32[2,6,8,128]{3,2,1,0:T(8,128)S(1)}, f32[2,6,8,128]{3,2,1,0:T(8,128)S(1)}, u32[]{:S(2)}, u32[]{:S(2)}) %collective-permute-start.24) | collective-permute-done | bytes 49184 | tf_op jit(solution)/shard_map/ppermute | solution.py:596
  6.6 0.1 shard_map.93.near_ref
  6.7 1.3 %collective-permute-start.25 = (f32[6,8,128]{2,1,0:T(8,128)S(1)}, f32[6,8,128]{2,1,0:T(8,128)S(1)}, u32[]{:S(2)}, u32[]{:S(2)}) collective-permute-start(f32[6,8,128]{2,1,0:T(8,128)S(1)} %shard_map.93.near_ref), channel_id=1, source_target_pairs={{0,2},{2,4},{3,1},{4,6},{5,3},{6,8},{7,5},{8,10},{9,7},{10,12},{11... | collective-permute-start | bytes 73736 | tf_op jit(solution)/shard_map/ppermute | solution.py:562
  8.0 3.3 %collective-permute-done.25.far_ref.near_ref = f32[6,8,128]{2,1,0:T(8,128)S(1)} collective-permute-done((f32[6,8,128]{2,1,0:T(8,128)S(1)}, f32[6,8,128]{2,1,0:T(8,128)S(1)}, u32[]{:S(2)}, u32[]{:S(2)}) %collective-permute-start.25) | collective-permute-done | bytes 24608 | tf_op jit(solution)/shard_map/ppermute | solution.py:562
  11.3 0.1 shard_map.94
  11.4 0.0 copy-start.1
  11.4 1.3 %collective-permute-start.26 = (f32[6,8,128]{2,1,0:T(8,128)S(1)}, f32[6,8,128]{2,1,0:T(8,128)S(1)}, u32[]{:S(2)}, u32[]{:S(2)}) collective-permute-start(f32[6,8,128]{2,1,0:T(8,128)S(1)} %shard_map.94), channel_id=1, source_target_pairs={{0,4},{2,6},{4,8},{5,1},{6,10},{7,3},{8,12},{9,5},{10,14},{11,7},{... | collective-permute-start | bytes 73736 | tf_op jit(solution)/shard_map/ppermute | solution.py:562
  12.7 4.8 %collective-permute-done.26.far_ref = f32[6,8,128]{2,1,0:T(8,128)S(1)} collective-permute-done((f32[6,8,128]{2,1,0:T(8,128)S(1)}, f32[6,8,128]{2,1,0:T(8,128)S(1)}, u32[]{:S(2)}, u32[]{:S(2)}) %collective-permute-start.26) | collective-permute-done | bytes 24608 | tf_op jit(solution)/shard_map/ppermute | solution.py:562
  17.5 0.1 shard_map.95.mine_ref
  17.6 0.4 collective-permute-start.27
  18.0 0.9 %collective-permute-done.27.other_ref = f32[6,8,128]{2,1,0:T(8,128)S(1)} collective-permute-done((f32[6,8,128]{2,1,0:T(8,128)S(1)}, f32[6,8,128]{2,1,0:T(8,128)S(1)}, u32[]{:S(2)}, u32[]{:S(2)}) %collective-permute-start.27) | collective-permute-done | bytes 24608 | tf_op jit(solution)/shard_map/ppermute | solution.py:601
  18.9 0.0 copy-done.2
  18.9 0.0 copy-done
  18.9 0.0 copy-done.1
  18.9 26.1 %shard_map.96 = (f32[3,76,8,128]{3,2,1,0:T(8,128)S(1)}, f32[256,128]{1,0:T(8,128)}) custom-call(s32[1]{0:T(128)S(6)} %copy.96.live_ref, f32[3,8192]{1,0:T(4,128)S(1)} %copy-done.2, f32[1,8192]{1,0:T(1,128)S(1)} %bitcast.171, f32[3,8192]{1,0:T(4,128)S(1)} %copy-done, f32[2,6,8,128]{3,2,1,0:T(8,128)S(1)} %collective-permute-done.24.near_ref.partner_ref, ...), custom_call_target="tpu_custom_call" | custom-call | tf_op jit(solution)/shard_map/pallas_call | solution.py:607
  45.0 0.0 copy-start.4
  45.0 19.6 %all-to-all-start = ((f32[256,1,128]{2,1,0:T(1,128)}), f32[256,1,128]{2,1,0:T(1,128)S(1)}, u32[]{:S(2)}, u32[]{:S(2)}) async-start(f32[256,1,128]{2,1,0:T(1,128)} %bitcast.53), calls=%async_computation | async-start | bytes 262144 | tf_op jit(solution)/shard_map/all_to_all | solution.py:621
  64.7 0.0 copy-done.4
  64.7 9.7 %shard_map.97.fluid_basis_ref = f32[24,3,8,128]{3,2,1,0:T(8,128)S(1)} custom-call(s32[1]{0:T(128)S(6)} %copy.96.live_ref, f32[3,8192]{1,0:T(4,128)S(1)} %copy-done.2, f32[1,8192]{1,0:T(1,128)S(1)} %bitcast.172, f32[3,8192]{1,0:T(4,128)S(1)} %copy-done, f32[3,3072]{1,0:T(4,128)S(1)} %copy-done.4, ...), custom_call_target="tpu_custom_call" | custom-call | flops 6000000000 | bytes 10000000 | tf_op jit(solution)/shard_map/pallas_call | solution.py:622
  74.4 3.2 %all-to-all-done = f32[256,1,128]{2,1,0:T(1,128)S(1)} async-done(((f32[256,1,128]{2,1,0:T(1,128)}), f32[256,1,128]{2,1,0:T(1,128)S(1)}, u32[]{:S(2)}, u32[]{:S(2)}) %all-to-all-start) | async-done | bytes 131104 | tf_op jit(solution)/shard_map/all_to_all | solution.py:621
  77.6 1.3 %shard_map.98 = (f32[3,8192]{1,0:T(4,128)}, f32[3,8192]{1,0:T(4,128)S(1)}, f32[3,3072]{1,0:T(4,128)}, s32[1]{0:T(128)}) custom-call(s32[1]{0:T(128)S(6)} %copy.96.live_ref, f32[256,128]{1,0:T(8,128)S(1)} %bitcast.168, f32[1,8192]{1,0:T(1,128)S(1)} %bitcast.173, f32[3,8192]{1,0:T(4,128)S(1)} %copy-done, f32[3,76,8,128]{3,2,1,0:T(8,128)S(1)} %get-tuple-element.426.basis_ref, ...), custom_call_target="tpu_custom_call" | custom-call | tf_op jit(solution)/shard_map/pallas_call | solution.py:636
  79.5 0.2 conditional.1
  79.8 0.0 copy-start.6
  79.8 0.6 copy-done.6
Async XLA Ops:
  1.3 17.6 %copy-start.2 = (f32[3,8192]{1,0:T(4,128)S(1)}, f32[3,8192]{1,0:T(4,128)}, u32[]{:S(2)}) copy-start(f32[3,8192]{1,0:T(4,128)} %jitter_ref.5) | copy-start | bytes 294916
  2.3 16.6 %copy-start = (f32[3,8192]{1,0:T(4,128)S(1)}, f32[3,8192]{1,0:T(4,128)}, u32[]{:S(2)}) copy-start(f32[3,8192]{1,0:T(4,128)} %displacement_ref.7) | copy-start | bytes 294916
  2.4 4.2 %collective-permute-start.24 = (f32[2,6,8,128]{3,2,1,0:T(8,128)S(1)}, f32[2,6,8,128]{3,2,1,0:T(8,128)S(1)}, u32[]{:S(2)}, u32[]{:S(2)}) collective-permute-start(f32[2,6,8,128]{3,2,1,0:T(8,128)S(1)} %shard_map.92.far_ref), channel_id=1, source_target_pairs={{0,1},{1,0},{2,3},{3,2},{4,5},{5,4},{6,7},{7,6},{8,9},{9,8},{10,11... | collective-permute-start | bytes 147464 | tf_op jit(solution)/shard_map/ppermute | solution.py:596
  6.7 4.6 %collective-permute-start.25 = (f32[6,8,128]{2,1,0:T(8,128)S(1)}, f32[6,8,128]{2,1,0:T(8,128)S(1)}, u32[]{:S(2)}, u32[]{:S(2)}) collective-permute-start(f32[6,8,128]{2,1,0:T(8,128)S(1)} %shard_map.93.near_ref), channel_id=1, source_target_pairs={{0,2},{2,4},{3,1},{4,6},{5,3},{6,8},{7,5},{8,10},{9,7},{10,12},{11... | collective-permute-start | bytes 73736 | tf_op jit(solution)/shard_map/ppermute | solution.py:562
  11.4 7.5 %copy-start.1 = (f32[8192]{0:T(1024)S(1)}, f32[8192]{0:T(1024)}, u32[]{:S(2)}) copy-start(f32[8192]{0:T(1024)} %param.24) | copy-start | bytes 98308
  11.4 6.1 %collective-permute-start.26 = (f32[6,8,128]{2,1,0:T(8,128)S(1)}, f32[6,8,128]{2,1,0:T(8,128)S(1)}, u32[]{:S(2)}, u32[]{:S(2)}) collective-permute-start(f32[6,8,128]{2,1,0:T(8,128)S(1)} %shard_map.94), channel_id=1, source_target_pairs={{0,4},{2,6},{4,8},{5,1},{6,10},{7,3},{8,12},{9,5},{10,14},{11,7},{... | collective-permute-start | bytes 73736 | tf_op jit(solution)/shard_map/ppermute | solution.py:562
  17.6 1.3 %collective-permute-start.27 = (f32[6,8,128]{2,1,0:T(8,128)S(1)}, f32[6,8,128]{2,1,0:T(8,128)S(1)}, u32[]{:S(2)}, u32[]{:S(2)}) collective-permute-start(f32[6,8,128]{2,1,0:T(8,128)S(1)} %shard_map.95.mine_ref), channel_id=1, source_target_pairs={{0,1},{1,0},{2,3},{3,2},{4,5},{5,4},{6,7},{7,6},{8,9},{9,8},{10,11... | collective-permute-start | bytes 73736 | tf_op jit(solution)/shard_map/ppermute | solution.py:601
  45.0 19.6 %copy-start.4 = (f32[3,3072]{1,0:T(4,128)S(1)}, f32[3,3072]{1,0:T(4,128)}, u32[]{:S(2)}) copy-start(f32[3,3072]{1,0:T(4,128)} %fluid_ref.1) | copy-start | bytes 110596
  45.0 32.6 %all-to-all-start = ((f32[256,1,128]{2,1,0:T(1,128)}), f32[256,1,128]{2,1,0:T(1,128)S(1)}, u32[]{:S(2)}, u32[]{:S(2)}) async-start(f32[256,1,128]{2,1,0:T(1,128)} %bitcast.53), calls=%async_computation | async-start | bytes 262144 | tf_op jit(solution)/shard_map/all_to_all | solution.py:621
  79.8 0.7 copy-start.6

commit v4 on v3

--- a/solution.py
+++ b/solution.py
@@ -13,7 +13,6 @@
 PIECES = 48
 MAX_AMPLIFICATION = 50.0
 MOMENTS = 2 * ITERS + 1
-GROUP = 8
 APPLY_UNROLL = 16
 
 stretch_factors = (1.0, 6.0, 6.0)
@@ -165,11 +164,55 @@
     return jnp.transpose(source_rows(points, norm)).astype(jnp.bfloat16)
 
 
+def generate_two(source, target, matrix, block, row):
+    first, second = target_groups(target[block]), target_groups(target[block + 1])
+    for place in range(4):
+        columns = []
+        if place < 3:
+            columns.append(target_rows(first, place))
+        if place > 0:
+            columns.append(target_rows(second, place - 1))
+        distances = jnp.dot(
+            source[block + place],
+            jnp.concatenate(columns, axis=1),
+            preferred_element_type=jnp.float32,
+        )
+        values = wendland_scaled(distances)
+        if place < 3:
+            store_pair(matrix.at[row], values[:, :BLK], place * BLK)
+        if place > 0:
+            store_pair(matrix.at[row + 1], values[:, -BLK:], (place - 1) * BLK)
+
+
+def own_kernel(first, rows, last, jitter_ref, *refs):
+    matrix, source, target = refs[-3:]
+
+    def prepare(block, carry):
+        lanes = pl.ds(pl.multiple_of((first + block) * BLK, BLK), BLK)
+        jitter = jnp.concatenate([jitter_ref[:, lanes], jnp.zeros((5, BLK), jnp.float32)], axis=0)
+        points = centred(jitter)
+        norm = jnp.sum(points * points, axis=0, keepdims=True)
+        source[block] = source_of(points, norm)
+        target[block] = target_values(points, norm)
+        return carry
+
+    lax.fori_loop(0, rows + 2, prepare, 0, unroll=4)
+
+    def generate(pair, carry):
+        generate_two(source, target, matrix, 2 * pair, HALO + first + 2 * pair)
+        return carry
+
+    lax.fori_loop(0, rows // 2, generate, 0, unroll=4)
+    if last:
+        for row in range(HALO + first + rows, matrix.shape[0]):
+            matrix[row] = jnp.zeros(matrix.shape[1:], matrix.dtype)
+
+
 def chain_kernel(
     axes, block_count,
-    live_ref, jitter_ref, smoothing_ref, displacement_ref, partner_ref, mine_ref, other_ref,
-    basis_ref, moments_ref,
-    joined, source, target, inverse, w0, z0, z1, z2, b0, b1, b2, matrix,
+    live_ref, jitter_ref, smoothing_ref, displacement_ref, partner_ref, mine_ref, other_ref, _,
+    basis_ref, moments_ref, matrix,
+    joined, source, target, inverse, w0, z0, z1, z2, b0, b1, b2,
 ):
     w1_ref, w2_ref, w3_ref = (basis_ref.at[k] for k in range(3))
     live = live_ref[0]
@@ -179,9 +222,7 @@
     )
 
     def prepare(block, carry):
-        points, norm, scale, rhs = parts_of(joined[BASE - HALO + block])
-        source[block] = source_of(points, norm)
-        target[block] = target_values(points, norm)
+        _, _, scale, rhs = parts_of(joined[BASE - HALO + block])
         inverse[block] = scale
         w0[block] = rhs
         z0[block] = rhs * scale
@@ -190,25 +231,13 @@
 
     lax.fori_loop(0, width, prepare, 0, unroll=4)
 
-
-    def generate_two(block):
-        first, second = target_groups(target[block]), target_groups(target[block + 1])
-        for place in range(4):
-            columns = []
-            if place < 3:
-                columns.append(target_rows(first, place))
-            if place > 0:
-                columns.append(target_rows(second, place - 1))
-            distances = jnp.dot(
-                source[block + place],
-                jnp.concatenate(columns, axis=1),
-                preferred_element_type=jnp.float32,
-            )
-            values = wendland_scaled(distances)
-            if place < 3:
-                store_pair(matrix.at[block], values[:, :BLK], place * BLK)
-            if place > 0:
-                store_pair(matrix.at[block + 1], values[:, -BLK:], (place - 1) * BLK)
+    for start in (0, live + HALO - 2):
+        for block in range(HALO + 2):
+            points, norm, _, _ = parts_of(joined[BASE - HALO + start + block])
+            source[block] = source_of(points, norm)
+            target[block] = target_values(points, norm)
+        for row in range(0, HALO, 2):
+            generate_two(source, target, matrix, row, start + row)
 
     def apply_row(block, values, pairs, place_next):
         near = jnp.concatenate([pairs[block + place] for place in range(3)], axis=1)
@@ -247,24 +276,7 @@
     def third_next(block, image):
         w3_ref[block] = image
 
-    def generate_group(group):
-        for row in range(0, GROUP, 2):
-            generate_two(2 + group * GROUP + row)
-
-    def apply_group(group):
-        for row in range(GROUP):
-            apply_row(2 + group * GROUP + row, z0, b0, first_next)
-
-    def apply_then_generate(group, carry):
-        apply_group(group - 1)
-        generate_group(group)
-        return carry
-
-    groups = (width - 4) // GROUP
-    generate_two(0)
-    generate_group(0)
-    lax.fori_loop(1, groups, apply_then_generate, 0)
-    apply_group(groups - 1)
+    apply(z0, b0, 2, width - 2, first_next)
     apply(z1, b1, 4, width - 4, second_next)
     apply(z2, b2, 6, width - 6, third_next)
 
@@ -604,20 +616,41 @@
     pairs = pltpu.VMEM((width, 16, BLK), jnp.bfloat16)
     joined = pltpu.VMEM((2 * BASE + block_count, 8, BLK), jnp.float32)
     source = pltpu.VMEM((width, BLK, PIECES), jnp.bfloat16)
-    basis, moments = pl.pallas_call(
+    matrix_shape = jax.ShapeDtypeStruct((width - 2, 3 * BLK, 2 * BLK), jnp.bfloat16)
+    own_rows = block_count - 2
+    first_rows = block_count // 2
+
+    def own_part(first, rows, *matrix):
+        return pl.pallas_call(
+            functools.partial(own_kernel, first, rows, first + rows == own_rows),
+            out_shape=matrix_shape,
+            in_specs=[in_vmem] * (1 + len(matrix)),
+            out_specs=in_vmem,
+            input_output_aliases={1: 0} if matrix else {},
+            scratch_shapes=[
+                pltpu.VMEM((rows + 2, BLK, PIECES), jnp.bfloat16),
+                pltpu.VMEM((rows + 2, 8, BLK), jnp.float32),
+            ],
+            compiler_params=small,
+            cost_estimate=pl.CostEstimate(flops=4 * 10**9, bytes_accessed=10**6, transcendentals=10**6),
+        )(wing_jitter, *matrix)
+
+    matrix = own_part(first_rows, own_rows - first_rows, own_part(0, first_rows))
+    basis, moments, _ = pl.pallas_call(
         functools.partial(chain_kernel, axes, block_count),
-        out_shape=(floats(3, width, 8, BLK), floats(lax.axis_size(axes), BLK)),
-        in_specs=[in_smem] + [in_vmem] * 6,
-        out_specs=(in_vmem,) * 2,
+        out_shape=(floats(3, width, 8, BLK), floats(lax.axis_size(axes), BLK), matrix_shape),
+        in_specs=[in_smem] + [in_vmem] * 7,
+        out_specs=(in_vmem,) * 3,
+        input_output_aliases={7: 2},
         scratch_shapes=[
             joined,
-            source,
-            *[vectors] * 6,
+            pltpu.VMEM((HALO + 2, BLK, PIECES), jnp.bfloat16),
+            pltpu.VMEM((HALO + 2, 8, BLK), jnp.float32),
+            *[vectors] * 5,
             *[pairs] * 3,
-            pltpu.VMEM((width - 2, 3 * BLK, 2 * BLK), jnp.bfloat16),
         ],
-        compiler_params=pltpu.CompilerParams(vmem_limit_bytes=48 * 2**20),
-    )(live_blocks, wing_jitter, smoothing_row, displacement, partner, mine, other)
+        compiler_params=pltpu.CompilerParams(vmem_limit_bytes=12 * 2**20),
+    )(live_blocks, wing_jitter, smoothing_row, displacement, partner, mine, other, matrix)
     moments = lax.all_to_all(moments, axes, 0, 0, tiled=True)
     fluid_basis = pl.pallas_call(
         functools.partial(fluid_kernel, axes, fluid_count),

time: 80.7 us -> 78.7 us (0.975)
  waiting for transfers between devices: 13.1 us -> 7.39 us
  Pallas kernels: 38.5 us -> 42 us
    pallas_call x0 -> x2, Pallas kernels: none -> 10.8 us  [own_part(): pl.pallas_call(functools.partial(own_kernel, first, rows, first + rows ==...]
    pallas_call x1, Pallas kernels: 26.1 us -> 18.8 us  [per_device(): pl.pallas_call(functools.partial(chain_kernel, axes, block_count), out_sh...]
    ppermute x2, waiting for transfers between devices: 8.05 us -> 3.27 us  [along_chips(): lax.ppermute(values, axes, [(i, j) for i, j in route if 0 <= j < count])]
    ppermute x1, starting transfers between devices: 0.38 us -> 3.66 us  [per_device(): other = lax.ppermute(mine, axes, cores)]
    all_to_all x1, starting transfers between devices: 19.6 us -> 16.5 us  [per_device(): moments = lax.all_to_all(moments, axes, 0, 0, tiled=True)]
    ppermute x1, waiting for transfers between devices: 0.9 us -> 0.01 us  [per_device(): other = lax.ppermute(mine, axes, cores)]
  transfers between devices with their start and end apart: 5 -> 5, of which waited for: 5 -> 3; matrix products, arithmetic and copies ran while one was open for 0% -> 0% of each run, Pallas kernels for 12% -> 26%
where the time goes in v4:
time: 78.7 us; the launch traced here: 78.5 us
  Pallas kernels  42 us (53%)
  starting transfers between devices  26.1 us (33%)
  waiting for transfers between devices  7.39 us (9%)
  between operations  2.13 us (3%)
    pallas_call x1, Pallas kernels, per_device(): pl.pallas_call(functools.partial(chain_kernel, axes, block_count), out_sh...  18.8 us
    all_to_all x1, starting transfers between devices, per_device(): moments = lax.all_to_all(moments, axes, 0, 0, tiled=True)  16.5 us
    pallas_call x2, Pallas kernels, own_part(): pl.pallas_call(functools.partial(own_kernel, first, rows, first + rows ==...  10.8 us
    pallas_call x1, Pallas kernels, per_device(): pl.pallas_call(functools.partial(fluid_kernel, axes, fluid_count), out_sh...  9.67 us
    ppermute x1, starting transfers between devices, per_device(): other = lax.ppermute(mine, axes, cores)  3.66 us
    ppermute x1, starting transfers between devices, per_device(): partner = lax.ppermute(ends, axes, cores)  3.33 us
    ppermute x2, waiting for transfers between devices, along_chips(): lax.ppermute(values, axes, [(i, j) for i, j in route if 0 <= j < count])  3.27 us
    all_to_all x1, waiting for transfers between devices, per_device(): moments = lax.all_to_all(moments, axes, 0, 0, tiled=True)  3.23 us
  transfers between devices with their start and end apart: 5, of which 3 were waited for; matrix products, arithmetic and copies ran while one was open for 0% of the time, Pallas kernels for 26%

profile of v4, /device:TPU:1, one launch (start us, length us, event | category | flops | bytes accessed | tf_op | source)
XLA Modules:
  0.0 78.5 jit_solution(8267931120158321506)
XLA Ops:
  0.6 0.0 copy-start.2
  1.3 1.0 %shard_map.92.far_ref = f32[2,6,8,128]{3,2,1,0:T(8,128)S(1)} custom-call(s32[1]{0:T(128)S(6)} %copy.100.live_ref, f32[3,8192]{1,0:T(4,128)} %jitter_ref.9, f32[1,8192]{1,0:T(1,128)} %bitcast.170, f32[3,8192]{1,0:T(4,128)} %displacement_ref.7), custom_call_target="tpu_custom_call" | custom-call | tf_op jit(solution)/shard_map/pallas_call | solution.py:589
  2.4 3.3 %collective-permute-start.24 = (f32[2,6,8,128]{3,2,1,0:T(8,128)S(1)}, f32[2,6,8,128]{3,2,1,0:T(8,128)S(1)}, u32[]{:S(2)}, u32[]{:S(2)}) collective-permute-start(f32[2,6,8,128]{3,2,1,0:T(8,128)S(1)} %shard_map.92.far_ref), channel_id=1, source_target_pairs={{0,1},{1,0},{2,3},{3,2},{4,5},{5,4},{6,7},{7,6},{8,9},{9,8},{10,11... | collective-permute-start | bytes 147464 | tf_op jit(solution)/shard_map/ppermute | solution.py:608
  5.7 0.9 %collective-permute-done.24.near_ref.partner_ref = f32[2,6,8,128]{3,2,1,0:T(8,128)S(1)} collective-permute-done((f32[2,6,8,128]{3,2,1,0:T(8,128)S(1)}, f32[2,6,8,128]{3,2,1,0:T(8,128)S(1)}, u32[]{:S(2)}, u32[]{:S(2)}) %collective-permute-start.24) | collective-permute-done | bytes 49184 | tf_op jit(solution)/shard_map/ppermute | solution.py:608
  6.6 0.1 shard_map.93.near_ref
  6.7 1.3 %collective-permute-start.25 = (f32[6,8,128]{2,1,0:T(8,128)S(1)}, f32[6,8,128]{2,1,0:T(8,128)S(1)}, u32[]{:S(2)}, u32[]{:S(2)}) collective-permute-start(f32[6,8,128]{2,1,0:T(8,128)S(1)} %shard_map.93.near_ref), channel_id=1, source_target_pairs={{0,2},{2,4},{3,1},{4,6},{5,3},{6,8},{7,5},{8,10},{9,7},{10,12},{11... | collective-permute-start | bytes 73736 | tf_op jit(solution)/shard_map/ppermute | solution.py:574
  8.0 3.3 %collective-permute-done.25.far_ref.near_ref = f32[6,8,128]{2,1,0:T(8,128)S(1)} collective-permute-done((f32[6,8,128]{2,1,0:T(8,128)S(1)}, f32[6,8,128]{2,1,0:T(8,128)S(1)}, u32[]{:S(2)}, u32[]{:S(2)}) %collective-permute-start.25) | collective-permute-done | bytes 24608 | tf_op jit(solution)/shard_map/ppermute | solution.py:574
  11.3 0.1 shard_map.94
  11.4 1.3 %collective-permute-start.26 = (f32[6,8,128]{2,1,0:T(8,128)S(1)}, f32[6,8,128]{2,1,0:T(8,128)S(1)}, u32[]{:S(2)}, u32[]{:S(2)}) collective-permute-start(f32[6,8,128]{2,1,0:T(8,128)S(1)} %shard_map.94), channel_id=1, source_target_pairs={{0,4},{2,6},{4,8},{5,1},{6,10},{7,3},{8,12},{9,5},{10,14},{11,7},{... | collective-permute-start | bytes 73736 | tf_op jit(solution)/shard_map/ppermute | solution.py:574
  12.7 5.9 %shard_map.96.refs_0_ = bf16[74,384,256]{2,1,0:T(8,128)(2,1)S(1)} custom-call(f32[3,8192]{1,0:T(4,128)} %jitter_ref.9), custom_call_target="tpu_custom_call" | custom-call | flops 4000000000 | bytes 1000000 | tf_op jit(solution)/shard_map/pallas_call | solution.py:624
  18.6 0.0 collective-permute-done.26.far_ref
  18.6 0.1 shard_map.95.mine_ref
  18.8 0.0 copy-start
  18.8 0.0 copy-start.1
  18.8 3.7 %collective-permute-start.27 = (f32[6,8,128]{2,1,0:T(8,128)S(1)}, f32[6,8,128]{2,1,0:T(8,128)S(1)}, u32[]{:S(2)}, u32[]{:S(2)}) collective-permute-start(f32[6,8,128]{2,1,0:T(8,128)S(1)} %shard_map.95.mine_ref), channel_id=1, source_target_pairs={{0,1},{1,0},{2,3},{3,2},{4,5},{5,4},{6,7},{7,6},{8,9},{9,8},{10,11... | collective-permute-start | bytes 73736 | tf_op jit(solution)/shard_map/ppermute | solution.py:613
  22.4 0.0 copy-done.2
  22.4 4.9 %shard_map.97._ = bf16[74,384,256]{2,1,0:T(8,128)(2,1)S(1)} custom-call(f32[3,8192]{1,0:T(4,128)S(1)} %copy-done.2, bf16[74,384,256]{2,1,0:T(8,128)(2,1)S(1)} %shard_map.96.refs_0_), custom_call_target="tpu_custom_call", output_to_operand_aliasing={{}: (1, {})} | custom-call | flops 4000000000 | bytes 1000000 | tf_op jit(solution)/shard_map/pallas_call | solution.py:624
  27.4 0.0 copy-start.3
  27.4 0.0 collective-permute-done.27.other_ref
  27.4 0.0 copy-done
  27.4 0.0 copy-done.1
  27.4 18.8 %shard_map.98 = (f32[3,76,8,128]{3,2,1,0:T(8,128)S(1)}, f32[256,128]{1,0:T(8,128)}, bf16[74,384,256]{2,1,0:T(8,128)(2,1)S(1)}) custom-call(s32[1]{0:T(128)S(6)} %copy.100.live_ref, f32[3,8192]{1,0:T(4,128)S(1)} %copy-done.2, f32[1,8192]{1,0:T(1,128)S(1)} %bitcast.171, f32[3,8192]{1,0:T(4,128)S(1)} %copy-done, ...), custom_call_target="tpu_custom_call", output_to_operand_aliasing={{2}: (7, {})} | custom-call | tf_op jit(solution)/shard_map/pallas_call | solution.py:639
  46.2 16.5 %all-to-all-start = ((f32[256,1,128]{2,1,0:T(1,128)}), f32[256,1,128]{2,1,0:T(1,128)S(1)}, u32[]{:S(2)}, u32[]{:S(2)}) async-start(f32[256,1,128]{2,1,0:T(1,128)} %bitcast.53), calls=%async_computation | async-start | bytes 262144 | tf_op jit(solution)/shard_map/all_to_all | solution.py:654
  62.7 0.0 copy-done.3
  62.7 9.7 %shard_map.99.fluid_basis_ref = f32[24,3,8,128]{3,2,1,0:T(8,128)S(1)} custom-call(s32[1]{0:T(128)S(6)} %copy.100.live_ref, f32[3,8192]{1,0:T(4,128)S(1)} %copy-done.2, f32[1,8192]{1,0:T(1,128)S(1)} %bitcast.172, f32[3,8192]{1,0:T(4,128)S(1)} %copy-done, f32[3,3072]{1,0:T(4,128)S(1)} %copy-done.3, ...), custom_call_target="tpu_custom_call" | custom-call | flops 6000000000 | bytes 10000000 | tf_op jit(solution)/shard_map/pallas_call | solution.py:655
  72.4 3.2 %all-to-all-done = f32[256,1,128]{2,1,0:T(1,128)S(1)} async-done(((f32[256,1,128]{2,1,0:T(1,128)}), f32[256,1,128]{2,1,0:T(1,128)S(1)}, u32[]{:S(2)}, u32[]{:S(2)}) %all-to-all-start) | async-done | bytes 131104 | tf_op jit(solution)/shard_map/all_to_all | solution.py:654
  75.6 1.3 %shard_map.100 = (f32[3,8192]{1,0:T(4,128)}, f32[3,8192]{1,0:T(4,128)S(1)}, f32[3,3072]{1,0:T(4,128)}, s32[1]{0:T(128)}) custom-call(s32[1]{0:T(128)S(6)} %copy.100.live_ref, f32[256,128]{1,0:T(8,128)S(1)} %bitcast.168, f32[1,8192]{1,0:T(1,128)S(1)} %bitcast.173, f32[3,8192]{1,0:T(4,128)S(1)} %copy-done, f32[3,76,8,128]{3,2,1,0:T(8,128)S(1)} %get-tuple-element.426.basis_ref, ...), custom_call_target="tpu_custom_call" | custom-call | tf_op jit(solution)/shard_map/pallas_call | solution.py:669
  77.6 0.2 conditional.1
  77.8 0.0 copy-start.5
  77.8 0.6 copy-done.5
Async XLA Ops:
  0.6 21.8 %copy-start.2 = (f32[3,8192]{1,0:T(4,128)S(1)}, f32[3,8192]{1,0:T(4,128)}, u32[]{:S(2)}) copy-start(f32[3,8192]{1,0:T(4,128)} %jitter_ref.9) | copy-start | bytes 294916
  2.4 4.2 %collective-permute-start.24 = (f32[2,6,8,128]{3,2,1,0:T(8,128)S(1)}, f32[2,6,8,128]{3,2,1,0:T(8,128)S(1)}, u32[]{:S(2)}, u32[]{:S(2)}) collective-permute-start(f32[2,6,8,128]{3,2,1,0:T(8,128)S(1)} %shard_map.92.far_ref), channel_id=1, source_target_pairs={{0,1},{1,0},{2,3},{3,2},{4,5},{5,4},{6,7},{7,6},{8,9},{9,8},{10,11... | collective-permute-start | bytes 147464 | tf_op jit(solution)/shard_map/ppermute | solution.py:608
  6.7 4.6 %collective-permute-start.25 = (f32[6,8,128]{2,1,0:T(8,128)S(1)}, f32[6,8,128]{2,1,0:T(8,128)S(1)}, u32[]{:S(2)}, u32[]{:S(2)}) collective-permute-start(f32[6,8,128]{2,1,0:T(8,128)S(1)} %shard_map.93.near_ref), channel_id=1, source_target_pairs={{0,2},{2,4},{3,1},{4,6},{5,3},{6,8},{7,5},{8,10},{9,7},{10,12},{11... | collective-permute-start | bytes 73736 | tf_op jit(solution)/shard_map/ppermute | solution.py:574
  11.4 7.2 %collective-permute-start.26 = (f32[6,8,128]{2,1,0:T(8,128)S(1)}, f32[6,8,128]{2,1,0:T(8,128)S(1)}, u32[]{:S(2)}, u32[]{:S(2)}) collective-permute-start(f32[6,8,128]{2,1,0:T(8,128)S(1)} %shard_map.94), channel_id=1, source_target_pairs={{0,4},{2,6},{4,8},{5,1},{6,10},{7,3},{8,12},{9,5},{10,14},{11,7},{... | collective-permute-start | bytes 73736 | tf_op jit(solution)/shard_map/ppermute | solution.py:574
  18.8 8.6 %copy-start = (f32[3,8192]{1,0:T(4,128)S(1)}, f32[3,8192]{1,0:T(4,128)}, u32[]{:S(2)}) copy-start(f32[3,8192]{1,0:T(4,128)} %displacement_ref.7) | copy-start | bytes 294916
  18.8 8.6 %copy-start.1 = (f32[8192]{0:T(1024)S(1)}, f32[8192]{0:T(1024)}, u32[]{:S(2)}) copy-start(f32[8192]{0:T(1024)} %param.24) | copy-start | bytes 98308
  18.8 8.6 %collective-permute-start.27 = (f32[6,8,128]{2,1,0:T(8,128)S(1)}, f32[6,8,128]{2,1,0:T(8,128)S(1)}, u32[]{:S(2)}, u32[]{:S(2)}) collective-permute-start(f32[6,8,128]{2,1,0:T(8,128)S(1)} %shard_map.95.mine_ref), channel_id=1, source_target_pairs={{0,1},{1,0},{2,3},{3,2},{4,5},{5,4},{6,7},{7,6},{8,9},{9,8},{10,11... | collective-permute-start | bytes 73736 | tf_op jit(solution)/shard_map/ppermute | solution.py:613
  27.4 35.3 %copy-start.3 = (f32[3,3072]{1,0:T(4,128)S(1)}, f32[3,3072]{1,0:T(4,128)}, u32[]{:S(2)}) copy-start(f32[3,3072]{1,0:T(4,128)} %fluid_ref.1) | copy-start | bytes 110596
  46.2 29.4 %all-to-all-start = ((f32[256,1,128]{2,1,0:T(1,128)}), f32[256,1,128]{2,1,0:T(1,128)S(1)}, u32[]{:S(2)}, u32[]{:S(2)}) async-start(f32[256,1,128]{2,1,0:T(1,128)} %bitcast.53), calls=%async_computation | async-start | bytes 262144 | tf_op jit(solution)/shard_map/all_to_all | solution.py:654
  77.8 0.7 copy-start.5

commit v5 on v4

--- a/solution.py
+++ b/solution.py
@@ -38,7 +38,8 @@
     return jnp.max(row).astype(jnp.int32)
 
 
-def join_kernel(axes, end, near_ref, far_ref, joined_ref, buffer):
+def join_kernel(axes, end, near_ref, far_ref, *refs):
+    joined_ref, buffer = refs[-2:]
     core = lax.rem(lax.axis_index(axes), 2)
     near = near_ref[core] if end else near_ref[...]
     far = far_ref[core] if end else far_ref[...]
@@ -185,7 +186,8 @@
 
 
 def own_kernel(first, rows, last, jitter_ref, *refs):
-    matrix, source, target = refs[-3:]
+    matrix, mark_ref, source, target = refs[-4:]
+    mark_ref[...] = jnp.zeros_like(mark_ref)
 
     def prepare(block, carry):
         lanes = pl.ds(pl.multiple_of((first + block) * BLK, BLK), BLK)
@@ -594,28 +596,16 @@
         compiler_params=small,
     )(live_blocks, wing_jitter, smoothing_row, displacement)
 
-    def join(near, far, end=False):
+    def join(near, far, *after, end=False):
         return pl.pallas_call(
             functools.partial(join_kernel, axes, end),
             out_shape=floats(HALO, 8, BLK),
-            in_specs=[in_vmem] * 2,
+            in_specs=[in_vmem] * 2 + [pl.BlockSpec(memory_space=pl.ANY)] * len(after),
             out_specs=in_vmem,
             scratch_shapes=[pltpu.VMEM((3 * HALO, 8, BLK), jnp.float32)],
             compiler_params=small,
-        )(near, far)
-
-    cores = [(i, i ^ 1) for i in range(lax.axis_size(axes))]
-    partner = lax.ppermute(ends, axes, cores)
-    chip = join(partner, ends, end=True)
-    next_chip = along_chips(chip, axes, 1)
-    beyond = along_chips(join(chip, next_chip), axes, 2)
-    mine = join(next_chip, beyond)
-    other = lax.ppermute(mine, axes, cores)
-
-    vectors = pltpu.VMEM((width, 8, BLK), jnp.float32)
-    pairs = pltpu.VMEM((width, 16, BLK), jnp.bfloat16)
-    joined = pltpu.VMEM((2 * BASE + block_count, 8, BLK), jnp.float32)
-    source = pltpu.VMEM((width, BLK, PIECES), jnp.bfloat16)
+        )(near, far, *after)
+
     matrix_shape = jax.ShapeDtypeStruct((width - 2, 3 * BLK, 2 * BLK), jnp.bfloat16)
     own_rows = block_count - 2
     first_rows = block_count // 2
@@ -623,9 +613,9 @@
     def own_part(first, rows, *matrix):
         return pl.pallas_call(
             functools.partial(own_kernel, first, rows, first + rows == own_rows),
-            out_shape=matrix_shape,
+            out_shape=(matrix_shape, floats(8, BLK)),
             in_specs=[in_vmem] * (1 + len(matrix)),
-            out_specs=in_vmem,
+            out_specs=(in_vmem, in_vmem),
             input_output_aliases={1: 0} if matrix else {},
             scratch_shapes=[
                 pltpu.VMEM((rows + 2, BLK, PIECES), jnp.bfloat16),
@@ -635,7 +625,21 @@
             cost_estimate=pl.CostEstimate(flops=4 * 10**9, bytes_accessed=10**6, transcendentals=10**6),
         )(wing_jitter, *matrix)
 
-    matrix = own_part(first_rows, own_rows - first_rows, own_part(0, first_rows))
+    matrix, first_mark = own_part(0, first_rows)
+    matrix, second_mark = own_part(first_rows, own_rows - first_rows, matrix)
+
+    cores = [(i, i ^ 1) for i in range(lax.axis_size(axes))]
+    partner = lax.ppermute(ends, axes, cores)
+    chip = join(partner, ends, end=True)
+    next_chip = along_chips(chip, axes, 1)
+    beyond = along_chips(join(chip, next_chip, first_mark), axes, 2)
+    mine = join(next_chip, beyond, second_mark)
+    other = lax.ppermute(mine, axes, cores)
+
+    vectors = pltpu.VMEM((width, 8, BLK), jnp.float32)
+    pairs = pltpu.VMEM((width, 16, BLK), jnp.bfloat16)
+    joined = pltpu.VMEM((2 * BASE + block_count, 8, BLK), jnp.float32)
+    source = pltpu.VMEM((width, BLK, PIECES), jnp.bfloat16)
     basis, moments, _ = pl.pallas_call(
         functools.partial(chain_kernel, axes, block_count),
         out_shape=(floats(3, width, 8, BLK), floats(lax.axis_size(axes), BLK), matrix_shape),

time: 78.7 us -> 74 us (0.940)
  waiting for transfers between devices: 7.39 us -> 4.97 us
  starting transfers between devices: 26.1 us -> 23.8 us
    ppermute x2, waiting for transfers between devices: 3.27 us -> 0.01 us  [along_chips(): lax.ppermute(values, axes, [(i, j) for i, j in route if 0 <= j < count])]
    all_to_all x1, starting transfers between devices: 16.5 us -> 13.3 us  [per_device(): moments = lax.all_to_all(moments, axes, 0, 0, tiled=True)]
    ppermute x1, waiting for transfers between devices: 0.01 us -> 0.85 us  [per_device(): other = lax.ppermute(mine, axes, cores)]
  transfers between devices with their start and end apart: 5 -> 5, of which waited for: 3 -> 3; matrix products, arithmetic and copies ran while one was open for 0% -> 0% of each run, Pallas kernels for 26% -> 28%
where the time goes in v5:
time: 74 us; the launch traced here: 73.8 us
  Pallas kernels  42 us (57%)
  starting transfers between devices  23.8 us (32%)
  waiting for transfers between devices  4.97 us (7%)
  between operations  2.13 us (3%)
    pallas_call x1, Pallas kernels, per_device(): pl.pallas_call(functools.partial(chain_kernel, axes, block_count), out_sh...  18.8 us
    all_to_all x1, starting transfers between devices, per_device(): moments = lax.all_to_all(moments, axes, 0, 0, tiled=True)  13.3 us
    pallas_call x2, Pallas kernels, own_part(): pl.pallas_call(functools.partial(own_kernel, first, rows, first + rows ==...  10.8 us
    pallas_call x1, Pallas kernels, per_device(): pl.pallas_call(functools.partial(fluid_kernel, axes, fluid_count), out_sh...  9.67 us
    ppermute x1, starting transfers between devices, per_device(): other = lax.ppermute(mine, axes, cores)  4.4 us
    ppermute x1, starting transfers between devices, per_device(): partner = lax.ppermute(ends, axes, cores)  3.33 us
    all_to_all x1, waiting for transfers between devices, per_device(): moments = lax.all_to_all(moments, axes, 0, 0, tiled=True)  3.23 us
    ppermute x2, starting transfers between devices, along_chips(): lax.ppermute(values, axes, [(i, j) for i, j in route if 0 <= j < count])  2.72 us
  transfers between devices with their start and end apart: 5, of which 3 were waited for; matrix products, arithmetic and copies ran while one was open for 0% of the time, Pallas kernels for 28%

profile of v5, /device:TPU:1, one launch (start us, length us, event | category | flops | bytes accessed | tf_op | source)
XLA Modules:
  0.0 73.8 jit_solution(11486951441343908103)
XLA Ops:
  0.6 0.0 copy-start.2
  1.3 1.0 %shard_map.92.far_ref = f32[2,6,8,128]{3,2,1,0:T(8,128)S(1)} custom-call(s32[1]{0:T(128)S(6)} %copy.100.live_ref, f32[3,8192]{1,0:T(4,128)} %jitter_ref.9, f32[1,8192]{1,0:T(1,128)} %bitcast.170, f32[3,8192]{1,0:T(4,128)} %displacement_ref.7), custom_call_target="tpu_custom_call" | custom-call | tf_op jit(solution)/shard_map/pallas_call | solution.py:591
  2.4 3.3 %collective-permute-start.24 = (f32[2,6,8,128]{3,2,1,0:T(8,128)S(1)}, f32[2,6,8,128]{3,2,1,0:T(8,128)S(1)}, u32[]{:S(2)}, u32[]{:S(2)}) collective-permute-start(f32[2,6,8,128]{3,2,1,0:T(8,128)S(1)} %shard_map.92.far_ref), channel_id=1, source_target_pairs={{0,1},{1,0},{2,3},{3,2},{4,5},{5,4},{6,7},{7,6},{8,9},{9,8},{10,11... | collective-permute-start | bytes 147464 | tf_op jit(solution)/shard_map/ppermute | solution.py:632
  5.7 0.9 %collective-permute-done.24.near_ref.partner_ref = f32[2,6,8,128]{3,2,1,0:T(8,128)S(1)} collective-permute-done((f32[2,6,8,128]{3,2,1,0:T(8,128)S(1)}, f32[2,6,8,128]{3,2,1,0:T(8,128)S(1)}, u32[]{:S(2)}, u32[]{:S(2)}) %collective-permute-start.24) | collective-permute-done | bytes 49184 | tf_op jit(solution)/shard_map/ppermute | solution.py:632
  6.6 0.1 shard_map.93.near_ref
  6.7 0.0 copy-start
  6.7 0.0 copy-start.1
  6.7 1.4 %collective-permute-start.25 = (f32[6,8,128]{2,1,0:T(8,128)S(1)}, f32[6,8,128]{2,1,0:T(8,128)S(1)}, u32[]{:S(2)}, u32[]{:S(2)}) collective-permute-start(f32[6,8,128]{2,1,0:T(8,128)S(1)} %shard_map.93.near_ref), channel_id=1, source_target_pairs={{0,2},{2,4},{3,1},{4,6},{5,3},{6,8},{7,5},{8,10},{9,7},{10,12},{11... | collective-permute-start | bytes 73736 | tf_op jit(solution)/shard_map/ppermute | solution.py:576
  8.2 5.9 %shard_map.94 = (bf16[74,384,256]{2,1,0:T(8,128)(2,1)S(1)}, f32[8,128]{1,0:T(8,128)S(1)}) custom-call(f32[3,8192]{1,0:T(4,128)} %jitter_ref.9), custom_call_target="tpu_custom_call" | custom-call | flops 4000000000 | bytes 1000000 | tf_op jit(solution)/shard_map/pallas_call | solution.py:614
  14.1 0.0 collective-permute-done.25.far_ref.near_ref
  14.1 0.1 shard_map.95
  14.2 1.3 %collective-permute-start.26 = (f32[6,8,128]{2,1,0:T(8,128)S(1)}, f32[6,8,128]{2,1,0:T(8,128)S(1)}, u32[]{:S(2)}, u32[]{:S(2)}) collective-permute-start(f32[6,8,128]{2,1,0:T(8,128)S(1)} %shard_map.95), channel_id=1, source_target_pairs={{0,4},{2,6},{4,8},{5,1},{6,10},{7,3},{8,12},{9,5},{10,14},{11,7},{... | collective-permute-start | bytes 73736 | tf_op jit(solution)/shard_map/ppermute | solution.py:576
  15.5 0.0 copy-done.2
  15.5 0.0 copy-start.3
  15.5 4.9 %shard_map.96 = (bf16[74,384,256]{2,1,0:T(8,128)(2,1)S(1)}, f32[8,128]{1,0:T(8,128)S(1)}) custom-call(f32[3,8192]{1,0:T(4,128)S(1)} %copy-done.2, bf16[74,384,256]{2,1,0:T(8,128)(2,1)S(1)} %get-tuple-element.430.refs_0_), custom_call_target="tpu_custom_call", output_to_operand_aliasing={{0}: (1, {})} | custom-call | flops 4000000000 | bytes 1000000 | tf_op jit(solution)/shard_map/pallas_call | solution.py:614
  20.5 0.0 collective-permute-done.26.far_ref
  20.5 0.1 shard_map.97.mine_ref
  20.6 4.4 %collective-permute-start.27 = (f32[6,8,128]{2,1,0:T(8,128)S(1)}, f32[6,8,128]{2,1,0:T(8,128)S(1)}, u32[]{:S(2)}, u32[]{:S(2)}) collective-permute-start(f32[6,8,128]{2,1,0:T(8,128)S(1)} %shard_map.97.mine_ref), channel_id=1, source_target_pairs={{0,1},{1,0},{2,3},{3,2},{4,5},{5,4},{6,7},{7,6},{8,9},{9,8},{10,11... | collective-permute-start | bytes 73736 | tf_op jit(solution)/shard_map/ppermute | solution.py:637
  25.0 0.8 %collective-permute-done.27.other_ref = f32[6,8,128]{2,1,0:T(8,128)S(1)} collective-permute-done((f32[6,8,128]{2,1,0:T(8,128)S(1)}, f32[6,8,128]{2,1,0:T(8,128)S(1)}, u32[]{:S(2)}, u32[]{:S(2)}) %collective-permute-start.27) | collective-permute-done | bytes 24608 | tf_op jit(solution)/shard_map/ppermute | solution.py:637
  25.9 0.0 copy-done
  25.9 0.0 copy-done.1
  25.9 18.8 %shard_map.98 = (f32[3,76,8,128]{3,2,1,0:T(8,128)S(1)}, f32[256,128]{1,0:T(8,128)}, bf16[74,384,256]{2,1,0:T(8,128)(2,1)S(1)}) custom-call(s32[1]{0:T(128)S(6)} %copy.100.live_ref, f32[3,8192]{1,0:T(4,128)S(1)} %copy-done.2, f32[1,8192]{1,0:T(1,128)S(1)} %bitcast.171, f32[3,8192]{1,0:T(4,128)S(1)} %copy-done, ...), custom_call_target="tpu_custom_call", output_to_operand_aliasing={{2}: (7, {})} | custom-call | tf_op jit(solution)/shard_map/pallas_call | solution.py:643
  44.7 13.3 %all-to-all-start = ((f32[256,1,128]{2,1,0:T(1,128)}), f32[256,1,128]{2,1,0:T(1,128)S(1)}, u32[]{:S(2)}, u32[]{:S(2)}) async-start(f32[256,1,128]{2,1,0:T(1,128)} %bitcast.53), calls=%async_computation | async-start | bytes 262144 | tf_op jit(solution)/shard_map/all_to_all | solution.py:658
  58.0 0.0 copy-done.3
  58.0 9.7 %shard_map.99.fluid_basis_ref = f32[24,3,8,128]{3,2,1,0:T(8,128)S(1)} custom-call(s32[1]{0:T(128)S(6)} %copy.100.live_ref, f32[3,8192]{1,0:T(4,128)S(1)} %copy-done.2, f32[1,8192]{1,0:T(1,128)S(1)} %bitcast.172, f32[3,8192]{1,0:T(4,128)S(1)} %copy-done, f32[3,3072]{1,0:T(4,128)S(1)} %copy-done.3, ...), custom_call_target="tpu_custom_call" | custom-call | flops 6000000000 | bytes 10000000 | tf_op jit(solution)/shard_map/pallas_call | solution.py:659
  67.7 3.2 %all-to-all-done = f32[256,1,128]{2,1,0:T(1,128)S(1)} async-done(((f32[256,1,128]{2,1,0:T(1,128)}), f32[256,1,128]{2,1,0:T(1,128)S(1)}, u32[]{:S(2)}, u32[]{:S(2)}) %all-to-all-start) | async-done | bytes 131104 | tf_op jit(solution)/shard_map/all_to_all | solution.py:658
  70.9 1.3 %shard_map.100 = (f32[3,8192]{1,0:T(4,128)}, f32[3,8192]{1,0:T(4,128)S(1)}, f32[3,3072]{1,0:T(4,128)}, s32[1]{0:T(128)}) custom-call(s32[1]{0:T(128)S(6)} %copy.100.live_ref, f32[256,128]{1,0:T(8,128)S(1)} %bitcast.168, f32[1,8192]{1,0:T(1,128)S(1)} %bitcast.173, f32[3,8192]{1,0:T(4,128)S(1)} %copy-done, f32[3,76,8,128]{3,2,1,0:T(8,128)S(1)} %get-tuple-element.434.basis_ref, ...), custom_call_target="tpu_custom_call" | custom-call | tf_op jit(solution)/shard_map/pallas_call | solution.py:673
  72.9 0.2 conditional.1
  73.1 0.0 copy-start.5
  73.1 0.6 copy-done.5
Async XLA Ops:
  0.6 14.9 %copy-start.2 = (f32[3,8192]{1,0:T(4,128)S(1)}, f32[3,8192]{1,0:T(4,128)}, u32[]{:S(2)}) copy-start(f32[3,8192]{1,0:T(4,128)} %jitter_ref.9) | copy-start | bytes 294916
  2.4 4.2 %collective-permute-start.24 = (f32[2,6,8,128]{3,2,1,0:T(8,128)S(1)}, f32[2,6,8,128]{3,2,1,0:T(8,128)S(1)}, u32[]{:S(2)}, u32[]{:S(2)}) collective-permute-start(f32[2,6,8,128]{3,2,1,0:T(8,128)S(1)} %shard_map.92.far_ref), channel_id=1, source_target_pairs={{0,1},{1,0},{2,3},{3,2},{4,5},{5,4},{6,7},{7,6},{8,9},{9,8},{10,11... | collective-permute-start | bytes 147464 | tf_op jit(solution)/shard_map/ppermute | solution.py:632
  6.7 19.2 %copy-start = (f32[3,8192]{1,0:T(4,128)S(1)}, f32[3,8192]{1,0:T(4,128)}, u32[]{:S(2)}) copy-start(f32[3,8192]{1,0:T(4,128)} %displacement_ref.7) | copy-start | bytes 294916
  6.7 19.2 %copy-start.1 = (f32[8192]{0:T(1024)S(1)}, f32[8192]{0:T(1024)}, u32[]{:S(2)}) copy-start(f32[8192]{0:T(1024)} %param.24) | copy-start | bytes 98308
  6.7 7.3 %collective-permute-start.25 = (f32[6,8,128]{2,1,0:T(8,128)S(1)}, f32[6,8,128]{2,1,0:T(8,128)S(1)}, u32[]{:S(2)}, u32[]{:S(2)}) collective-permute-start(f32[6,8,128]{2,1,0:T(8,128)S(1)} %shard_map.93.near_ref), channel_id=1, source_target_pairs={{0,2},{2,4},{3,1},{4,6},{5,3},{6,8},{7,5},{8,10},{9,7},{10,12},{11... | collective-permute-start | bytes 73736 | tf_op jit(solution)/shard_map/ppermute | solution.py:576
  14.2 6.2 %collective-permute-start.26 = (f32[6,8,128]{2,1,0:T(8,128)S(1)}, f32[6,8,128]{2,1,0:T(8,128)S(1)}, u32[]{:S(2)}, u32[]{:S(2)}) collective-permute-start(f32[6,8,128]{2,1,0:T(8,128)S(1)} %shard_map.95), channel_id=1, source_target_pairs={{0,4},{2,6},{4,8},{5,1},{6,10},{7,3},{8,12},{9,5},{10,14},{11,7},{... | collective-permute-start | bytes 73736 | tf_op jit(solution)/shard_map/ppermute | solution.py:576
  15.5 42.5 %copy-start.3 = (f32[3,3072]{1,0:T(4,128)S(1)}, f32[3,3072]{1,0:T(4,128)}, u32[]{:S(2)}) copy-start(f32[3,3072]{1,0:T(4,128)} %fluid_ref.1) | copy-start | bytes 110596
  20.6 5.2 %collective-permute-start.27 = (f32[6,8,128]{2,1,0:T(8,128)S(1)}, f32[6,8,128]{2,1,0:T(8,128)S(1)}, u32[]{:S(2)}, u32[]{:S(2)}) collective-permute-start(f32[6,8,128]{2,1,0:T(8,128)S(1)} %shard_map.97.mine_ref), channel_id=1, source_target_pairs={{0,1},{1,0},{2,3},{3,2},{4,5},{5,4},{6,7},{7,6},{8,9},{9,8},{10,11... | collective-permute-start | bytes 73736 | tf_op jit(solution)/shard_map/ppermute | solution.py:637
  44.7 26.3 %all-to-all-start = ((f32[256,1,128]{2,1,0:T(1,128)}), f32[256,1,128]{2,1,0:T(1,128)S(1)}, u32[]{:S(2)}, u32[]{:S(2)}) async-start(f32[256,1,128]{2,1,0:T(1,128)} %bitcast.53), calls=%async_computation | async-start | bytes 262144 | tf_op jit(solution)/shard_map/all_to_all | solution.py:658
  73.1 0.7 copy-start.5

commit v6 on v5

--- a/solution.py
+++ b/solution.py
@@ -642,7 +642,7 @@
     source = pltpu.VMEM((width, BLK, PIECES), jnp.bfloat16)
     basis, moments, _ = pl.pallas_call(
         functools.partial(chain_kernel, axes, block_count),
-        out_shape=(floats(3, width, 8, BLK), floats(lax.axis_size(axes), BLK), matrix_shape),
+        out_shape=(floats(3, width, 8, BLK), floats(8, BLK), matrix_shape),
         in_specs=[in_smem] + [in_vmem] * 7,
         out_specs=(in_vmem,) * 3,
         input_output_aliases={7: 2},
@@ -655,7 +655,16 @@
         ],
         compiler_params=pltpu.CompilerParams(vmem_limit_bytes=12 * 2**20),
     )(live_blocks, wing_jitter, smoothing_row, displacement, partner, mine, other, matrix)
-    moments = lax.all_to_all(moments, axes, 0, 0, tiled=True)
+    moments = moments + lax.ppermute(moments, axes, cores)
+    chips = lax.axis_size(axes) // 2
+    moments = lax.all_to_all(
+        jnp.broadcast_to(moments[0:1], (chips, BLK)),
+        axes,
+        0,
+        0,
+        axis_index_groups=[[2 * chip + core for chip in range(chips)] for core in range(2)],
+        tiled=True,
+    )
     fluid_basis = pl.pallas_call(
         functools.partial(fluid_kernel, axes, fluid_count),
         out_shape=floats(fluid_count, 3, 8, BLK),

time: 74 us -> 74 us (level)
  waiting for transfers between devices: 4.97 us -> 3.55 us
  starting transfers between devices: 23.8 us -> 25.2 us
    all_to_all x1, waiting for transfers between devices: 3.23 us -> 0.99 us  [per_device(): lax.all_to_all(jnp.broadcast_to(moments[0:1], (chips, BLK)), axes, 0, 0,...]
    all_to_all x1, starting transfers between devices: 13.3 us -> 14.3 us  [per_device(): lax.all_to_all(jnp.broadcast_to(moments[0:1], (chips, BLK)), axes, 0, 0,...]
    ppermute x0 -> x1, waiting for transfers between devices: none -> 0.82 us  [per_device(): moments = moments + lax.ppermute(moments, axes, cores)]
  transfers between devices with their start and end apart: 5 -> 6, of which waited for: 3 -> 4; matrix products, arithmetic and copies ran while one was open for 0% -> 0% of each run, Pallas kernels for 28% -> 28%
where the time goes in v6:
time: 74 us; the launch traced here: 73.8 us
  Pallas kernels  41.3 us (56%)
  starting transfers between devices  25.2 us (34%)
  waiting for transfers between devices  3.55 us (5%)
  between operations  2.13 us (3%)
  local copies, waits for them, and re-layouts  1.35 us (2%)
    pallas_call x1, Pallas kernels, per_device(): pl.pallas_call(functools.partial(chain_kernel, axes, block_count), out_sh...  18.1 us
    all_to_all x1, starting transfers between devices, per_device(): lax.all_to_all(jnp.broadcast_to(moments[0:1], (chips, BLK)), axes, 0, 0,...  14.3 us
    pallas_call x2, Pallas kernels, own_part(): pl.pallas_call(functools.partial(own_kernel, first, rows, first + rows ==...  10.8 us
    pallas_call x1, Pallas kernels, per_device(): pl.pallas_call(functools.partial(fluid_kernel, axes, fluid_count), out_sh...  9.66 us
    ppermute x1, starting transfers between devices, per_device(): other = lax.ppermute(mine, axes, cores)  4.38 us
    ppermute x1, starting transfers between devices, per_device(): partner = lax.ppermute(ends, axes, cores)  3.33 us
    ppermute x2, starting transfers between devices, along_chips(): lax.ppermute(values, axes, [(i, j) for i, j in route if 0 <= j < count])  2.72 us
  transfers between devices with their start and end apart: 6, of which 4 were waited for; matrix products, arithmetic and copies ran while one was open for 0% of the time, Pallas kernels for 28%

profile of v6, /device:TPU:1, one launch (start us, length us, event | category | flops | bytes accessed | tf_op | source)
XLA Modules:
  0.0 73.8 jit_solution(72133077096723315)
XLA Ops:
  0.6 0.0 copy-start.2
  1.3 1.0 %shard_map.92.far_ref = f32[2,6,8,128]{3,2,1,0:T(8,128)S(1)} custom-call(s32[1]{0:T(128)S(6)} %copy.99.live_ref, f32[3,8192]{1,0:T(4,128)} %jitter_ref.9, f32[1,8192]{1,0:T(1,128)} %bitcast.169, f32[3,8192]{1,0:T(4,128)} %displacement_ref.7), custom_call_target="tpu_custom_call" | custom-call | tf_op jit(solution)/shard_map/pallas_call | solution.py:591
  2.4 3.3 %collective-permute-start.24 = (f32[2,6,8,128]{3,2,1,0:T(8,128)S(1)}, f32[2,6,8,128]{3,2,1,0:T(8,128)S(1)}, u32[]{:S(2)}, u32[]{:S(2)}) collective-permute-start(f32[2,6,8,128]{3,2,1,0:T(8,128)S(1)} %shard_map.92.far_ref), channel_id=1, source_target_pairs={{0,1},{1,0},{2,3},{3,2},{4,5},{5,4},{6,7},{7,6},{8,9},{9,8},{10,11... | collective-permute-start | bytes 147464 | tf_op jit(solution)/shard_map/ppermute | solution.py:632
  5.7 0.9 %collective-permute-done.24.near_ref.partner_ref = f32[2,6,8,128]{3,2,1,0:T(8,128)S(1)} collective-permute-done((f32[2,6,8,128]{3,2,1,0:T(8,128)S(1)}, f32[2,6,8,128]{3,2,1,0:T(8,128)S(1)}, u32[]{:S(2)}, u32[]{:S(2)}) %collective-permute-start.24) | collective-permute-done | bytes 49184 | tf_op jit(solution)/shard_map/ppermute | solution.py:632
  6.6 0.1 shard_map.93.near_ref
  6.7 0.0 copy-start
  6.7 0.0 copy-start.1
  6.7 1.4 %collective-permute-start.25 = (f32[6,8,128]{2,1,0:T(8,128)S(1)}, f32[6,8,128]{2,1,0:T(8,128)S(1)}, u32[]{:S(2)}, u32[]{:S(2)}) collective-permute-start(f32[6,8,128]{2,1,0:T(8,128)S(1)} %shard_map.93.near_ref), channel_id=1, source_target_pairs={{0,2},{2,4},{3,1},{4,6},{5,3},{6,8},{7,5},{8,10},{9,7},{10,12},{11... | collective-permute-start | bytes 73736 | tf_op jit(solution)/shard_map/ppermute | solution.py:576
  8.2 5.9 %shard_map.94 = (bf16[74,384,256]{2,1,0:T(8,128)(2,1)S(1)}, f32[8,128]{1,0:T(8,128)S(1)}) custom-call(f32[3,8192]{1,0:T(4,128)} %jitter_ref.9), custom_call_target="tpu_custom_call" | custom-call | flops 4000000000 | bytes 1000000 | tf_op jit(solution)/shard_map/pallas_call | solution.py:614
  14.1 0.0 collective-permute-done.25.far_ref.near_ref
  14.1 0.1 shard_map.95
  14.2 1.3 %collective-permute-start.26 = (f32[6,8,128]{2,1,0:T(8,128)S(1)}, f32[6,8,128]{2,1,0:T(8,128)S(1)}, u32[]{:S(2)}, u32[]{:S(2)}) collective-permute-start(f32[6,8,128]{2,1,0:T(8,128)S(1)} %shard_map.95), channel_id=1, source_target_pairs={{0,4},{2,6},{4,8},{5,1},{6,10},{7,3},{8,12},{9,5},{10,14},{11,7},{... | collective-permute-start | bytes 73736 | tf_op jit(solution)/shard_map/ppermute | solution.py:576
  15.5 0.0 copy-done.2
  15.5 0.0 copy-start.3
  15.5 4.9 %shard_map.96 = (bf16[74,384,256]{2,1,0:T(8,128)(2,1)S(1)}, f32[8,128]{1,0:T(8,128)S(1)}) custom-call(f32[3,8192]{1,0:T(4,128)S(1)} %copy-done.2, bf16[74,384,256]{2,1,0:T(8,128)(2,1)S(1)} %get-tuple-element.430.refs_0_), custom_call_target="tpu_custom_call", output_to_operand_aliasing={{0}: (1, {})} | custom-call | flops 4000000000 | bytes 1000000 | tf_op jit(solution)/shard_map/pallas_call | solution.py:614
  20.5 0.0 collective-permute-done.26.far_ref
  20.5 0.1 shard_map.97.mine_ref
  20.6 4.4 %collective-permute-start.27 = (f32[6,8,128]{2,1,0:T(8,128)S(1)}, f32[6,8,128]{2,1,0:T(8,128)S(1)}, u32[]{:S(2)}, u32[]{:S(2)}) collective-permute-start(f32[6,8,128]{2,1,0:T(8,128)S(1)} %shard_map.97.mine_ref), channel_id=1, source_target_pairs={{0,1},{1,0},{2,3},{3,2},{4,5},{5,4},{6,7},{7,6},{8,9},{9,8},{10,11... | collective-permute-start | bytes 73736 | tf_op jit(solution)/shard_map/ppermute | solution.py:637
  25.0 0.8 %collective-permute-done.27.other_ref = f32[6,8,128]{2,1,0:T(8,128)S(1)} collective-permute-done((f32[6,8,128]{2,1,0:T(8,128)S(1)}, f32[6,8,128]{2,1,0:T(8,128)S(1)}, u32[]{:S(2)}, u32[]{:S(2)}) %collective-permute-start.27) | collective-permute-done | bytes 24608 | tf_op jit(solution)/shard_map/ppermute | solution.py:637
  25.9 0.0 copy-done
  25.9 0.0 copy-done.1
  25.9 18.1 %shard_map.98 = (f32[3,76,8,128]{3,2,1,0:T(8,128)S(1)}, f32[8,128]{1,0:T(8,128)S(1)}, bf16[74,384,256]{2,1,0:T(8,128)(2,1)S(1)}) custom-call(s32[1]{0:T(128)S(6)} %copy.99.live_ref, f32[3,8192]{1,0:T(4,128)S(1)} %copy-done.2, f32[1,8192]{1,0:T(1,128)S(1)} %bitcast.170, f32[3,8192]{1,0:T(4,128)S(1)} %copy-done, ...), custom_call_target="tpu_custom_call", output_to_operand_aliasing={{2}: (7, {})} | custom-call | tf_op jit(solution)/shard_map/pallas_call | solution.py:643
  44.0 0.4 collective-permute-start.28
  44.4 0.8 %collective-permute-done.28 = f32[8,128]{1,0:T(8,128)S(1)} collective-permute-done((f32[8,128]{1,0:T(8,128)S(1)}, f32[8,128]{1,0:T(8,128)S(1)}, u32[]{:S(2)}, u32[]{:S(2)}) %collective-permute-start.28) | collective-permute-done | bytes 4128 | tf_op jit(solution)/shard_map/ppermute | solution.py:658
  45.3 0.7 broadcast_in_dim.37
  45.9 14.3 %all-to-all-start = ((f32[128,1,128]{2,1,0:T(1,128)}), f32[128,1,128]{2,1,0:T(1,128)S(1)}, u32[]{:S(2)}, u32[]{:S(2)}) async-start(f32[128,1,128]{2,1,0:T(1,128)} %broadcast_in_dim.37), calls=%async_computation | async-start | bytes 131072 | tf_op jit(solution)/shard_map/all_to_all | solution.py:660
  60.3 9.7 %shard_map.99.fluid_basis_ref = f32[24,3,8,128]{3,2,1,0:T(8,128)S(1)} custom-call(s32[1]{0:T(128)S(6)} %copy.99.live_ref, f32[3,8192]{1,0:T(4,128)S(1)} %copy-done.2, f32[1,8192]{1,0:T(1,128)S(1)} %bitcast.171, f32[3,8192]{1,0:T(4,128)S(1)} %copy-done, f32[3,3072]{1,0:T(4,128)S(1)} %copy-done.3, ...), custom_call_target="tpu_custom_call" | custom-call | flops 6000000000 | bytes 10000000 | tf_op jit(solution)/shard_map/pallas_call | solution.py:668
  69.9 1.0 %all-to-all-done = f32[128,1,128]{2,1,0:T(1,128)S(1)} async-done(((f32[128,1,128]{2,1,0:T(1,128)}), f32[128,1,128]{2,1,0:T(1,128)S(1)}, u32[]{:S(2)}, u32[]{:S(2)}) %all-to-all-start) | async-done | bytes 65568 | tf_op jit(solution)/shard_map/all_to_all | solution.py:660
  70.9 1.3 %shard_map.100 = (f32[3,8192]{1,0:T(4,128)}, f32[3,8192]{1,0:T(4,128)S(1)}, f32[3,3072]{1,0:T(4,128)}, s32[1]{0:T(128)}) custom-call(s32[1]{0:T(128)S(6)} %copy.99.live_ref, f32[128,128]{1,0:T(8,128)S(1)} %bitcast.167, f32[1,8192]{1,0:T(1,128)S(1)} %bitcast.172, f32[3,8192]{1,0:T(4,128)S(1)} %copy-done, f32[3,76,8,128]{3,2,1,0:T(8,128)S(1)} %get-tuple-element.434.basis_ref, ...), custom_call_target="tpu_custom_call" | custom-call | tf_op jit(solution)/shard_map/pallas_call | solution.py:682
  72.9 0.2 conditional.1
  73.1 0.0 copy-start.5
  73.1 0.6 copy-done.5
  (3 shorter events, 0.0 us)
Async XLA Ops:
  0.6 14.9 %copy-start.2 = (f32[3,8192]{1,0:T(4,128)S(1)}, f32[3,8192]{1,0:T(4,128)}, u32[]{:S(2)}) copy-start(f32[3,8192]{1,0:T(4,128)} %jitter_ref.9) | copy-start | bytes 294916
  2.4 4.2 %collective-permute-start.24 = (f32[2,6,8,128]{3,2,1,0:T(8,128)S(1)}, f32[2,6,8,128]{3,2,1,0:T(8,128)S(1)}, u32[]{:S(2)}, u32[]{:S(2)}) collective-permute-start(f32[2,6,8,128]{3,2,1,0:T(8,128)S(1)} %shard_map.92.far_ref), channel_id=1, source_target_pairs={{0,1},{1,0},{2,3},{3,2},{4,5},{5,4},{6,7},{7,6},{8,9},{9,8},{10,11... | collective-permute-start | bytes 147464 | tf_op jit(solution)/shard_map/ppermute | solution.py:632
  6.7 19.2 %copy-start = (f32[3,8192]{1,0:T(4,128)S(1)}, f32[3,8192]{1,0:T(4,128)}, u32[]{:S(2)}) copy-start(f32[3,8192]{1,0:T(4,128)} %displacement_ref.7) | copy-start | bytes 294916
  6.7 19.2 %copy-start.1 = (f32[8192]{0:T(1024)S(1)}, f32[8192]{0:T(1024)}, u32[]{:S(2)}) copy-start(f32[8192]{0:T(1024)} %param.24) | copy-start | bytes 98308
  6.7 7.4 %collective-permute-start.25 = (f32[6,8,128]{2,1,0:T(8,128)S(1)}, f32[6,8,128]{2,1,0:T(8,128)S(1)}, u32[]{:S(2)}, u32[]{:S(2)}) collective-permute-start(f32[6,8,128]{2,1,0:T(8,128)S(1)} %shard_map.93.near_ref), channel_id=1, source_target_pairs={{0,2},{2,4},{3,1},{4,6},{5,3},{6,8},{7,5},{8,10},{9,7},{10,12},{11... | collective-permute-start | bytes 73736 | tf_op jit(solution)/shard_map/ppermute | solution.py:576
  14.2 6.3 %collective-permute-start.26 = (f32[6,8,128]{2,1,0:T(8,128)S(1)}, f32[6,8,128]{2,1,0:T(8,128)S(1)}, u32[]{:S(2)}, u32[]{:S(2)}) collective-permute-start(f32[6,8,128]{2,1,0:T(8,128)S(1)} %shard_map.95), channel_id=1, source_target_pairs={{0,4},{2,6},{4,8},{5,1},{6,10},{7,3},{8,12},{9,5},{10,14},{11,7},{... | collective-permute-start | bytes 73736 | tf_op jit(solution)/shard_map/ppermute | solution.py:576
  15.5 44.7 %copy-start.3 = (f32[3,3072]{1,0:T(4,128)S(1)}, f32[3,3072]{1,0:T(4,128)}, u32[]{:S(2)}) copy-start(f32[3,3072]{1,0:T(4,128)} %fluid_ref.1) | copy-start | bytes 110596
  20.6 5.2 %collective-permute-start.27 = (f32[6,8,128]{2,1,0:T(8,128)S(1)}, f32[6,8,128]{2,1,0:T(8,128)S(1)}, u32[]{:S(2)}, u32[]{:S(2)}) collective-permute-start(f32[6,8,128]{2,1,0:T(8,128)S(1)} %shard_map.97.mine_ref), channel_id=1, source_target_pairs={{0,1},{1,0},{2,3},{3,2},{4,5},{5,4},{6,7},{7,6},{8,9},{9,8},{10,11... | collective-permute-start | bytes 73736 | tf_op jit(solution)/shard_map/ppermute | solution.py:637
  44.0 1.3 %collective-permute-start.28 = (f32[8,128]{1,0:T(8,128)S(1)}, f32[8,128]{1,0:T(8,128)S(1)}, u32[]{:S(2)}, u32[]{:S(2)}) collective-permute-start(f32[8,128]{1,0:T(8,128)S(1)} %get-tuple-element.433), channel_id=1, source_target_pairs={{0,1},{1,0},{2,3},{3,2},{4,5},{5,4},{6,7},{7,6},{8,9},{9,8},{10,11... | collective-permute-start | bytes 12296 | tf_op jit(solution)/shard_map/ppermute | solution.py:658
  45.9 25.0 %all-to-all-start = ((f32[128,1,128]{2,1,0:T(1,128)}), f32[128,1,128]{2,1,0:T(1,128)S(1)}, u32[]{:S(2)}, u32[]{:S(2)}) async-start(f32[128,1,128]{2,1,0:T(1,128)} %broadcast_in_dim.37), calls=%async_computation | async-start | bytes 131072 | tf_op jit(solution)/shard_map/all_to_all | solution.py:660
  73.1 0.7 copy-start.5

commit v7 on v6

--- a/solution.py
+++ b/solution.py
@@ -186,8 +186,7 @@
 
 
 def own_kernel(first, rows, last, jitter_ref, *refs):
-    matrix, mark_ref, source, target = refs[-4:]
-    mark_ref[...] = jnp.zeros_like(mark_ref)
+    matrix, source, target = refs[-3:]
 
     def prepare(block, carry):
         lanes = pl.ds(pl.multiple_of((first + block) * BLK, BLK), BLK)
@@ -311,7 +310,7 @@
 def fluid_kernel(
     axes, fluid_count,
     live_ref, jitter_ref, smoothing_ref, displacement_ref, fluid_ref, partner_ref, mine_ref, other_ref,
-    basis_ref,
+    basis_ref, first_source, second_source,
     fluid_basis_ref,
     joined, source, b0, b1, b2, matrix,
 ):
@@ -322,14 +321,24 @@
     )
 
     def prepare(block, carry):
-        points, norm, scale, rhs = parts_of(joined[BASE - HALO + block])
-        source[block] = source_of(points, norm)
+        _, _, scale, rhs = parts_of(joined[BASE - HALO + block])
         b0[block] = vector_pair(rhs * scale)
         b1[block] = vector_pair(basis_ref[0, block] * scale)
         b2[block] = vector_pair(basis_ref[1, block] * scale)
         return carry
 
     lax.fori_loop(HALO - 2, width - HALO + 2, prepare, 0, unroll=4)
+    half = first_source.shape[0] - 2
+
+    def put_source(block, carry):
+        source[HALO + block] = first_source[block]
+        source[HALO + half + block] = second_source[block]
+        return carry
+
+    lax.fori_loop(0, half, put_source, 0, unroll=4)
+    for block in (HALO - 2, HALO - 1, HALO + live, HALO + live + 1):
+        points, norm, _, _ = parts_of(joined[BASE - HALO + block])
+        source[block] = source_of(points, norm)
 
     def anchor_of(index):
         return lax.div(index * live, jnp.int32(fluid_count))
@@ -613,27 +622,24 @@
     def own_part(first, rows, *matrix):
         return pl.pallas_call(
             functools.partial(own_kernel, first, rows, first + rows == own_rows),
-            out_shape=(matrix_shape, floats(8, BLK)),
+            out_shape=(matrix_shape, jax.ShapeDtypeStruct((rows + 2, BLK, PIECES), jnp.bfloat16)),
             in_specs=[in_vmem] * (1 + len(matrix)),
             out_specs=(in_vmem, in_vmem),
             input_output_aliases={1: 0} if matrix else {},
-            scratch_shapes=[
-                pltpu.VMEM((rows + 2, BLK, PIECES), jnp.bfloat16),
-                pltpu.VMEM((rows + 2, 8, BLK), jnp.float32),
-            ],
+            scratch_shapes=[pltpu.VMEM((rows + 2, 8, BLK), jnp.float32)],
             compiler_params=small,
             cost_estimate=pl.CostEstimate(flops=4 * 10**9, bytes_accessed=10**6, transcendentals=10**6),
         )(wing_jitter, *matrix)
 
-    matrix, first_mark = own_part(0, first_rows)
-    matrix, second_mark = own_part(first_rows, own_rows - first_rows, matrix)
+    matrix, first_source = own_part(0, first_rows)
+    matrix, second_source = own_part(first_rows, own_rows - first_rows, matrix)
 
     cores = [(i, i ^ 1) for i in range(lax.axis_size(axes))]
     partner = lax.ppermute(ends, axes, cores)
     chip = join(partner, ends, end=True)
     next_chip = along_chips(chip, axes, 1)
-    beyond = along_chips(join(chip, next_chip, first_mark), axes, 2)
-    mine = join(next_chip, beyond, second_mark)
+    beyond = along_chips(join(chip, next_chip, first_source), axes, 2)
+    mine = join(next_chip, beyond, second_source)
     other = lax.ppermute(mine, axes, cores)
 
     vectors = pltpu.VMEM((width, 8, BLK), jnp.float32)
@@ -668,7 +674,7 @@
     fluid_basis = pl.pallas_call(
         functools.partial(fluid_kernel, axes, fluid_count),
         out_shape=floats(fluid_count, 3, 8, BLK),
-        in_specs=[in_smem] + [in_vmem] * 8,
+        in_specs=[in_smem] + [in_vmem] * 10,
         out_specs=in_vmem,
         scratch_shapes=[
             joined,
@@ -678,7 +684,8 @@
         ],
         compiler_params=pltpu.CompilerParams(vmem_limit_bytes=24 * 2**20),
         cost_estimate=pl.CostEstimate(flops=6 * 10**9, bytes_accessed=10**7, transcendentals=2 * 10**6),
-    )(live_blocks, wing_jitter, smoothing_row, displacement, fluid_jitter, partner, mine, other, basis)
+    )(live_blocks, wing_jitter, smoothing_row, displacement, fluid_jitter, partner, mine, other, basis,
+      first_source, second_source)
     coefs, residual, fluid_values, good = pl.pallas_call(
         functools.partial(finish_kernel, block_count, fluid_count),
         out_shape=(

time: 74 us -> 75 us (1.014)
    pallas_call x1, Pallas kernels: 1.28 us -> 2.2 us  [per_device(): pl.pallas_call(functools.partial(finish_kernel, block_count, fluid_count)...]
  transfers between devices with their start and end apart: 6 -> 6, of which waited for: 4 -> 4; matrix products, arithmetic and copies ran while one was open for 0% -> 0% of each run, Pallas kernels for 28% -> 27%
where the time goes in v7:
time: 75 us; the launch traced here: 74.7 us
  Pallas kernels  42 us (56%)
  starting transfers between devices  25.2 us (34%)
  waiting for transfers between devices  3.81 us (5%)
  between operations  2.11 us (3%)
  local copies, waits for them, and re-layouts  1.34 us (2%)
    pallas_call x1, Pallas kernels, per_device(): pl.pallas_call(functools.partial(chain_kernel, axes, block_count), out_sh...  18.1 us
    all_to_all x1, starting transfers between devices, per_device(): lax.all_to_all(jnp.broadcast_to(moments[0:1], (chips, BLK)), axes, 0, 0,...  14.3 us
    pallas_call x2, Pallas kernels, own_part(): pl.pallas_call(functools.partial(own_kernel, first, rows, first + rows ==...  10.8 us
    pallas_call x1, Pallas kernels, per_device(): pl.pallas_call(functools.partial(fluid_kernel, axes, fluid_count), out_sh...  9.41 us
    ppermute x1, starting transfers between devices, per_device(): other = lax.ppermute(mine, axes, cores)  4.4 us
    ppermute x1, starting transfers between devices, per_device(): partner = lax.ppermute(ends, axes, cores)  3.33 us
    ppermute x2, starting transfers between devices, along_chips(): lax.ppermute(values, axes, [(i, j) for i, j in route if 0 <= j < count])  2.72 us
    pallas_call x1, Pallas kernels, per_device(): pl.pallas_call(functools.partial(finish_kernel, block_count, fluid_count)...  2.2 us
  transfers between devices with their start and end apart: 6, of which 4 were waited for; matrix products, arithmetic and copies ran while one was open for 0% of the time, Pallas kernels for 27%

profile of v7, /device:TPU:1, one launch (start us, length us, event | category | flops | bytes accessed | tf_op | source)
XLA Modules:
  0.0 74.7 jit_solution(2452986606328904275)
XLA Ops:
  0.6 0.0 copy-start.4
  1.3 1.0 %shard_map.92.far_ref = f32[2,6,8,128]{3,2,1,0:T(8,128)S(1)} custom-call(s32[1]{0:T(128)S(6)} %copy.99.live_ref, f32[3,8192]{1,0:T(4,128)} %jitter_ref.9, f32[1,8192]{1,0:T(1,128)} %bitcast.169, f32[3,8192]{1,0:T(4,128)} %displacement_ref.7), custom_call_target="tpu_custom_call" | custom-call | tf_op jit(solution)/shard_map/pallas_call | solution.py:600
  2.4 3.3 %collective-permute-start.24 = (f32[2,6,8,128]{3,2,1,0:T(8,128)S(1)}, f32[2,6,8,128]{3,2,1,0:T(8,128)S(1)}, u32[]{:S(2)}, u32[]{:S(2)}) collective-permute-start(f32[2,6,8,128]{3,2,1,0:T(8,128)S(1)} %shard_map.92.far_ref), channel_id=1, source_target_pairs={{0,1},{1,0},{2,3},{3,2},{4,5},{5,4},{6,7},{7,6},{8,9},{9,8},{10,11... | collective-permute-start | bytes 147464 | tf_op jit(solution)/shard_map/ppermute | solution.py:638
  5.7 0.9 %collective-permute-done.24.near_ref.partner_ref = f32[2,6,8,128]{3,2,1,0:T(8,128)S(1)} collective-permute-done((f32[2,6,8,128]{3,2,1,0:T(8,128)S(1)}, f32[2,6,8,128]{3,2,1,0:T(8,128)S(1)}, u32[]{:S(2)}, u32[]{:S(2)}) %collective-permute-start.24) | collective-permute-done | bytes 49184 | tf_op jit(solution)/shard_map/ppermute | solution.py:638
  6.6 0.1 shard_map.93.near_ref
  6.7 0.0 copy-start
  6.7 0.0 copy-start.2
  6.7 1.4 %collective-permute-start.25 = (f32[6,8,128]{2,1,0:T(8,128)S(1)}, f32[6,8,128]{2,1,0:T(8,128)S(1)}, u32[]{:S(2)}, u32[]{:S(2)}) collective-permute-start(f32[6,8,128]{2,1,0:T(8,128)S(1)} %shard_map.93.near_ref), channel_id=1, source_target_pairs={{0,2},{2,4},{3,1},{4,6},{5,3},{6,8},{7,5},{8,10},{9,7},{10,12},{11... | collective-permute-start | bytes 73736 | tf_op jit(solution)/shard_map/ppermute | solution.py:585
  8.2 5.9 %shard_map.94 = (bf16[74,384,256]{2,1,0:T(8,128)(2,1)S(1)}, bf16[34,128,48]{2,1,0:T(8,128)(2,1)S(1)}) custom-call(f32[3,8192]{1,0:T(4,128)} %jitter_ref.9), custom_call_target="tpu_custom_call" | custom-call | flops 4000000000 | bytes 1000000 | tf_op jit(solution)/shard_map/pallas_call | solution.py:623
  14.1 0.0 collective-permute-done.25.far_ref.near_ref
  14.1 0.1 shard_map.95
  14.2 1.3 %collective-permute-start.26 = (f32[6,8,128]{2,1,0:T(8,128)S(1)}, f32[6,8,128]{2,1,0:T(8,128)S(1)}, u32[]{:S(2)}, u32[]{:S(2)}) collective-permute-start(f32[6,8,128]{2,1,0:T(8,128)S(1)} %shard_map.95), channel_id=1, source_target_pairs={{0,4},{2,6},{4,8},{5,1},{6,10},{7,3},{8,12},{9,5},{10,14},{11,7},{... | collective-permute-start | bytes 73736 | tf_op jit(solution)/shard_map/ppermute | solution.py:585
  15.5 0.0 copy-done.4
  15.5 4.9 %shard_map.96 = (bf16[74,384,256]{2,1,0:T(8,128)(2,1)S(1)}, bf16[32,128,48]{2,1,0:T(8,128)(2,1)S(1)}) custom-call(f32[3,8192]{1,0:T(4,128)S(1)} %copy-done.4, bf16[74,384,256]{2,1,0:T(8,128)(2,1)S(1)} %get-tuple-element.430.refs_0_), custom_call_target="tpu_custom_call", output_to_operand_aliasing={{0}: (1, {})} | custom-call | flops 4000000000 | bytes 1000000 | tf_op jit(solution)/shard_map/pallas_call | solution.py:623
  20.4 0.0 collective-permute-done.26.far_ref
  20.5 0.1 shard_map.97.mine_ref
  20.6 4.4 %collective-permute-start.27 = (f32[6,8,128]{2,1,0:T(8,128)S(1)}, f32[6,8,128]{2,1,0:T(8,128)S(1)}, u32[]{:S(2)}, u32[]{:S(2)}) collective-permute-start(f32[6,8,128]{2,1,0:T(8,128)S(1)} %shard_map.97.mine_ref), channel_id=1, source_target_pairs={{0,1},{1,0},{2,3},{3,2},{4,5},{5,4},{6,7},{7,6},{8,9},{9,8},{10,11... | collective-permute-start | bytes 73736 | tf_op jit(solution)/shard_map/ppermute | solution.py:643
  25.0 0.8 %collective-permute-done.27.other_ref = f32[6,8,128]{2,1,0:T(8,128)S(1)} collective-permute-done((f32[6,8,128]{2,1,0:T(8,128)S(1)}, f32[6,8,128]{2,1,0:T(8,128)S(1)}, u32[]{:S(2)}, u32[]{:S(2)}) %collective-permute-start.27) | collective-permute-done | bytes 24608 | tf_op jit(solution)/shard_map/ppermute | solution.py:643
  25.8 0.0 copy-done
  25.8 0.0 copy-done.2
  25.8 18.1 %shard_map.98 = (f32[3,76,8,128]{3,2,1,0:T(8,128)S(1)}, f32[8,128]{1,0:T(8,128)S(1)}, bf16[74,384,256]{2,1,0:T(8,128)(2,1)S(1)}) custom-call(s32[1]{0:T(128)S(6)} %copy.99.live_ref, f32[3,8192]{1,0:T(4,128)S(1)} %copy-done.4, f32[1,8192]{1,0:T(1,128)S(1)} %bitcast.172, f32[3,8192]{1,0:T(4,128)S(1)} %copy-done, ...), custom_call_target="tpu_custom_call", output_to_operand_aliasing={{2}: (7, {})} | custom-call | tf_op jit(solution)/shard_map/pallas_call | solution.py:649
  44.0 0.4 collective-permute-start.28
  44.4 0.8 %collective-permute-done.28 = f32[8,128]{1,0:T(8,128)S(1)} collective-permute-done((f32[8,128]{1,0:T(8,128)S(1)}, f32[8,128]{1,0:T(8,128)S(1)}, u32[]{:S(2)}, u32[]{:S(2)}) %collective-permute-start.28) | collective-permute-done | bytes 4128 | tf_op jit(solution)/shard_map/ppermute | solution.py:664
  45.2 0.7 broadcast_in_dim.37
  45.9 14.3 %all-to-all-start = ((f32[128,1,128]{2,1,0:T(1,128)}), f32[128,1,128]{2,1,0:T(1,128)S(1)}, u32[]{:S(2)}, u32[]{:S(2)}) async-start(f32[128,1,128]{2,1,0:T(1,128)} %broadcast_in_dim.37), calls=%async_computation | async-start | bytes 131072 | tf_op jit(solution)/shard_map/all_to_all | solution.py:666
  60.3 9.4 %shard_map.99.fluid_basis_ref = f32[24,3,8,128]{3,2,1,0:T(8,128)S(1)} custom-call(s32[1]{0:T(128)S(6)} %copy.99.live_ref, f32[3,8192]{1,0:T(4,128)} %jitter_ref.9, f32[1,8192]{1,0:T(1,128)} %bitcast.170, f32[3,8192]{1,0:T(4,128)} %displacement_ref.7, f32[3,3072]{1,0:T(4,128)} %fluid_ref.1, f32[2,6,8,128]{3,2,1,0:T(8,128)S(1)} %collective-permute-done.24.near_ref.partner_ref, ...), custom_call_target="tpu_custom_call" | custom-call | flops 6000000000 | bytes 10000000 | tf_op jit(solution)/shard_map/pallas_call | solution.py:674
  69.7 1.2 %all-to-all-done = f32[128,1,128]{2,1,0:T(1,128)S(1)} async-done(((f32[128,1,128]{2,1,0:T(1,128)}), f32[128,1,128]{2,1,0:T(1,128)S(1)}, u32[]{:S(2)}, u32[]{:S(2)}) %all-to-all-start) | async-done | bytes 65568 | tf_op jit(solution)/shard_map/all_to_all | solution.py:666
  70.9 2.2 %shard_map.100 = (f32[3,8192]{1,0:T(4,128)}, f32[3,8192]{1,0:T(4,128)S(1)}, f32[3,3072]{1,0:T(4,128)}, s32[1]{0:T(128)}) custom-call(s32[1]{0:T(128)S(6)} %copy.99.live_ref, f32[128,128]{1,0:T(8,128)S(1)} %bitcast.167, f32[1,8192]{1,0:T(1,128)} %bitcast.171, f32[3,8192]{1,0:T(4,128)} %displacement_ref.7, f32[3,76,8,128]{3,2,1,0:T(8,128)S(1)} %get-tuple-element.434.basis_ref, ...), custom_call_target="tpu_custom_call" | custom-call | tf_op jit(solution)/shard_map/pallas_call | solution.py:689
  73.8 0.2 conditional.1
  74.0 0.0 copy-start.7
  74.0 0.6 copy-done.7
  (2 shorter events, 0.0 us)
Async XLA Ops:
  0.6 14.9 %copy-start.4 = (f32[3,8192]{1,0:T(4,128)S(1)}, f32[3,8192]{1,0:T(4,128)}, u32[]{:S(2)}) copy-start(f32[3,8192]{1,0:T(4,128)} %jitter_ref.9) | copy-start | bytes 294916
  2.4 4.2 %collective-permute-start.24 = (f32[2,6,8,128]{3,2,1,0:T(8,128)S(1)}, f32[2,6,8,128]{3,2,1,0:T(8,128)S(1)}, u32[]{:S(2)}, u32[]{:S(2)}) collective-permute-start(f32[2,6,8,128]{3,2,1,0:T(8,128)S(1)} %shard_map.92.far_ref), channel_id=1, source_target_pairs={{0,1},{1,0},{2,3},{3,2},{4,5},{5,4},{6,7},{7,6},{8,9},{9,8},{10,11... | collective-permute-start | bytes 147464 | tf_op jit(solution)/shard_map/ppermute | solution.py:638
  6.7 19.1 %copy-start = (f32[3,8192]{1,0:T(4,128)S(1)}, f32[3,8192]{1,0:T(4,128)}, u32[]{:S(2)}) copy-start(f32[3,8192]{1,0:T(4,128)} %displacement_ref.7) | copy-start | bytes 294916
  6.7 19.1 %copy-start.2 = (f32[8192]{0:T(1024)S(1)}, f32[8192]{0:T(1024)}, u32[]{:S(2)}) copy-start(f32[8192]{0:T(1024)} %param.24) | copy-start | bytes 98308
  6.7 7.3 %collective-permute-start.25 = (f32[6,8,128]{2,1,0:T(8,128)S(1)}, f32[6,8,128]{2,1,0:T(8,128)S(1)}, u32[]{:S(2)}, u32[]{:S(2)}) collective-permute-start(f32[6,8,128]{2,1,0:T(8,128)S(1)} %shard_map.93.near_ref), channel_id=1, source_target_pairs={{0,2},{2,4},{3,1},{4,6},{5,3},{6,8},{7,5},{8,10},{9,7},{10,12},{11... | collective-permute-start | bytes 73736 | tf_op jit(solution)/shard_map/ppermute | solution.py:585
  14.2 6.2 %collective-permute-start.26 = (f32[6,8,128]{2,1,0:T(8,128)S(1)}, f32[6,8,128]{2,1,0:T(8,128)S(1)}, u32[]{:S(2)}, u32[]{:S(2)}) collective-permute-start(f32[6,8,128]{2,1,0:T(8,128)S(1)} %shard_map.95), channel_id=1, source_target_pairs={{0,4},{2,6},{4,8},{5,1},{6,10},{7,3},{8,12},{9,5},{10,14},{11,7},{... | collective-permute-start | bytes 73736 | tf_op jit(solution)/shard_map/ppermute | solution.py:585
  20.6 5.2 %collective-permute-start.27 = (f32[6,8,128]{2,1,0:T(8,128)S(1)}, f32[6,8,128]{2,1,0:T(8,128)S(1)}, u32[]{:S(2)}, u32[]{:S(2)}) collective-permute-start(f32[6,8,128]{2,1,0:T(8,128)S(1)} %shard_map.97.mine_ref), channel_id=1, source_target_pairs={{0,1},{1,0},{2,3},{3,2},{4,5},{5,4},{6,7},{7,6},{8,9},{9,8},{10,11... | collective-permute-start | bytes 73736 | tf_op jit(solution)/shard_map/ppermute | solution.py:643
  44.0 1.3 %collective-permute-start.28 = (f32[8,128]{1,0:T(8,128)S(1)}, f32[8,128]{1,0:T(8,128)S(1)}, u32[]{:S(2)}, u32[]{:S(2)}) collective-permute-start(f32[8,128]{1,0:T(8,128)S(1)} %get-tuple-element.433), channel_id=1, source_target_pairs={{0,1},{1,0},{2,3},{3,2},{4,5},{5,4},{6,7},{7,6},{8,9},{9,8},{10,11... | collective-permute-start | bytes 12296 | tf_op jit(solution)/shard_map/ppermute | solution.py:664
  45.9 25.0 %all-to-all-start = ((f32[128,1,128]{2,1,0:T(1,128)}), f32[128,1,128]{2,1,0:T(1,128)S(1)}, u32[]{:S(2)}, u32[]{:S(2)}) async-start(f32[128,1,128]{2,1,0:T(1,128)} %broadcast_in_dim.37), calls=%async_computation | async-start | bytes 131072 | tf_op jit(solution)/shard_map/all_to_all | solution.py:666
  74.0 0.7 copy-start.7

commit v8 on v5

--- a/solution.py
+++ b/solution.py
@@ -198,7 +198,7 @@
         target[block] = target_values(points, norm)
         return carry
 
-    lax.fori_loop(0, rows + 2, prepare, 0, unroll=4)
+    lax.fori_loop(0, rows + 2, prepare, 0, unroll=8)
 
     def generate(pair, carry):
         generate_two(source, target, matrix, 2 * pair, HALO + first + 2 * pair)
@@ -231,7 +231,7 @@
         b0[block] = vector_pair(rhs * scale)
         return carry
 
-    lax.fori_loop(0, width, prepare, 0, unroll=4)
+    lax.fori_loop(0, width, prepare, 0, unroll=8)
 
     for start in (0, live + HALO - 2):
         for block in range(HALO + 2):
@@ -298,7 +298,7 @@
         return tuple(s + kept * (a * b) for s, (a, b) in zip(sums, pairs))
 
     zero = jnp.zeros((8, BLK), jnp.float32)
-    sums = lax.fori_loop(0, block_count, add_up, (zero,) * MOMENTS, unroll=4)
+    sums = lax.fori_loop(0, block_count, add_up, (zero,) * MOMENTS, unroll=8)
     lane = lax.broadcasted_iota(jnp.int32, (8, BLK), 1)
     row = lax.broadcasted_iota(jnp.int32, (8, BLK), 0)
     moments = zero
@@ -329,7 +329,7 @@
         b2[block] = vector_pair(basis_ref[1, block] * scale)
         return carry
 
-    lax.fori_loop(HALO - 2, width - HALO + 2, prepare, 0, unroll=4)
+    lax.fori_loop(HALO - 2, width - HALO + 2, prepare, 0, unroll=8)
 
     def anchor_of(index):
         return lax.div(index * live, jnp.int32(fluid_count))
@@ -360,7 +360,7 @@
         return carry
 
     lax.fori_loop(0, fluid_count, generate_fluid, 0, unroll=4)
-    lax.fori_loop(0, fluid_count, apply_fluid, 0, unroll=4)
+    lax.fori_loop(0, fluid_count, apply_fluid, 0, unroll=8)
 
 
 def step_coefficients(moments):
@@ -427,14 +427,14 @@
         residual_ref[:, lanes] = jnp.where(is_live, remaining, 0.0)
         return carry
 
-    lax.fori_loop(0, block_count, one_block, 0, unroll=4)
+    lax.fori_loop(0, block_count, one_block, 0, unroll=8)
 
     def one_fluid(index, carry):
         lanes = pl.ds(pl.multiple_of(index * BLK, BLK), BLK)
         fluid_ref[:, lanes] = sum(a * fluid_basis_ref[index, k][0:3] for k, a in enumerate(solved))
         return carry
 
-    lax.fori_loop(0, fluid_count, one_fluid, 0, unroll=4)
+    lax.fori_loop(0, fluid_count, one_fluid, 0, unroll=8)
 
 
 def wendland(row_points, col_points):

time: 74 us -> 73.4 us (level)
  Pallas kernels: 42 us -> 40.2 us
  waiting for transfers between devices: 4.97 us -> 5.95 us
    pallas_call x1, Pallas kernels: 9.67 us -> 8.85 us  [per_device(): pl.pallas_call(functools.partial(fluid_kernel, axes, fluid_count), out_sh...]
    all_to_all x1, waiting for transfers between devices: 3.23 us -> 4.05 us  [per_device(): moments = lax.all_to_all(moments, axes, 0, 0, tiled=True)]
  transfers between devices with their start and end apart: 5 -> 5, of which waited for: 3 -> 4; matrix products, arithmetic and copies ran while one was open for 0% -> 0% of each run, Pallas kernels for 28% -> 26%
where the time goes in v8:
time: 73.4 us; the launch traced here: 73.2 us
  Pallas kernels  40.2 us (55%)
  starting transfers between devices  24 us (33%)
  waiting for transfers between devices  5.95 us (8%)
  between operations  2.12 us (3%)
    pallas_call x1, Pallas kernels, per_device(): pl.pallas_call(functools.partial(chain_kernel, axes, block_count), out_sh...  18.6 us
    all_to_all x1, starting transfers between devices, per_device(): moments = lax.all_to_all(moments, axes, 0, 0, tiled=True)  13.7 us
    pallas_call x2, Pallas kernels, own_part(): pl.pallas_call(functools.partial(own_kernel, first, rows, first + rows ==...  10.1 us
    pallas_call x1, Pallas kernels, per_device(): pl.pallas_call(functools.partial(fluid_kernel, axes, fluid_count), out_sh...  8.85 us
    ppermute x1, starting transfers between devices, per_device(): other = lax.ppermute(mine, axes, cores)  4.25 us
    all_to_all x1, waiting for transfers between devices, per_device(): moments = lax.all_to_all(moments, axes, 0, 0, tiled=True)  4.05 us
    ppermute x1, starting transfers between devices, per_device(): partner = lax.ppermute(ends, axes, cores)  3.33 us
    ppermute x2, starting transfers between devices, along_chips(): lax.ppermute(values, axes, [(i, j) for i, j in route if 0 <= j < count])  2.72 us
  transfers between devices with their start and end apart: 5, of which 4 were waited for; matrix products, arithmetic and copies ran while one was open for 0% of the time, Pallas kernels for 26%

profile of v8, /device:TPU:1, one launch (start us, length us, event | category | flops | bytes accessed | tf_op | source)
XLA Modules:
  0.0 73.2 jit_solution(6125999336987046812)
XLA Ops:
  0.6 0.0 copy-start.2
  1.3 1.0 %shard_map.92.far_ref = f32[2,6,8,128]{3,2,1,0:T(8,128)S(1)} custom-call(s32[1]{0:T(128)S(6)} %copy.100.live_ref, f32[3,8192]{1,0:T(4,128)} %jitter_ref.9, f32[1,8192]{1,0:T(1,128)} %bitcast.170, f32[3,8192]{1,0:T(4,128)} %displacement_ref.7), custom_call_target="tpu_custom_call" | custom-call | tf_op jit(solution)/shard_map/pallas_call | solution.py:591
  2.4 3.3 %collective-permute-start.24 = (f32[2,6,8,128]{3,2,1,0:T(8,128)S(1)}, f32[2,6,8,128]{3,2,1,0:T(8,128)S(1)}, u32[]{:S(2)}, u32[]{:S(2)}) collective-permute-start(f32[2,6,8,128]{3,2,1,0:T(8,128)S(1)} %shard_map.92.far_ref), channel_id=1, source_target_pairs={{0,1},{1,0},{2,3},{3,2},{4,5},{5,4},{6,7},{7,6},{8,9},{9,8},{10,11... | collective-permute-start | bytes 147464 | tf_op jit(solution)/shard_map/ppermute | solution.py:632
  5.7 0.9 %collective-permute-done.24.near_ref.partner_ref = f32[2,6,8,128]{3,2,1,0:T(8,128)S(1)} collective-permute-done((f32[2,6,8,128]{3,2,1,0:T(8,128)S(1)}, f32[2,6,8,128]{3,2,1,0:T(8,128)S(1)}, u32[]{:S(2)}, u32[]{:S(2)}) %collective-permute-start.24) | collective-permute-done | bytes 49184 | tf_op jit(solution)/shard_map/ppermute | solution.py:632
  6.6 0.1 shard_map.93.near_ref
  6.7 0.0 copy-start
  6.7 0.0 copy-start.1
  6.7 1.4 %collective-permute-start.25 = (f32[6,8,128]{2,1,0:T(8,128)S(1)}, f32[6,8,128]{2,1,0:T(8,128)S(1)}, u32[]{:S(2)}, u32[]{:S(2)}) collective-permute-start(f32[6,8,128]{2,1,0:T(8,128)S(1)} %shard_map.93.near_ref), channel_id=1, source_target_pairs={{0,2},{2,4},{3,1},{4,6},{5,3},{6,8},{7,5},{8,10},{9,7},{10,12},{11... | collective-permute-start | bytes 73736 | tf_op jit(solution)/shard_map/ppermute | solution.py:576
  8.2 5.5 %shard_map.94 = (bf16[74,384,256]{2,1,0:T(8,128)(2,1)S(1)}, f32[8,128]{1,0:T(8,128)S(1)}) custom-call(f32[3,8192]{1,0:T(4,128)} %jitter_ref.9), custom_call_target="tpu_custom_call" | custom-call | flops 4000000000 | bytes 1000000 | tf_op jit(solution)/shard_map/pallas_call | solution.py:614
  13.7 0.0 collective-permute-done.25.far_ref.near_ref
  13.7 0.1 shard_map.95
  13.8 1.3 %collective-permute-start.26 = (f32[6,8,128]{2,1,0:T(8,128)S(1)}, f32[6,8,128]{2,1,0:T(8,128)S(1)}, u32[]{:S(2)}, u32[]{:S(2)}) collective-permute-start(f32[6,8,128]{2,1,0:T(8,128)S(1)} %shard_map.95), channel_id=1, source_target_pairs={{0,4},{2,6},{4,8},{5,1},{6,10},{7,3},{8,12},{9,5},{10,14},{11,7},{... | collective-permute-start | bytes 73736 | tf_op jit(solution)/shard_map/ppermute | solution.py:576
  15.2 0.0 copy-done.2
  15.2 0.0 copy-start.3
  15.2 4.6 %shard_map.96 = (bf16[74,384,256]{2,1,0:T(8,128)(2,1)S(1)}, f32[8,128]{1,0:T(8,128)S(1)}) custom-call(f32[3,8192]{1,0:T(4,128)S(1)} %copy-done.2, bf16[74,384,256]{2,1,0:T(8,128)(2,1)S(1)} %get-tuple-element.430.refs_0_), custom_call_target="tpu_custom_call", output_to_operand_aliasing={{0}: (1, {})} | custom-call | flops 4000000000 | bytes 1000000 | tf_op jit(solution)/shard_map/pallas_call | solution.py:614
  19.8 0.2 collective-permute-done.26.far_ref
  19.9 0.1 shard_map.97.mine_ref
  20.1 4.3 %collective-permute-start.27 = (f32[6,8,128]{2,1,0:T(8,128)S(1)}, f32[6,8,128]{2,1,0:T(8,128)S(1)}, u32[]{:S(2)}, u32[]{:S(2)}) collective-permute-start(f32[6,8,128]{2,1,0:T(8,128)S(1)} %shard_map.97.mine_ref), channel_id=1, source_target_pairs={{0,1},{1,0},{2,3},{3,2},{4,5},{5,4},{6,7},{7,6},{8,9},{9,8},{10,11... | collective-permute-start | bytes 73736 | tf_op jit(solution)/shard_map/ppermute | solution.py:637
  24.3 0.8 %collective-permute-done.27.other_ref = f32[6,8,128]{2,1,0:T(8,128)S(1)} collective-permute-done((f32[6,8,128]{2,1,0:T(8,128)S(1)}, f32[6,8,128]{2,1,0:T(8,128)S(1)}, u32[]{:S(2)}, u32[]{:S(2)}) %collective-permute-start.27) | collective-permute-done | bytes 24608 | tf_op jit(solution)/shard_map/ppermute | solution.py:637
  25.2 0.0 copy-done
  25.2 0.0 copy-done.1
  25.2 18.6 %shard_map.98 = (f32[3,76,8,128]{3,2,1,0:T(8,128)S(1)}, f32[256,128]{1,0:T(8,128)}, bf16[74,384,256]{2,1,0:T(8,128)(2,1)S(1)}) custom-call(s32[1]{0:T(128)S(6)} %copy.100.live_ref, f32[3,8192]{1,0:T(4,128)S(1)} %copy-done.2, f32[1,8192]{1,0:T(1,128)S(1)} %bitcast.171, f32[3,8192]{1,0:T(4,128)S(1)} %copy-done, ...), custom_call_target="tpu_custom_call", output_to_operand_aliasing={{2}: (7, {})} | custom-call | tf_op jit(solution)/shard_map/pallas_call | solution.py:643
  43.8 13.7 %all-to-all-start = ((f32[256,1,128]{2,1,0:T(1,128)}), f32[256,1,128]{2,1,0:T(1,128)S(1)}, u32[]{:S(2)}, u32[]{:S(2)}) async-start(f32[256,1,128]{2,1,0:T(1,128)} %bitcast.53), calls=%async_computation | async-start | bytes 262144 | tf_op jit(solution)/shard_map/all_to_all | solution.py:658
  57.5 0.0 copy-done.3
  57.5 8.8 %shard_map.99.fluid_basis_ref = f32[24,3,8,128]{3,2,1,0:T(8,128)S(1)} custom-call(s32[1]{0:T(128)S(6)} %copy.100.live_ref, f32[3,8192]{1,0:T(4,128)S(1)} %copy-done.2, f32[1,8192]{1,0:T(1,128)S(1)} %bitcast.172, f32[3,8192]{1,0:T(4,128)S(1)} %copy-done, f32[3,3072]{1,0:T(4,128)S(1)} %copy-done.3, ...), custom_call_target="tpu_custom_call" | custom-call | flops 6000000000 | bytes 10000000 | tf_op jit(solution)/shard_map/pallas_call | solution.py:659
  66.3 4.0 %all-to-all-done = f32[256,1,128]{2,1,0:T(1,128)S(1)} async-done(((f32[256,1,128]{2,1,0:T(1,128)}), f32[256,1,128]{2,1,0:T(1,128)S(1)}, u32[]{:S(2)}, u32[]{:S(2)}) %all-to-all-start) | async-done | bytes 131104 | tf_op jit(solution)/shard_map/all_to_all | solution.py:658
  70.4 1.2 %shard_map.100 = (f32[3,8192]{1,0:T(4,128)}, f32[3,8192]{1,0:T(4,128)S(1)}, f32[3,3072]{1,0:T(4,128)}, s32[1]{0:T(128)}) custom-call(s32[1]{0:T(128)S(6)} %copy.100.live_ref, f32[256,128]{1,0:T(8,128)S(1)} %bitcast.168, f32[1,8192]{1,0:T(1,128)S(1)} %bitcast.173, f32[3,8192]{1,0:T(4,128)S(1)} %copy-done, f32[3,76,8,128]{3,2,1,0:T(8,128)S(1)} %get-tuple-element.434.basis_ref, ...), custom_call_target="tpu_custom_call" | custom-call | tf_op jit(solution)/shard_map/pallas_call | solution.py:673
  72.3 0.2 conditional.1
  72.5 0.0 copy-start.5
  72.5 0.6 copy-done.5
Async XLA Ops:
  0.6 14.5 %copy-start.2 = (f32[3,8192]{1,0:T(4,128)S(1)}, f32[3,8192]{1,0:T(4,128)}, u32[]{:S(2)}) copy-start(f32[3,8192]{1,0:T(4,128)} %jitter_ref.9) | copy-start | bytes 294916
  2.4 4.2 %collective-permute-start.24 = (f32[2,6,8,128]{3,2,1,0:T(8,128)S(1)}, f32[2,6,8,128]{3,2,1,0:T(8,128)S(1)}, u32[]{:S(2)}, u32[]{:S(2)}) collective-permute-start(f32[2,6,8,128]{3,2,1,0:T(8,128)S(1)} %shard_map.92.far_ref), channel_id=1, source_target_pairs={{0,1},{1,0},{2,3},{3,2},{4,5},{5,4},{6,7},{7,6},{8,9},{9,8},{10,11... | collective-permute-start | bytes 147464 | tf_op jit(solution)/shard_map/ppermute | solution.py:632
  6.7 18.5 %copy-start = (f32[3,8192]{1,0:T(4,128)S(1)}, f32[3,8192]{1,0:T(4,128)}, u32[]{:S(2)}) copy-start(f32[3,8192]{1,0:T(4,128)} %displacement_ref.7) | copy-start | bytes 294916
  6.7 18.5 %copy-start.1 = (f32[8192]{0:T(1024)S(1)}, f32[8192]{0:T(1024)}, u32[]{:S(2)}) copy-start(f32[8192]{0:T(1024)} %param.24) | copy-start | bytes 98308
  6.7 7.0 %collective-permute-start.25 = (f32[6,8,128]{2,1,0:T(8,128)S(1)}, f32[6,8,128]{2,1,0:T(8,128)S(1)}, u32[]{:S(2)}, u32[]{:S(2)}) collective-permute-start(f32[6,8,128]{2,1,0:T(8,128)S(1)} %shard_map.93.near_ref), channel_id=1, source_target_pairs={{0,2},{2,4},{3,1},{4,6},{5,3},{6,8},{7,5},{8,10},{9,7},{10,12},{11... | collective-permute-start | bytes 73736 | tf_op jit(solution)/shard_map/ppermute | solution.py:576
  13.8 6.1 %collective-permute-start.26 = (f32[6,8,128]{2,1,0:T(8,128)S(1)}, f32[6,8,128]{2,1,0:T(8,128)S(1)}, u32[]{:S(2)}, u32[]{:S(2)}) collective-permute-start(f32[6,8,128]{2,1,0:T(8,128)S(1)} %shard_map.95), channel_id=1, source_target_pairs={{0,4},{2,6},{4,8},{5,1},{6,10},{7,3},{8,12},{9,5},{10,14},{11,7},{... | collective-permute-start | bytes 73736 | tf_op jit(solution)/shard_map/ppermute | solution.py:576
  15.2 42.3 %copy-start.3 = (f32[3,3072]{1,0:T(4,128)S(1)}, f32[3,3072]{1,0:T(4,128)}, u32[]{:S(2)}) copy-start(f32[3,3072]{1,0:T(4,128)} %fluid_ref.1) | copy-start | bytes 110596
  20.1 5.1 %collective-permute-start.27 = (f32[6,8,128]{2,1,0:T(8,128)S(1)}, f32[6,8,128]{2,1,0:T(8,128)S(1)}, u32[]{:S(2)}, u32[]{:S(2)}) collective-permute-start(f32[6,8,128]{2,1,0:T(8,128)S(1)} %shard_map.97.mine_ref), channel_id=1, source_target_pairs={{0,1},{1,0},{2,3},{3,2},{4,5},{5,4},{6,7},{7,6},{8,9},{9,8},{10,11... | collective-permute-start | bytes 73736 | tf_op jit(solution)/shard_map/ppermute | solution.py:637
  43.8 26.6 %all-to-all-start = ((f32[256,1,128]{2,1,0:T(1,128)}), f32[256,1,128]{2,1,0:T(1,128)S(1)}, u32[]{:S(2)}, u32[]{:S(2)}) async-start(f32[256,1,128]{2,1,0:T(1,128)} %bitcast.53), calls=%async_computation | async-start | bytes 262144 | tf_op jit(solution)/shard_map/all_to_all | solution.py:658
  72.5 0.7 copy-start.5
